TPU v7x, 1024 devices: a whole 4x8x16 slice. The times are simulated.
1024 devices in a mesh: gx: 8 (over y), gy: 4 (over x), gz: 32 (over z, core).
Axes of the slice: x: 4, y: 8, z: 16, core: 2. Of those that a mesh axis runs over, the one named last changes fastest.
Arguments:
- relative: float32 [19, 128, 32, 1024], P(None, 'gz', 'gy', 'gx'), may hold values from 0.7 to 1.3
- fluid: int32 [128, 32, 1024], P('gz', 'gy', 'gx'), may hold values from 0 to 1, as said below
- block_fluid: int32 [64, 4, 8], P('gz', 'gy', 'gx'), may hold values from 0 to 2048, as said below
- new_owner: int32 [64, 4, 8], P('gz', 'gy', 'gx'), may hold values from 0 to 31, as said below
Outputs:
- relative_out: float32 [19, 128, 32, 1024], P(None, 'gz', 'gy', 'gx')
- block_density: float32 [64, 4, 8], P('gz', 'gy', 'gx')
Inputs may be any that keep to these rules, and one draw needn't show every extreme that they name: 1 marks fluid, 0 solid. `block_fluid`: the number of voxels of the block where fluid is 1. `new_owner`: a block only trades places across a boundary between gz neighbours: the last slot of one device with the first slot of the device above it, both entries of that pair naming the other device; every other entry names its own device.
All inputs are finite; a program needn't handle non-finite values.
Results may differ from a plain program's by a relative error of at most 0.00015.
Values sent between devices are 32-bit elements; how exact they have to be, the bound alone decides.
No kernel may reach another device: no remote copies, remote signals or barrier semaphores. Data moves between devices by JAX's collectives and lax.ppermute only.
A program may use at most 32 MiB of HBM per device.

v0:
```python
import jax
import jax.numpy as jnp
from jax import lax
from jax.sharding import PartitionSpec as P

BLK = 2
STEPS = 4


VELOCITIES = [
    (0, 0, 0),
    (1, 0, 0),
    (-1, 0, 0),
    (0, 1, 0),
    (0, -1, 0),
    (0, 0, 1),
    (0, 0, -1),
    (1, 1, 0),
    (-1, -1, 0),
    (1, -1, 0),
    (-1, 1, 0),
    (1, 0, 1),
    (-1, 0, -1),
    (1, 0, -1),
    (-1, 0, 1),
    (0, 1, 1),
    (0, -1, -1),
    (0, 1, -1),
    (0, -1, 1),
]
OPPOSITE = [0, 2, 1, 4, 3, 6, 5, 8, 7, 10, 9, 12, 11, 14, 13, 16, 15, 18, 17]
WEIGHTS = [1.0 / 3.0] + [1.0 / 18.0] * 6 + [1.0 / 36.0] * 12
OMEGA = 1.5


def passed_along(shard, axis, by):
    size = lax.axis_size(axis)
    pairs = [(i, i + by) for i in range(size) if 0 <= i + by < size]
    return lax.ppermute(shard, axis, pairs)


def with_halo(block, sides, width):
    for axis, dim in sides:
        count = lax.axis_size(axis)
        forward = [(i, i + 1) for i in range(count - 1)]
        backward = [(target, source) for source, target in forward]
        low = lax.ppermute(
            lax.slice_in_dim(block, block.shape[dim] - width, None, axis=dim), axis, forward
        )
        high = lax.ppermute(lax.slice_in_dim(block, 0, width, axis=dim), axis, backward)
        block = jnp.concatenate([low, block, high], axis=dim)
    return block


def collide(populations, fluid_flag):
    wet = fluid_flag[0] > 0.5
    density = jnp.sum(populations, axis=0)
    safe_density = jnp.where(wet, density, 1.0)
    speeds = []
    for axis_pick in range(3):
        moment = sum(
            (
                VELOCITIES[index][axis_pick] * populations[index]
                for index in range(1, 19)
                if VELOCITIES[index][axis_pick] != 0
            )
        )
        speeds.append(jnp.where(wet, moment / safe_density, 0.0))
    square = speeds[0] * speeds[0] + speeds[1] * speeds[1] + speeds[2] * speeds[2]
    relaxed = []
    for index in range(19):
        along = (
            VELOCITIES[index][0] * speeds[0]
            + VELOCITIES[index][1] * speeds[1]
            + VELOCITIES[index][2] * speeds[2]
        )
        balance = (
            WEIGHTS[index] * density * (1.0 + 3.0 * along + 4.5 * along * along - 1.5 * square)
        )
        relaxed.append(
            fluid_flag[0] * (populations[index] + OMEGA * (balance - populations[index]))
        )
    return jnp.stack(relaxed)


def stream(relaxed_pad, fluid_pad):
    size_z = relaxed_pad.shape[1] - 2
    size_y = relaxed_pad.shape[2] - 2
    size_x = relaxed_pad.shape[3] - 2
    centre = fluid_pad[0, 1 : 1 + size_z, 1 : 1 + size_y, 1 : 1 + size_x]
    read = []
    for index in range(19):
        step_z, step_y, step_x = VELOCITIES[index]
        source = relaxed_pad[
            index,
            1 - step_z : 1 - step_z + size_z,
            1 - step_y : 1 - step_y + size_y,
            1 - step_x : 1 - step_x + size_x,
        ]
        open_side = fluid_pad[
            0,
            1 - step_z : 1 - step_z + size_z,
            1 - step_y : 1 - step_y + size_y,
            1 - step_x : 1 - step_x + size_x,
        ]
        bounce = relaxed_pad[OPPOSITE[index], 1 : 1 + size_z, 1 : 1 + size_y, 1 : 1 + size_x]
        read.append(centre * jnp.where(open_side > 0.5, source, bounce))
    return jnp.stack(read)


def on_device(relative, fluid, block_fluid, new_owner):
    extent_z = relative.shape[1]
    slab_depth = extent_z // BLK
    own_index = lax.axis_index("gz")
    lowest_slab = relative[:, :slab_depth]
    upper_slab = relative[:, extent_z - slab_depth :]
    middle = relative[:, slab_depth : extent_z - slab_depth]
    from_lower = passed_along(upper_slab, "gz", 1)
    from_upper = passed_along(lowest_slab, "gz", -1)
    take_low = new_owner[0, 0, 0] == own_index - 1
    take_high = new_owner[BLK - 1, 0, 0] == own_index + 1
    home = jnp.concatenate(
        [
            jnp.where(take_low, from_lower, lowest_slab),
            middle,
            jnp.where(take_high, from_upper, upper_slab),
        ],
        axis=1,
    )
    weights = jnp.array(WEIGHTS, jnp.float32).reshape(19, 1, 1, 1)
    fluid_flag = fluid.astype(jnp.float32)[None]
    populations = weights * home * fluid_flag
    fluid_pad = fluid_flag
    for sweep in range(STEPS):
        relaxed = collide(populations, fluid_flag)
        if sweep == 0:
            stacked = jnp.concatenate([relaxed, fluid_flag], axis=0)
            padded = with_halo(stacked, (("gx", 3), ("gy", 2), ("gz", 1)), 1)
            relaxed_pad = padded[:19]
            fluid_pad = padded[19:]
        else:
            relaxed_pad = with_halo(relaxed, (("gx", 3), ("gy", 2), ("gz", 1)), 1)
        populations = stream(relaxed_pad, fluid_pad)
    relative_out = populations / weights
    density = jnp.sum(populations, axis=0)
    block_mass = density.reshape(BLK, slab_depth, density.shape[1], density.shape[2]).sum(
        axis=(1, 2, 3)
    )
    block_density = block_mass.reshape(BLK, 1, 1) / jnp.maximum(block_fluid, 1).astype(jnp.float32)
    return (relative_out, block_density)


def solution(mesh):
    return jax.shard_map(
        on_device,
        mesh=mesh,
        in_specs=(
            P(None, "gz", "gy", "gx"),
            P("gz", "gy", "gx"),
            P("gz", "gy", "gx"),
            P("gz", "gy", "gx"),
        ),
        out_specs=(P(None, "gz", "gy", "gx"), P("gz", "gy", "gx")),
        check_vma=False,
    )
```

profile of v0, /device:TPU:193, one launch (start us, length us, event | category | flops | bytes accessed | tf_op | source)
XLA Modules:
  0.0 164.4 jit_solution(5844909077940117648)
XLA Ops:
  0.6 1.1 fusion.862
  1.7 5.8 %collective-permute-start = (f32[19,2,8,128]{3,2,1,0:T(8,128)S(1)}, f32[19,2,8,128]{3,2,1,0:T(8,128)S(1)}, u32[]{:S(2)}, u32[]{:S(2)}) collective-permute-start(f32[19,2,8,128]{3,2,1,0:T(8,128)S(1)} %get-tuple-element.293), channel_id=1, source_target_pairs={{0,1},{1,2},{2,3},{3,4},{4,5},{5,6},{6,7},{7,8},{8,9},{9,10},{10,1... | collective-permute-start | bytes 466952 | tf_op jit(solution)/shard_map/ppermute | solution.py:39
  7.5 1.9 %collective-permute-start.1 = (f32[19,2,8,128]{3,2,1,0:T(8,128)S(1)}, f32[19,2,8,128]{3,2,1,0:T(8,128)S(1)}, u32[]{:S(2)}, u32[]{:S(2)}) collective-permute-start(f32[19,2,8,128]{3,2,1,0:T(8,128)S(1)} %get-tuple-element.294), channel_id=1, source_target_pairs={{1,0},{2,1},{3,2},{4,3},{5,4},{6,5},{7,6},{8,7},{9,8},{10,9},{11,1... | collective-permute-start | bytes 466952 | tf_op jit(solution)/shard_map/ppermute | solution.py:39
  9.5 0.6 copy-done.2
  10.1 0.6 fusion.863
  12.0 3.3 %collective-permute-done.1 = f32[19,2,8,128]{3,2,1,0:T(8,128)S(1)} collective-permute-done((f32[19,2,8,128]{3,2,1,0:T(8,128)S(1)}, f32[19,2,8,128]{3,2,1,0:T(8,128)S(1)}, u32[]{:S(2)}, u32[]{:S(2)}) %collective-permute-start.1) | collective-permute-done | bytes 155680 | tf_op jit(solution)/shard_map/ppermute | solution.py:39
  15.3 0.6 copy-done.4
  16.8 3.2 %collective-permute-start.2 = (f32[20,4,8,1]{3,2,1,0:T(8,128)S(1)}, f32[20,4,8,1]{3,2,1,0:T(8,128)S(1)}, u32[]{:S(2)}, u32[]{:S(2)}) collective-permute-start(f32[20,4,8,1]{3,2,1,0:T(8,128)S(1)} %get-tuple-element.283), channel_id=1, source_target_pairs={{0,128},{128,256},{256,384},{384,512},{512,640},{640,768},{768,896... | collective-permute-start | bytes 7688 | tf_op jit(solution)/shard_map/ppermute | solution.py:47
  20.0 1.3 collective-permute-start.3
  21.3 2.7 %collective-permute-done.2 = f32[20,4,8,1]{3,2,1,0:T(8,128)S(1)} collective-permute-done((f32[20,4,8,1]{3,2,1,0:T(8,128)S(1)}, f32[20,4,8,1]{3,2,1,0:T(8,128)S(1)}, u32[]{:S(2)}, u32[]{:S(2)}) %collective-permute-start.2) | collective-permute-done | bytes 2592 | tf_op jit(solution)/shard_map/ppermute | solution.py:47
  24.0 3.8 %collective-permute-done.3 = f32[20,4,8,1]{3,2,1,0:T(8,128)S(1)} collective-permute-done((f32[20,4,8,1]{3,2,1,0:T(8,128)S(1)}, f32[20,4,8,1]{3,2,1,0:T(8,128)S(1)}, u32[]{:S(2)}, u32[]{:S(2)}) %collective-permute-start.3) | collective-permute-done | bytes 2592 | tf_op jit(solution)/shard_map/ppermute | solution.py:50
  27.8 0.6 pad_maximum_fusion.22
  28.4 3.1 %collective-permute-start.4 = (f32[20,4,1,130]{3,2,1,0:T(1,128)S(1)}, f32[20,4,1,130]{3,2,1,0:T(1,128)S(1)}, u32[]{:S(2)}, u32[]{:S(2)}) collective-permute-start(f32[20,4,1,130]{3,2,1,0:T(1,128)S(1)} %get-tuple-element.275), channel_id=1, source_target_pairs={{0,32},{32,64},{64,96},{1,33},{33,65},{65,97},{2,34},{34,66},{66,9... | collective-permute-start | bytes 124808 | tf_op jit(solution)/shard_map/ppermute | solution.py:47
  31.5 1.3 collective-permute-start.5
  33.0 3.7 %collective-permute-done.5 = f32[20,4,1,130]{3,2,1,0:T(1,128)S(1)} collective-permute-done((f32[20,4,1,130]{3,2,1,0:T(1,128)S(1)}, f32[20,4,1,130]{3,2,1,0:T(1,128)S(1)}, u32[]{:S(2)}, u32[]{:S(2)}) %collective-permute-start.5) | collective-permute-done | bytes 41632 | tf_op jit(solution)/shard_map/ppermute | solution.py:50
  36.7 0.3 pad_maximum_fusion
  37.1 1.9 %collective-permute-start.7 = (f32[20,1,10,130]{3,2,1,0:T(8,128)S(1)}, f32[20,1,10,130]{3,2,1,0:T(8,128)S(1)}, u32[]{:S(2)}, u32[]{:S(2)}) collective-permute-start(f32[20,1,10,130]{3,2,1,0:T(8,128)S(1)} %get-tuple-element.267), channel_id=1, source_target_pairs={{1,0},{2,1},{3,2},{4,3},{5,4},{6,5},{7,6},{8,7},{9,8},{10,9},{11,1... | collective-permute-start | bytes 312008 | tf_op jit(solution)/shard_map/ppermute | solution.py:50
  39.0 7.9 %collective-permute-start.6 = (f32[20,1,10,130]{3,2,1,0:T(8,128)S(1)}, f32[20,1,10,130]{3,2,1,0:T(8,128)S(1)}, u32[]{:S(2)}, u32[]{:S(2)}) collective-permute-start(f32[20,1,10,130]{3,2,1,0:T(8,128)S(1)} %get-tuple-element.268), channel_id=1, source_target_pairs={{0,1},{1,2},{2,3},{3,4},{4,5},{5,6},{6,7},{7,8},{8,9},{9,10},{10,1... | collective-permute-start | bytes 312008 | tf_op jit(solution)/shard_map/ppermute | solution.py:47
  46.9 2.8 %collective-permute-done.7 = f32[20,1,10,130]{3,2,1,0:T(8,128)S(1)} collective-permute-done((f32[20,1,10,130]{3,2,1,0:T(8,128)S(1)}, f32[20,1,10,130]{3,2,1,0:T(8,128)S(1)}, u32[]{:S(2)}, u32[]{:S(2)}) %collective-permute-start.7) | collective-permute-done | bytes 104032 | tf_op jit(solution)/shard_map/ppermute | solution.py:50
  49.8 1.2 collective-permute-done.6
  50.9 0.4 constant_dynamic-update-slice_fusion.38
  52.0 3.2 %collective-permute-start.8 = (f32[19,4,8,1]{3,2,1,0:T(8,128)S(1)}, f32[19,4,8,1]{3,2,1,0:T(8,128)S(1)}, u32[]{:S(2)}, u32[]{:S(2)}) collective-permute-start(f32[19,4,8,1]{3,2,1,0:T(8,128)S(1)} %get-tuple-element.289), channel_id=1, source_target_pairs={{0,128},{128,256},{256,384},{384,512},{512,640},{640,768},{768,896... | collective-permute-start | bytes 7304 | tf_op jit(solution)/shard_map/ppermute | solution.py:47
  55.2 1.3 collective-permute-start.9
  56.5 3.3 %collective-permute-done.8 = f32[19,4,8,1]{3,2,1,0:T(8,128)S(1)} collective-permute-done((f32[19,4,8,1]{3,2,1,0:T(8,128)S(1)}, f32[19,4,8,1]{3,2,1,0:T(8,128)S(1)}, u32[]{:S(2)}, u32[]{:S(2)}) %collective-permute-start.8) | collective-permute-done | bytes 2464 | tf_op jit(solution)/shard_map/ppermute | solution.py:47
  59.8 4.1 %collective-permute-done.9 = f32[19,4,8,1]{3,2,1,0:T(8,128)S(1)} collective-permute-done((f32[19,4,8,1]{3,2,1,0:T(8,128)S(1)}, f32[19,4,8,1]{3,2,1,0:T(8,128)S(1)}, u32[]{:S(2)}, u32[]{:S(2)}) %collective-permute-start.9) | collective-permute-done | bytes 2464 | tf_op jit(solution)/shard_map/ppermute | solution.py:50
  63.9 0.5 pad_maximum_fusion.31
  64.5 3.1 %collective-permute-start.10 = (f32[19,4,1,130]{3,2,1,0:T(1,128)S(1)}, f32[19,4,1,130]{3,2,1,0:T(1,128)S(1)}, u32[]{:S(2)}, u32[]{:S(2)}) collective-permute-start(f32[19,4,1,130]{3,2,1,0:T(1,128)S(1)} %get-tuple-element.281), channel_id=1, source_target_pairs={{0,32},{32,64},{64,96},{1,33},{33,65},{65,97},{2,34},{34,66},{66,9... | collective-permute-start | bytes 118568 | tf_op jit(solution)/shard_map/ppermute | solution.py:47
  67.6 1.3 collective-permute-start.11
  69.1 3.7 %collective-permute-done.11 = f32[19,4,1,130]{3,2,1,0:T(1,128)S(1)} collective-permute-done((f32[19,4,1,130]{3,2,1,0:T(1,128)S(1)}, f32[19,4,1,130]{3,2,1,0:T(1,128)S(1)}, u32[]{:S(2)}, u32[]{:S(2)}) %collective-permute-start.11) | collective-permute-done | bytes 39552 | tf_op jit(solution)/shard_map/ppermute | solution.py:50
  72.8 0.3 pad_maximum_fusion.15
  73.1 1.9 %collective-permute-start.13 = (f32[19,1,10,130]{3,2,1,0:T(8,128)S(1)}, f32[19,1,10,130]{3,2,1,0:T(8,128)S(1)}, u32[]{:S(2)}, u32[]{:S(2)}) collective-permute-start(f32[19,1,10,130]{3,2,1,0:T(8,128)S(1)} %get-tuple-element.273), channel_id=1, source_target_pairs={{1,0},{2,1},{3,2},{4,3},{5,4},{6,5},{7,6},{8,7},{9,8},{10,9},{11,1... | collective-permute-start | bytes 296408 | tf_op jit(solution)/shard_map/ppermute | solution.py:50
  75.0 7.5 %collective-permute-start.12 = (f32[19,1,10,130]{3,2,1,0:T(8,128)S(1)}, f32[19,1,10,130]{3,2,1,0:T(8,128)S(1)}, u32[]{:S(2)}, u32[]{:S(2)}) collective-permute-start(f32[19,1,10,130]{3,2,1,0:T(8,128)S(1)} %get-tuple-element.274), channel_id=1, source_target_pairs={{0,1},{1,2},{2,3},{3,4},{4,5},{5,6},{6,7},{7,8},{8,9},{9,10},{10,1... | collective-permute-start | bytes 296408 | tf_op jit(solution)/shard_map/ppermute | solution.py:47
  82.5 2.6 %collective-permute-done.13 = f32[19,1,10,130]{3,2,1,0:T(8,128)S(1)} collective-permute-done((f32[19,1,10,130]{3,2,1,0:T(8,128)S(1)}, f32[19,1,10,130]{3,2,1,0:T(8,128)S(1)}, u32[]{:S(2)}, u32[]{:S(2)}) %collective-permute-start.13) | collective-permute-done | bytes 98832 | tf_op jit(solution)/shard_map/ppermute | solution.py:50
  85.1 1.2 collective-permute-done.12
  87.2 5.1 %collective-permute-start.14 = (f32[19,4,8,1]{3,2,1,0:T(8,128)S(1)}, f32[19,4,8,1]{3,2,1,0:T(8,128)S(1)}, u32[]{:S(2)}, u32[]{:S(2)}) collective-permute-start(f32[19,4,8,1]{3,2,1,0:T(8,128)S(1)} %get-tuple-element.287), channel_id=1, source_target_pairs={{0,128},{128,256},{256,384},{384,512},{512,640},{640,768},{768,896... | collective-permute-start | bytes 7304 | tf_op jit(solution)/shard_map/ppermute | solution.py:47
  92.3 1.3 collective-permute-start.15
  93.6 2.9 %collective-permute-done.14 = f32[19,4,8,1]{3,2,1,0:T(8,128)S(1)} collective-permute-done((f32[19,4,8,1]{3,2,1,0:T(8,128)S(1)}, f32[19,4,8,1]{3,2,1,0:T(8,128)S(1)}, u32[]{:S(2)}, u32[]{:S(2)}) %collective-permute-start.14) | collective-permute-done | bytes 2464 | tf_op jit(solution)/shard_map/ppermute | solution.py:47
  96.5 4.4 %collective-permute-done.15 = f32[19,4,8,1]{3,2,1,0:T(8,128)S(1)} collective-permute-done((f32[19,4,8,1]{3,2,1,0:T(8,128)S(1)}, f32[19,4,8,1]{3,2,1,0:T(8,128)S(1)}, u32[]{:S(2)}, u32[]{:S(2)}) %collective-permute-start.15) | collective-permute-done | bytes 2464 | tf_op jit(solution)/shard_map/ppermute | solution.py:50
  100.9 0.5 pad_maximum_fusion.28
  101.4 2.8 %collective-permute-start.16 = (f32[19,4,1,130]{3,2,1,0:T(1,128)S(1)}, f32[19,4,1,130]{3,2,1,0:T(1,128)S(1)}, u32[]{:S(2)}, u32[]{:S(2)}) collective-permute-start(f32[19,4,1,130]{3,2,1,0:T(1,128)S(1)} %get-tuple-element.279), channel_id=1, source_target_pairs={{0,32},{32,64},{64,96},{1,33},{33,65},{65,97},{2,34},{34,66},{66,9... | collective-permute-start | bytes 118568 | tf_op jit(solution)/shard_map/ppermute | solution.py:47
  104.2 1.3 collective-permute-start.17
  105.7 3.7 %collective-permute-done.17 = f32[19,4,1,130]{3,2,1,0:T(1,128)S(1)} collective-permute-done((f32[19,4,1,130]{3,2,1,0:T(1,128)S(1)}, f32[19,4,1,130]{3,2,1,0:T(1,128)S(1)}, u32[]{:S(2)}, u32[]{:S(2)}) %collective-permute-start.17) | collective-permute-done | bytes 39552 | tf_op jit(solution)/shard_map/ppermute | solution.py:50
  109.7 1.9 %collective-permute-start.19 = (f32[19,1,10,130]{3,2,1,0:T(8,128)S(1)}, f32[19,1,10,130]{3,2,1,0:T(8,128)S(1)}, u32[]{:S(2)}, u32[]{:S(2)}) collective-permute-start(f32[19,1,10,130]{3,2,1,0:T(8,128)S(1)} %get-tuple-element.271), channel_id=1, source_target_pairs={{1,0},{2,1},{3,2},{4,3},{5,4},{6,5},{7,6},{8,7},{9,8},{10,9},{11,1... | collective-permute-start | bytes 296408 | tf_op jit(solution)/shard_map/ppermute | solution.py:50
  111.6 8.0 %collective-permute-start.18 = (f32[19,1,10,130]{3,2,1,0:T(8,128)S(1)}, f32[19,1,10,130]{3,2,1,0:T(8,128)S(1)}, u32[]{:S(2)}, u32[]{:S(2)}) collective-permute-start(f32[19,1,10,130]{3,2,1,0:T(8,128)S(1)} %get-tuple-element.272), channel_id=1, source_target_pairs={{0,1},{1,2},{2,3},{3,4},{4,5},{5,6},{6,7},{7,8},{8,9},{9,10},{10,1... | collective-permute-start | bytes 296408 | tf_op jit(solution)/shard_map/ppermute | solution.py:47
  119.6 2.6 %collective-permute-done.19 = f32[19,1,10,130]{3,2,1,0:T(8,128)S(1)} collective-permute-done((f32[19,1,10,130]{3,2,1,0:T(8,128)S(1)}, f32[19,1,10,130]{3,2,1,0:T(8,128)S(1)}, u32[]{:S(2)}, u32[]{:S(2)}) %collective-permute-start.19) | collective-permute-done | bytes 98832 | tf_op jit(solution)/shard_map/ppermute | solution.py:50
  122.2 1.2 collective-permute-done.18
  124.3 3.4 %collective-permute-start.20 = (f32[19,4,8,1]{3,2,1,0:T(8,128)S(1)}, f32[19,4,8,1]{3,2,1,0:T(8,128)S(1)}, u32[]{:S(2)}, u32[]{:S(2)}) collective-permute-start(f32[19,4,8,1]{3,2,1,0:T(8,128)S(1)} %get-tuple-element.285), channel_id=1, source_target_pairs={{0,128},{128,256},{256,384},{384,512},{512,640},{640,768},{768,896... | collective-permute-start | bytes 7304 | tf_op jit(solution)/shard_map/ppermute | solution.py:47
  127.7 1.3 collective-permute-start.21
  129.0 2.7 %collective-permute-done.20 = f32[19,4,8,1]{3,2,1,0:T(8,128)S(1)} collective-permute-done((f32[19,4,8,1]{3,2,1,0:T(8,128)S(1)}, f32[19,4,8,1]{3,2,1,0:T(8,128)S(1)}, u32[]{:S(2)}, u32[]{:S(2)}) %collective-permute-start.20) | collective-permute-done | bytes 2464 | tf_op jit(solution)/shard_map/ppermute | solution.py:47
  131.7 4.1 %collective-permute-done.21 = f32[19,4,8,1]{3,2,1,0:T(8,128)S(1)} collective-permute-done((f32[19,4,8,1]{3,2,1,0:T(8,128)S(1)}, f32[19,4,8,1]{3,2,1,0:T(8,128)S(1)}, u32[]{:S(2)}, u32[]{:S(2)}) %collective-permute-start.21) | collective-permute-done | bytes 2464 | tf_op jit(solution)/shard_map/ppermute | solution.py:50
  135.8 0.5 pad_maximum_fusion.25
  136.3 1.6 collective-permute-start.22
  138.0 1.3 collective-permute-start.23
  139.4 3.7 %collective-permute-done.23 = f32[19,4,1,130]{3,2,1,0:T(1,128)S(1)} collective-permute-done((f32[19,4,1,130]{3,2,1,0:T(1,128)S(1)}, f32[19,4,1,130]{3,2,1,0:T(1,128)S(1)}, u32[]{:S(2)}, u32[]{:S(2)}) %collective-permute-start.23) | collective-permute-done | bytes 39552 | tf_op jit(solution)/shard_map/ppermute | solution.py:50
  143.1 0.3 pad_maximum_fusion.9
  143.4 8.3 %collective-permute-start.24 = (f32[19,1,10,130]{3,2,1,0:T(8,128)S(1)}, f32[19,1,10,130]{3,2,1,0:T(8,128)S(1)}, u32[]{:S(2)}, u32[]{:S(2)}) collective-permute-start(f32[19,1,10,130]{3,2,1,0:T(8,128)S(1)} %get-tuple-element.269), channel_id=1, source_target_pairs={{0,1},{1,2},{2,3},{3,4},{4,5},{5,6},{6,7},{7,8},{8,9},{9,10},{10,1... | collective-permute-start | bytes 296408 | tf_op jit(solution)/shard_map/ppermute | solution.py:47
  151.7 1.9 %collective-permute-start.25 = (f32[19,1,10,130]{3,2,1,0:T(8,128)S(1)}, f32[19,1,10,130]{3,2,1,0:T(8,128)S(1)}, u32[]{:S(2)}, u32[]{:S(2)}) collective-permute-start(f32[19,1,10,130]{3,2,1,0:T(8,128)S(1)} %get-tuple-element.270), channel_id=1, source_target_pairs={{1,0},{2,1},{3,2},{4,3},{5,4},{6,5},{7,6},{8,7},{9,8},{10,9},{11,1... | collective-permute-start | bytes 296408 | tf_op jit(solution)/shard_map/ppermute | solution.py:50
  153.7 1.9 %collective-permute-done.24 = f32[19,1,10,130]{3,2,1,0:T(8,128)S(1)} collective-permute-done((f32[19,1,10,130]{3,2,1,0:T(8,128)S(1)}, f32[19,1,10,130]{3,2,1,0:T(8,128)S(1)}, u32[]{:S(2)}, u32[]{:S(2)}) %collective-permute-start.24) | collective-permute-done | bytes 98832 | tf_op jit(solution)/shard_map/ppermute | solution.py:47
  155.5 5.6 %collective-permute-done.25 = f32[19,1,10,130]{3,2,1,0:T(8,128)S(1)} collective-permute-done((f32[19,1,10,130]{3,2,1,0:T(8,128)S(1)}, f32[19,1,10,130]{3,2,1,0:T(8,128)S(1)}, u32[]{:S(2)}, u32[]{:S(2)}) %collective-permute-start.25) | collective-permute-done | bytes 98832 | tf_op jit(solution)/shard_map/ppermute | solution.py:50
  161.2 0.3 add_reduce_fusion
  161.8 0.6 copy-done.3
  162.4 0.8 broadcast_multiply_fusion
  163.3 0.5 copy-done.5
  163.9 0.5 bitcast_divide_fusion
  (117 shorter events, 3.9 us)
Async XLA Ops:
  0.6 14.6 %copy-start.1 = (f32[19,4,8,128]{3,2,1,0:T(8,128)S(1)}, f32[19,4,8,128]{3,2,1,0:T(8,128)}, u32[]{:S(2)}) copy-start(f32[19,4,8,128]{3,2,1,0:T(8,128)} %param.5) | copy-start | bytes 933892
  0.6 8.8 %copy-start = (s32[4,8,128]{2,1,0:T(8,128)S(1)}, s32[4,8,128]{2,1,0:T(8,128)}, u32[]{:S(2)}) copy-start(s32[4,8,128]{2,1,0:T(8,128)} %param.6) | copy-start | bytes 49156
  1.7 10.3 %collective-permute-start = (f32[19,2,8,128]{3,2,1,0:T(8,128)S(1)}, f32[19,2,8,128]{3,2,1,0:T(8,128)S(1)}, u32[]{:S(2)}, u32[]{:S(2)}) collective-permute-start(f32[19,2,8,128]{3,2,1,0:T(8,128)S(1)} %get-tuple-element.293), channel_id=1, source_target_pairs={{0,1},{1,2},{2,3},{3,4},{4,5},{5,6},{6,7},{7,8},{8,9},{9,10},{10,1... | collective-permute-start | bytes 466952 | tf_op jit(solution)/shard_map/ppermute | solution.py:39
  7.5 7.8 %collective-permute-start.1 = (f32[19,2,8,128]{3,2,1,0:T(8,128)S(1)}, f32[19,2,8,128]{3,2,1,0:T(8,128)S(1)}, u32[]{:S(2)}, u32[]{:S(2)}) collective-permute-start(f32[19,2,8,128]{3,2,1,0:T(8,128)S(1)} %get-tuple-element.294), channel_id=1, source_target_pairs={{1,0},{2,1},{3,2},{4,3},{5,4},{6,5},{7,6},{8,7},{9,8},{10,9},{11,1... | collective-permute-start | bytes 466952 | tf_op jit(solution)/shard_map/ppermute | solution.py:39
  9.4 0.7 copy-start.2
  15.3 0.7 copy-start.4
  16.8 7.2 %collective-permute-start.2 = (f32[20,4,8,1]{3,2,1,0:T(8,128)S(1)}, f32[20,4,8,1]{3,2,1,0:T(8,128)S(1)}, u32[]{:S(2)}, u32[]{:S(2)}) collective-permute-start(f32[20,4,8,1]{3,2,1,0:T(8,128)S(1)} %get-tuple-element.283), channel_id=1, source_target_pairs={{0,128},{128,256},{256,384},{384,512},{512,640},{640,768},{768,896... | collective-permute-start | bytes 7688 | tf_op jit(solution)/shard_map/ppermute | solution.py:47
  20.0 7.8 %collective-permute-start.3 = (f32[20,4,8,1]{3,2,1,0:T(8,128)S(1)}, f32[20,4,8,1]{3,2,1,0:T(8,128)S(1)}, u32[]{:S(2)}, u32[]{:S(2)}) collective-permute-start(f32[20,4,8,1]{3,2,1,0:T(8,128)S(1)} %get-tuple-element.284), channel_id=1, source_target_pairs={{128,0},{256,128},{384,256},{512,384},{640,512},{768,640},{896,768... | collective-permute-start | bytes 7688 | tf_op jit(solution)/shard_map/ppermute | solution.py:50
  28.4 4.6 %collective-permute-start.4 = (f32[20,4,1,130]{3,2,1,0:T(1,128)S(1)}, f32[20,4,1,130]{3,2,1,0:T(1,128)S(1)}, u32[]{:S(2)}, u32[]{:S(2)}) collective-permute-start(f32[20,4,1,130]{3,2,1,0:T(1,128)S(1)} %get-tuple-element.275), channel_id=1, source_target_pairs={{0,32},{32,64},{64,96},{1,33},{33,65},{65,97},{2,34},{34,66},{66,9... | collective-permute-start | bytes 124808 | tf_op jit(solution)/shard_map/ppermute | solution.py:47
  31.5 5.2 %collective-permute-start.5 = (f32[20,4,1,130]{3,2,1,0:T(1,128)S(1)}, f32[20,4,1,130]{3,2,1,0:T(1,128)S(1)}, u32[]{:S(2)}, u32[]{:S(2)}) collective-permute-start(f32[20,4,1,130]{3,2,1,0:T(1,128)S(1)} %get-tuple-element.276), channel_id=1, source_target_pairs={{32,0},{64,32},{96,64},{33,1},{65,33},{97,65},{34,2},{66,34},{98,6... | collective-permute-start | bytes 124808 | tf_op jit(solution)/shard_map/ppermute | solution.py:50
  37.1 12.7 %collective-permute-start.7 = (f32[20,1,10,130]{3,2,1,0:T(8,128)S(1)}, f32[20,1,10,130]{3,2,1,0:T(8,128)S(1)}, u32[]{:S(2)}, u32[]{:S(2)}) collective-permute-start(f32[20,1,10,130]{3,2,1,0:T(8,128)S(1)} %get-tuple-element.267), channel_id=1, source_target_pairs={{1,0},{2,1},{3,2},{4,3},{5,4},{6,5},{7,6},{8,7},{9,8},{10,9},{11,1... | collective-permute-start | bytes 312008 | tf_op jit(solution)/shard_map/ppermute | solution.py:50
  39.0 11.9 %collective-permute-start.6 = (f32[20,1,10,130]{3,2,1,0:T(8,128)S(1)}, f32[20,1,10,130]{3,2,1,0:T(8,128)S(1)}, u32[]{:S(2)}, u32[]{:S(2)}) collective-permute-start(f32[20,1,10,130]{3,2,1,0:T(8,128)S(1)} %get-tuple-element.268), channel_id=1, source_target_pairs={{0,1},{1,2},{2,3},{3,4},{4,5},{5,6},{6,7},{7,8},{8,9},{9,10},{10,1... | collective-permute-start | bytes 312008 | tf_op jit(solution)/shard_map/ppermute | solution.py:47
  52.0 7.8 %collective-permute-start.8 = (f32[19,4,8,1]{3,2,1,0:T(8,128)S(1)}, f32[19,4,8,1]{3,2,1,0:T(8,128)S(1)}, u32[]{:S(2)}, u32[]{:S(2)}) collective-permute-start(f32[19,4,8,1]{3,2,1,0:T(8,128)S(1)} %get-tuple-element.289), channel_id=1, source_target_pairs={{0,128},{128,256},{256,384},{384,512},{512,640},{640,768},{768,896... | collective-permute-start | bytes 7304 | tf_op jit(solution)/shard_map/ppermute | solution.py:47
  55.2 8.7 %collective-permute-start.9 = (f32[19,4,8,1]{3,2,1,0:T(8,128)S(1)}, f32[19,4,8,1]{3,2,1,0:T(8,128)S(1)}, u32[]{:S(2)}, u32[]{:S(2)}) collective-permute-start(f32[19,4,8,1]{3,2,1,0:T(8,128)S(1)} %get-tuple-element.290), channel_id=1, source_target_pairs={{128,0},{256,128},{384,256},{512,384},{640,512},{768,640},{896,768... | collective-permute-start | bytes 7304 | tf_op jit(solution)/shard_map/ppermute | solution.py:50
  64.5 4.6 %collective-permute-start.10 = (f32[19,4,1,130]{3,2,1,0:T(1,128)S(1)}, f32[19,4,1,130]{3,2,1,0:T(1,128)S(1)}, u32[]{:S(2)}, u32[]{:S(2)}) collective-permute-start(f32[19,4,1,130]{3,2,1,0:T(1,128)S(1)} %get-tuple-element.281), channel_id=1, source_target_pairs={{0,32},{32,64},{64,96},{1,33},{33,65},{65,97},{2,34},{34,66},{66,9... | collective-permute-start | bytes 118568 | tf_op jit(solution)/shard_map/ppermute | solution.py:47
  67.6 5.1 %collective-permute-start.11 = (f32[19,4,1,130]{3,2,1,0:T(1,128)S(1)}, f32[19,4,1,130]{3,2,1,0:T(1,128)S(1)}, u32[]{:S(2)}, u32[]{:S(2)}) collective-permute-start(f32[19,4,1,130]{3,2,1,0:T(1,128)S(1)} %get-tuple-element.282), channel_id=1, source_target_pairs={{32,0},{64,32},{96,64},{33,1},{65,33},{97,65},{34,2},{66,34},{98,6... | collective-permute-start | bytes 118568 | tf_op jit(solution)/shard_map/ppermute | solution.py:50
  73.1 12.1 %collective-permute-start.13 = (f32[19,1,10,130]{3,2,1,0:T(8,128)S(1)}, f32[19,1,10,130]{3,2,1,0:T(8,128)S(1)}, u32[]{:S(2)}, u32[]{:S(2)}) collective-permute-start(f32[19,1,10,130]{3,2,1,0:T(8,128)S(1)} %get-tuple-element.273), channel_id=1, source_target_pairs={{1,0},{2,1},{3,2},{4,3},{5,4},{6,5},{7,6},{8,7},{9,8},{10,9},{11,1... | collective-permute-start | bytes 296408 | tf_op jit(solution)/shard_map/ppermute | solution.py:50
  75.0 11.3 %collective-permute-start.12 = (f32[19,1,10,130]{3,2,1,0:T(8,128)S(1)}, f32[19,1,10,130]{3,2,1,0:T(8,128)S(1)}, u32[]{:S(2)}, u32[]{:S(2)}) collective-permute-start(f32[19,1,10,130]{3,2,1,0:T(8,128)S(1)} %get-tuple-element.274), channel_id=1, source_target_pairs={{0,1},{1,2},{2,3},{3,4},{4,5},{5,6},{6,7},{7,8},{8,9},{9,10},{10,1... | collective-permute-start | bytes 296408 | tf_op jit(solution)/shard_map/ppermute | solution.py:47
  87.2 9.2 %collective-permute-start.14 = (f32[19,4,8,1]{3,2,1,0:T(8,128)S(1)}, f32[19,4,8,1]{3,2,1,0:T(8,128)S(1)}, u32[]{:S(2)}, u32[]{:S(2)}) collective-permute-start(f32[19,4,8,1]{3,2,1,0:T(8,128)S(1)} %get-tuple-element.287), channel_id=1, source_target_pairs={{0,128},{128,256},{256,384},{384,512},{512,640},{640,768},{768,896... | collective-permute-start | bytes 7304 | tf_op jit(solution)/shard_map/ppermute | solution.py:47
  92.3 8.6 %collective-permute-start.15 = (f32[19,4,8,1]{3,2,1,0:T(8,128)S(1)}, f32[19,4,8,1]{3,2,1,0:T(8,128)S(1)}, u32[]{:S(2)}, u32[]{:S(2)}) collective-permute-start(f32[19,4,8,1]{3,2,1,0:T(8,128)S(1)} %get-tuple-element.288), channel_id=1, source_target_pairs={{128,0},{256,128},{384,256},{512,384},{640,512},{768,640},{896,768... | collective-permute-start | bytes 7304 | tf_op jit(solution)/shard_map/ppermute | solution.py:50
  101.4 4.3 %collective-permute-start.16 = (f32[19,4,1,130]{3,2,1,0:T(1,128)S(1)}, f32[19,4,1,130]{3,2,1,0:T(1,128)S(1)}, u32[]{:S(2)}, u32[]{:S(2)}) collective-permute-start(f32[19,4,1,130]{3,2,1,0:T(1,128)S(1)} %get-tuple-element.279), channel_id=1, source_target_pairs={{0,32},{32,64},{64,96},{1,33},{33,65},{65,97},{2,34},{34,66},{66,9... | collective-permute-start | bytes 118568 | tf_op jit(solution)/shard_map/ppermute | solution.py:47
  104.2 5.1 %collective-permute-start.17 = (f32[19,4,1,130]{3,2,1,0:T(1,128)S(1)}, f32[19,4,1,130]{3,2,1,0:T(1,128)S(1)}, u32[]{:S(2)}, u32[]{:S(2)}) collective-permute-start(f32[19,4,1,130]{3,2,1,0:T(1,128)S(1)} %get-tuple-element.280), channel_id=1, source_target_pairs={{32,0},{64,32},{96,64},{33,1},{65,33},{97,65},{34,2},{66,34},{98,6... | collective-permute-start | bytes 118568 | tf_op jit(solution)/shard_map/ppermute | solution.py:50
  109.7 12.5 %collective-permute-start.19 = (f32[19,1,10,130]{3,2,1,0:T(8,128)S(1)}, f32[19,1,10,130]{3,2,1,0:T(8,128)S(1)}, u32[]{:S(2)}, u32[]{:S(2)}) collective-permute-start(f32[19,1,10,130]{3,2,1,0:T(8,128)S(1)} %get-tuple-element.271), channel_id=1, source_target_pairs={{1,0},{2,1},{3,2},{4,3},{5,4},{6,5},{7,6},{8,7},{9,8},{10,9},{11,1... | collective-permute-start | bytes 296408 | tf_op jit(solution)/shard_map/ppermute | solution.py:50
  111.6 11.8 %collective-permute-start.18 = (f32[19,1,10,130]{3,2,1,0:T(8,128)S(1)}, f32[19,1,10,130]{3,2,1,0:T(8,128)S(1)}, u32[]{:S(2)}, u32[]{:S(2)}) collective-permute-start(f32[19,1,10,130]{3,2,1,0:T(8,128)S(1)} %get-tuple-element.272), channel_id=1, source_target_pairs={{0,1},{1,2},{2,3},{3,4},{4,5},{5,6},{6,7},{7,8},{8,9},{9,10},{10,1... | collective-permute-start | bytes 296408 | tf_op jit(solution)/shard_map/ppermute | solution.py:47
  124.3 7.3 %collective-permute-start.20 = (f32[19,4,8,1]{3,2,1,0:T(8,128)S(1)}, f32[19,4,8,1]{3,2,1,0:T(8,128)S(1)}, u32[]{:S(2)}, u32[]{:S(2)}) collective-permute-start(f32[19,4,8,1]{3,2,1,0:T(8,128)S(1)} %get-tuple-element.285), channel_id=1, source_target_pairs={{0,128},{128,256},{256,384},{384,512},{512,640},{640,768},{768,896... | collective-permute-start | bytes 7304 | tf_op jit(solution)/shard_map/ppermute | solution.py:47
  127.7 8.1 %collective-permute-start.21 = (f32[19,4,8,1]{3,2,1,0:T(8,128)S(1)}, f32[19,4,8,1]{3,2,1,0:T(8,128)S(1)}, u32[]{:S(2)}, u32[]{:S(2)}) collective-permute-start(f32[19,4,8,1]{3,2,1,0:T(8,128)S(1)} %get-tuple-element.286), channel_id=1, source_target_pairs={{128,0},{256,128},{384,256},{512,384},{640,512},{768,640},{896,768... | collective-permute-start | bytes 7304 | tf_op jit(solution)/shard_map/ppermute | solution.py:50
  136.3 3.1 %collective-permute-start.22 = (f32[19,4,1,130]{3,2,1,0:T(1,128)S(1)}, f32[19,4,1,130]{3,2,1,0:T(1,128)S(1)}, u32[]{:S(2)}, u32[]{:S(2)}) collective-permute-start(f32[19,4,1,130]{3,2,1,0:T(1,128)S(1)} %get-tuple-element.277), channel_id=1, source_target_pairs={{0,32},{32,64},{64,96},{1,33},{33,65},{65,97},{2,34},{34,66},{66,9... | collective-permute-start | bytes 118568 | tf_op jit(solution)/shard_map/ppermute | solution.py:47
  138.0 5.1 %collective-permute-start.23 = (f32[19,4,1,130]{3,2,1,0:T(1,128)S(1)}, f32[19,4,1,130]{3,2,1,0:T(1,128)S(1)}, u32[]{:S(2)}, u32[]{:S(2)}) collective-permute-start(f32[19,4,1,130]{3,2,1,0:T(1,128)S(1)} %get-tuple-element.278), channel_id=1, source_target_pairs={{32,0},{64,32},{96,64},{33,1},{65,33},{97,65},{34,2},{66,34},{98,6... | collective-permute-start | bytes 118568 | tf_op jit(solution)/shard_map/ppermute | solution.py:50
  143.4 12.1 %collective-permute-start.24 = (f32[19,1,10,130]{3,2,1,0:T(8,128)S(1)}, f32[19,1,10,130]{3,2,1,0:T(8,128)S(1)}, u32[]{:S(2)}, u32[]{:S(2)}) collective-permute-start(f32[19,1,10,130]{3,2,1,0:T(8,128)S(1)} %get-tuple-element.269), channel_id=1, source_target_pairs={{0,1},{1,2},{2,3},{3,4},{4,5},{5,6},{6,7},{7,8},{8,9},{9,10},{10,1... | collective-permute-start | bytes 296408 | tf_op jit(solution)/shard_map/ppermute | solution.py:47
  151.7 9.4 %collective-permute-start.25 = (f32[19,1,10,130]{3,2,1,0:T(8,128)S(1)}, f32[19,1,10,130]{3,2,1,0:T(8,128)S(1)}, u32[]{:S(2)}, u32[]{:S(2)}) collective-permute-start(f32[19,1,10,130]{3,2,1,0:T(8,128)S(1)} %get-tuple-element.270), channel_id=1, source_target_pairs={{1,0},{2,1},{3,2},{4,3},{5,4},{6,5},{7,6},{8,7},{9,8},{10,9},{11,1... | collective-permute-start | bytes 296408 | tf_op jit(solution)/shard_map/ppermute | solution.py:50
  161.7 0.7 copy-start.3
  163.2 0.7 copy-start.5
where the time goes:
time: 165 us; the launch traced here: 164 us
  starting transfers between devices  82.9 us (50%)
  waiting for transfers between devices  65.8 us (40%)
  other arithmetic  7.82 us (5%)
  local copies, waits for them, and re-layouts  4.89 us (3%)
  between operations  2.94 us (2%)
    ppermute x12, starting transfers between devices, with_halo(): lax.ppermute(lax.slice_in_dim(block, block.shape[dim] - width, None, axis...  57.2 us
    ppermute x12, waiting for transfers between devices, with_halo(): lax.ppermute(lax.slice_in_dim(block, 0, width, axis=dim), axis, backward)  45 us
    ppermute x12, starting transfers between devices, with_halo(): lax.ppermute(lax.slice_in_dim(block, 0, width, axis=dim), axis, backward)  18 us
    ppermute x12, waiting for transfers between devices, with_halo(): lax.ppermute(lax.slice_in_dim(block, block.shape[dim] - width, None, axis...  17.5 us
    ppermute x2, starting transfers between devices, passed_along(): return lax.ppermute(shard, axis, pairs)  7.69 us
  transfers between devices with their start and end apart: 26, of which 25 were waited for; matrix products, arithmetic and copies ran while one was open for 0% of the time, Pallas kernels for 0%

commit v1 on v0

v1 whole, which is shorter than its diff:
```python
import functools

import jax
import jax.numpy as jnp
from jax import lax
from jax.experimental import pallas as pl
from jax.experimental.pallas import tpu as pltpu
from jax.sharding import PartitionSpec as P


VELOCITIES = [
    (0, 0, 0),
    (1, 0, 0),
    (-1, 0, 0),
    (0, 1, 0),
    (0, -1, 0),
    (0, 0, 1),
    (0, 0, -1),
    (1, 1, 0),
    (-1, -1, 0),
    (1, -1, 0),
    (-1, 1, 0),
    (1, 0, 1),
    (-1, 0, -1),
    (1, 0, -1),
    (-1, 0, 1),
    (0, 1, 1),
    (0, -1, -1),
    (0, 1, -1),
    (0, -1, 1),
]
OPPOSITE = [0, 2, 1, 4, 3, 6, 5, 8, 7, 10, 9, 12, 11, 14, 13, 16, 15, 18, 17]
Q = 19
UP_Y = [i for i in range(Q) if VELOCITIES[i][1] == 1]
DOWN_Y = [i for i in range(Q) if VELOCITIES[i][1] == -1]
SOLID = 3.0e38
F32 = jnp.float32
VMEM = pl.BlockSpec(memory_space=pltpu.VMEM)
SMEM = pl.BlockSpec(memory_space=pltpu.SMEM)
ANY = pl.BlockSpec(memory_space=pl.ANY)


def shape(*dims):
    return jax.ShapeDtypeStruct(dims, F32)


def lanes():
    return lax.broadcasted_iota(jnp.int32, (8, 128), 1)


def sublanes():
    return lax.broadcasted_iota(jnp.int32, (8, 128), 0)


def roll(value, sublane_shift, lane_shift):
    if sublane_shift % 8:
        value = pltpu.roll(value, sublane_shift % 8, 0)
    if lane_shift % 128:
        value = pltpu.roll(value, lane_shift % 128, 1)
    return value


def relax(g):
    sums = [g[k] + g[k + 1] for k in range(1, Q, 2)]
    diffs = [g[k] - g[k + 1] for k in range(1, Q, 2)]
    axis_sum = sums[0] + sums[1] + sums[2]
    edge_sum = (sums[3] + sums[4]) + (sums[5] + sums[6]) + (sums[7] + sums[8])
    density = 12.0 * g[0] + 2.0 * axis_sum + edge_sum
    moment_z = 2.0 * diffs[0] + ((diffs[3] + diffs[4]) + (diffs[5] + diffs[6]))
    moment_y = 2.0 * diffs[1] + ((diffs[3] - diffs[4]) + (diffs[7] + diffs[8]))
    moment_x = 2.0 * diffs[2] + ((diffs[5] - diffs[6]) + (diffs[7] - diffs[8]))
    inverse = 1.0 / density
    speed = [moment_z * inverse, moment_y * inverse, moment_x * inverse]
    square = speed[0] * speed[0] + speed[1] * speed[1] + speed[2] * speed[2]
    scaled = density * (1.5 / 36.0)
    base = scaled * (1.0 - 1.5 * square)
    linear = [(4.5 / 36.0) * m for m in (moment_z, moment_y, moment_x)]
    speed = [1.5 * s for s in speed]
    out = [base - 0.5 * g[0]]
    for pair in range(9):
        velocity = VELOCITIES[1 + 2 * pair]
        along = None
        twice = None
        for axis in range(3):
            if velocity[axis] == 0:
                continue
            if along is None:
                along, twice = linear[axis], speed[axis]
            elif velocity[axis] > 0:
                along, twice = along + linear[axis], twice + speed[axis]
            else:
                along, twice = along - linear[axis], twice - speed[axis]
        even = base + along * twice - 0.25 * sums[pair]
        odd = along - 0.25 * diffs[pair]
        out += [even + odd, even - odd]
    return out


def relax_wet(g, wet):
    return [jnp.where(wet, value, SOLID) for value in relax(g)]


def stream_row(ref, row, first):
    at = row - first
    out = [ref[0, at]]
    for i in range(1, Q):
        step_z, step_y, step_x = VELOCITIES[i]
        source = roll(ref[i, at - step_y], step_z, step_x)
        out.append(jnp.where(source == SOLID, ref[OPPOSITE[i], at], source))
    return out


def stream_patch(values):
    out = [values[0]]
    for i in range(1, Q):
        step_z, step_y, step_x = VELOCITIES[i]
        source = roll(values[i], step_z, 8 * step_y + step_x)
        out.append(jnp.where(source == SOLID, values[OPPOSITE[i]], source))
    return out


def over_rows(first, last, body):
    def step(row, carry):
        body(row)
        return carry

    lax.fori_loop(first, last, step, 0)


def gather_columns(values, rows):
    lane_row = lanes() // 8
    tile = jnp.full((8, 128), SOLID, F32)
    for row, value in zip(rows, values):
        tile = jnp.where(lane_row == row, roll(value, 0, 8 * row + 4), tile)
    return tile


def split_slabs(relative, fluid, low, high, sems):
    copies = [
        pltpu.make_async_copy(relative.at[:, 0:2], low.at[0:Q], sems.at[0]),
        pltpu.make_async_copy(relative.at[:, 2:4], high.at[0:Q], sems.at[1]),
    ]
    for copy in copies:
        copy.start()
    low[Q] = fluid[0:2].astype(F32)
    high[Q] = fluid[2:4].astype(F32)
    for copy in copies:
        copy.wait()


def first_relax(low, high, below, above, owner, own, y_low, y_high, turn):
    place = lax.axis_index("gz")
    swap_low = owner[0, 0, 0] == place - 1
    swap_high = owner[1, 0, 0] == place + 1
    kinds = [below[Q, 0], below[Q, 1], low[Q, 0], low[Q, 1], high[Q, 0], high[Q, 1], above[Q, 0], above[Q, 1]]
    for layer in range(8):
        turn[Q, 8 * layer : 8 * layer + 8] = kinds[layer]

    def home(i, carry):
        for k in range(2):
            mine, other = low[i, k], below[i, k]
            turn[i, 8 * k : 8 * k + 8] = jnp.where(swap_low, mine, other)
            turn[i, 8 * (k + 2) : 8 * (k + 3)] = jnp.where(swap_low, other, mine)
            mine, other = high[i, k], above[i, k]
            turn[i, 8 * (k + 4) : 8 * (k + 5)] = jnp.where(swap_high, other, mine)
            turn[i, 8 * (k + 6) : 8 * (k + 7)] = jnp.where(swap_high, mine, other)
        return carry

    lax.fori_loop(0, Q, home, 0)
    for row in range(8):
        wet = turn[Q, pl.ds(row, 8, stride=8)] > 0.5
        values = relax_wet([turn[i, pl.ds(row, 8, stride=8)] for i in range(Q)], wet)
        for i in range(Q):
            own[i, row] = values[i]
            if row < 3:
                y_low[3 * i + row] = values[i]
            if row > 4:
                y_high[3 * i + row - 5] = values[i]
        if row == 3:
            for k, i in enumerate(DOWN_Y):
                y_low[3 * Q + k] = values[i]
        if row == 4:
            for k, i in enumerate(UP_Y):
                y_high[3 * Q + k] = values[i]


def join_rows(own, below, above, main, edge):
    place = lax.axis_index("gy")
    at_low = place == 0
    at_high = place == lax.axis_size("gy") - 1
    for i in range(Q):
        rows = []
        if i in UP_Y:
            rows.append(jnp.where(at_low, SOLID, below[3 * Q + UP_Y.index(i)]))
        else:
            rows.append(jnp.full((8, 128), SOLID, F32))
        for k in range(3):
            rows.append(jnp.where(at_low, SOLID, below[3 * i + k]))
        for k in range(8):
            rows.append(own[i, k])
        for k in range(3):
            rows.append(jnp.where(at_high, SOLID, above[3 * i + k]))
        if i in DOWN_Y:
            rows.append(jnp.where(at_high, SOLID, above[3 * Q + DOWN_Y.index(i)]))
        else:
            rows.append(jnp.full((8, 128), SOLID, F32))
        for k in range(16):
            main[i, k] = rows[k]
        edge[i] = gather_columns(rows, range(16))


def two_steps(main, out, middle):
    def first(row):
        wet = main[0, row] != SOLID
        values = relax_wet(stream_row(main, row, 0), wet)
        for i in range(Q):
            middle[i, row - 1] = values[i]

    def second(row):
        wet = middle[0, row - 1] != SOLID
        values = relax_wet(stream_row(middle, row, 1), wet)
        for i in range(Q):
            out[i, row - 2] = values[i]

    over_rows(1, 15, first)
    over_rows(2, 14, second)


def patch_two_steps(inner, edge, left, right, main, below, above, halo):
    place = lax.axis_index("gx")
    at_low = place == 0
    at_high = place == lax.axis_size("gx") - 1
    low_side = lanes() % 8 < 4
    sides = []
    for side in range(2):
        values = []
        for i in range(Q):
            if side == 0:
                value = jnp.where(low_side, jnp.where(at_low, SOLID, left[i]), edge[i])
            else:
                value = jnp.where(low_side, edge[i], jnp.where(at_high, SOLID, right[i]))
            values.append(value)
        for step in range(2):
            wet = values[0] != SOLID
            values = relax_wet(stream_patch(values), wet)
        sides.append(values)
    lane = lanes()
    seam = (lane < 2) | (lane >= 126)
    sublane_pair = sublanes() // 2
    for i in range(Q):
        own_columns = jnp.where(low_side, sides[1][i], sides[0][i])
        halo[i] = jnp.where(low_side, sides[0][i], sides[1][i])
        for group in range(3):
            pack_low = None
            pack_high = None
            for k in range(4):
                row = 4 * group + k
                value = jnp.where(seam, roll(own_columns, 0, -(8 * (row + 2) + 4)), inner[i, row])
                main[i, row] = value
                to_low, to_high = roll(value, 2 * k - 2, 0), roll(value, 2 * k - 4, 0)
                if pack_low is None:
                    pack_low, pack_high = to_low, to_high
                else:
                    pack_low = jnp.where(sublane_pair == k, to_low, pack_low)
                    pack_high = jnp.where(sublane_pair == k, to_high, pack_high)
            below[3 * i + group] = pack_low
            above[3 * i + group] = pack_high
    for group in range(5):
        pack_low = None
        pack_high = None
        for k in range(4):
            value = halo[min(4 * group + k, Q - 1)]
            to_low, to_high = roll(value, 2 * k - 2, 0), roll(value, 2 * k - 4, 0)
            if pack_low is None:
                pack_low, pack_high = to_low, to_high
            else:
                pack_low = jnp.where(sublane_pair == k, to_low, pack_low)
                pack_high = jnp.where(sublane_pair == k, to_high, pack_high)
        below[3 * Q + group] = pack_low
        above[3 * Q + group] = pack_high


def last_two_steps(main, halo, below, above, block_fluid, out, block_density, joined, middle, turn):
    place = lax.axis_index("gz")
    at_low = place == 0
    at_high = place == lax.axis_size("gz") - 1
    sublane = sublanes()
    lane = lanes()
    low_side = lane % 8 < 4

    def with_layers(value, low, high, k):
        low = roll(jnp.where(at_low, SOLID, low), -2 * k, 0)
        high = roll(jnp.where(at_high, SOLID, high), 6 - 2 * k, 0)
        return jnp.where(sublane < 2, low, jnp.where(sublane >= 6, high, value))

    patches = [[], []]
    for i in range(Q):
        rows = []
        for group in range(3):
            low, high = below[3 * i + group], above[3 * i + group]
            for k in range(4):
                value = with_layers(main[i, 4 * group + k], low, high, k)
                joined[i, 4 * group + k] = value
                rows.append(value)
        edge = gather_columns(rows, range(2, 14))
        group, k = divmod(i, 4)
        side = with_layers(halo[i], below[3 * Q + group], above[3 * Q + group], k)
        patches[0].append(jnp.where(low_side, side, edge))
        patches[1].append(jnp.where(low_side, edge, side))

    def third(row):
        wet = joined[0, row - 2] != SOLID
        values = relax_wet(stream_row(joined, row, 2), wet)
        for i in range(Q):
            middle[i, row - 3] = values[i]

    over_rows(3, 13, third)
    for side in range(2):
        wet = patches[side][0] != SOLID
        values = relax_wet(stream_patch(patches[side]), wet)
        patches[side] = stream_patch(values)
    own_columns = [jnp.where(low_side, patches[1][i], patches[0][i]) for i in range(Q)]
    seam = (lane < 2) | (lane >= 126)
    for row in range(8):
        wet = middle[0, row + 1] != SOLID
        values = stream_row(middle, row + 4, 3)
        for i in range(Q):
            value = jnp.where(seam, roll(own_columns[i], 0, -(8 * (row + 4) + 4)), values[i])
            turn[i, 8 * row : 8 * row + 8] = jnp.where(wet, value, 0.0)
    for slot in range(2):
        mass = None
        for k in range(2):
            layer = 2 * slot + k
            values = [turn[i, pl.ds(layer + 2, 8, stride=8)] for i in range(Q)]
            for i in range(Q):
                out[i, layer] = values[i]
            axis_sum = functools.reduce(jnp.add, values[1:7])
            edge_sum = functools.reduce(jnp.add, values[7:])
            density = values[0] * (1.0 / 3.0) + axis_sum * (1.0 / 18.0) + edge_sum * (1.0 / 36.0)
            mass = density if mass is None else mass + density
        count = jnp.maximum(block_fluid[slot, 0, 0], 1).astype(F32)
        block_density[slot, 0, 0] = jnp.sum(mass) / count


def exchange(to_low, to_high, axis):
    count = lax.axis_size(axis)
    up = [(i, i + 1) for i in range(count - 1)]
    down = [(i + 1, i) for i in range(count - 1)]
    return lax.ppermute(to_high, axis, up), lax.ppermute(to_low, axis, down)


def call(kernel, outs, in_specs, out_specs=None, scratch=()):
    if out_specs is None:
        out_specs = [VMEM] * len(outs)
    return pl.pallas_call(
        kernel,
        out_shape=outs,
        in_specs=in_specs,
        out_specs=out_specs,
        scratch_shapes=list(scratch),
        compiler_params=pltpu.CompilerParams(vmem_limit_bytes=32 * 1024 * 1024),
    )


def on_device(relative, fluid, block_fluid, new_owner):
    low, high = call(
        split_slabs,
        [shape(Q + 1, 2, 8, 128)] * 2,
        [ANY, VMEM],
        scratch=[pltpu.SemaphoreType.DMA((2,))],
    )(relative, fluid)
    below, above = exchange(low, high, "gz")
    own, y_low, y_high = call(
        first_relax,
        [shape(Q, 8, 8, 128), shape(3 * Q + 5, 8, 128), shape(3 * Q + 5, 8, 128)],
        [VMEM] * 4 + [SMEM],
        scratch=[pltpu.VMEM((Q + 1, 64, 128), F32)],
    )(low, high, below, above, new_owner)
    below, above = exchange(y_low, y_high, "gy")
    main, edge = call(
        join_rows, [shape(Q, 16, 8, 128), shape(Q, 8, 128)], [VMEM] * 3
    )(own, below, above)
    left, right = exchange(edge, edge, "gx")
    inner = call(
        two_steps,
        [shape(Q, 12, 8, 128)],
        [VMEM],
        scratch=[pltpu.VMEM((Q, 14, 8, 128), F32)],
    )(main)[0]
    main, z_low, z_high, halo = call(
        patch_two_steps,
        [shape(Q, 12, 8, 128), shape(3 * Q + 5, 8, 128), shape(3 * Q + 5, 8, 128), shape(Q, 8, 128)],
        [VMEM] * 4,
    )(inner, edge, left, right)
    below, above = exchange(z_low, z_high, "gz")
    out, block_density = call(
        last_two_steps,
        [shape(Q, 4, 8, 128), shape(2, 1, 1)],
        [VMEM] * 4 + [SMEM],
        [VMEM, SMEM],
        scratch=[
            pltpu.VMEM((Q, 12, 8, 128), F32),
            pltpu.VMEM((Q, 10, 8, 128), F32),
            pltpu.VMEM((Q, 64, 128), F32),
        ],
    )(main, halo, below, above, block_fluid)
    return out, block_density


def solution(mesh):
    return jax.shard_map(
        on_device,
        mesh=mesh,
        in_specs=(
            P(None, "gz", "gy", "gx"),
            P("gz", "gy", "gx"),
            P("gz", "gy", "gx"),
            P("gz", "gy", "gx"),
        ),
        out_specs=(P(None, "gz", "gy", "gx"), P("gz", "gy", "gx")),
        check_vma=False,
    )
```

time: 165 us -> 59.1 us (0.36)
  the two profiles are of different devices: /device:TPU:193 before, /device:TPU:217 now
where the time goes in v1:
time: 59.1 us; the launch traced here: 58.7 us
  starting transfers between devices  27.5 us (47%)
  waiting for transfers between devices  19.2 us (32%)
  Pallas kernels  8.04 us (14%)
  local copies, waits for them, and re-layouts  3.12 us (5%)
  between operations  0.78 us (1%)
    ppermute x8, starting transfers between devices, exchange(): return (lax.ppermute(to_high, axis, up), lax.ppermute(to_low, axis, down))  27.5 us
    ppermute x8, waiting for transfers between devices, exchange(): return (lax.ppermute(to_high, axis, up), lax.ppermute(to_low, axis, down))  19.2 us
    pallas_call x1, Pallas kernels, on_device(): call(last_two_steps, [shape(Q, 4, 8, 128), shape(2, 1, 1)], [VMEM] * 4 +...  3.18 us
    pallas_call x1, Pallas kernels, on_device(): call(two_steps, [shape(Q, 12, 8, 128)], [VMEM], scratch=[pltpu.VMEM((Q, 1...  2.86 us
    unnamed x8, local copies, waits for them, and re-layouts  2.52 us
  transfers between devices with their start and end apart: 8, of which 6 were waited for; matrix products, arithmetic and copies ran while one was open for 1% of the time, Pallas kernels for 5%

profile of v1, /device:TPU:217, one launch (start us, length us, event | category | flops | bytes accessed | tf_op | source)
XLA Modules:
  0.0 58.7 jit_solution(7383445031821176751)
XLA Ops:
  0.6 0.0 copy-start
  0.6 1.0 %copy-done = f32[19,4,8,128]{3,2,1,0:T(8,128)S(1)} copy-done((f32[19,4,8,128]{3,2,1,0:T(8,128)S(1)}, f32[19,4,8,128]{3,2,1,0:T(8,128)}, u32[]{:S(2)}) %copy-start) | copy-done | bytes 311320
  1.6 0.0 copy-start.1
  1.6 0.7 %copy-done.1 = s32[4,8,128]{2,1,0:T(8,128)S(1)} copy-done((s32[4,8,128]{2,1,0:T(8,128)S(1)}, s32[4,8,128]{2,1,0:T(8,128)}, u32[]{:S(2)}) %copy-start.1) | copy-done | bytes 16408
  2.3 0.1 shard_map.59
  2.4 5.8 %collective-permute-start = (f32[20,2,8,128]{3,2,1,0:T(8,128)S(1)}, f32[20,2,8,128]{3,2,1,0:T(8,128)S(1)}, u32[]{:S(2)}, u32[]{:S(2)}) collective-permute-start(f32[20,2,8,128]{3,2,1,0:T(8,128)S(1)} %get-tuple-element.14.high), channel_id=1, source_target_pairs={{0,1},{1,2},{2,3},{3,4},{4,5},{5,6},{6,7},{7,8},{8,9},{9,10},{10,1... | collective-permute-start | bytes 491528 | tf_op jit(solution)/shard_map/ppermute | solution.py:349
  8.2 1.9 %collective-permute-start.1 = (f32[20,2,8,128]{3,2,1,0:T(8,128)S(1)}, f32[20,2,8,128]{3,2,1,0:T(8,128)S(1)}, u32[]{:S(2)}, u32[]{:S(2)}) collective-permute-start(f32[20,2,8,128]{3,2,1,0:T(8,128)S(1)} %get-tuple-element.13.low), channel_id=1, source_target_pairs={{1,0},{2,1},{3,2},{4,3},{5,4},{6,5},{7,6},{8,7},{9,8},{10,9},{11,1... | collective-permute-start | bytes 491528 | tf_op jit(solution)/shard_map/ppermute | solution.py:349
  10.1 0.7 %copy.6.owner = s32[2,1,1]{2,1,0:T(1,128)S(1)} copy(s32[2,1,1]{0,2,1:T(1,128)} %param.7) | data formatting | bytes 16 | tf_op args[3]
  10.8 0.0 collective-permute-done.below
  10.8 5.2 %collective-permute-done.1.above = f32[20,2,8,128]{3,2,1,0:T(8,128)S(1)} collective-permute-done((f32[20,2,8,128]{3,2,1,0:T(8,128)S(1)}, f32[20,2,8,128]{3,2,1,0:T(8,128)S(1)}, u32[]{:S(2)}, u32[]{:S(2)}) %collective-permute-start.1) | collective-permute-done | bytes 163872 | tf_op jit(solution)/shard_map/ppermute | solution.py:349
  16.0 1.0 %shard_map.60 = (f32[19,8,8,128]{3,2,1,0:T(8,128)S(1)}, f32[62,8,128]{2,1,0:T(8,128)S(1)}, f32[62,8,128]{2,1,0:T(8,128)S(1)}) custom-call(f32[20,2,8,128]{3,2,1,0:T(8,128)S(1)} %get-tuple-element.13.low, f32[20,2,8,128]{3,2,1,0:T(8,128)S(1)} %get-tuple-element.14.high, f32[20,2,8,128]{3,2,1,0:T(8,128)S(1)} %collective-permute-done.below, ...), custom_call_target="tpu_custom_call" | custom-call | tf_op jit(solution)/shard_map/pallas_call | solution.py:373
  17.0 3.1 %collective-permute-start.2 = (f32[62,8,128]{2,1,0:T(8,128)S(1)}, f32[62,8,128]{2,1,0:T(8,128)S(1)}, u32[]{:S(2)}, u32[]{:S(2)}) collective-permute-start(f32[62,8,128]{2,1,0:T(8,128)S(1)} %get-tuple-element.16), channel_id=1, source_target_pairs={{0,32},{32,64},{64,96},{1,33},{33,65},{65,97},{2,34},{34,66},{66,9... | collective-permute-start | bytes 761864 | tf_op jit(solution)/shard_map/ppermute | solution.py:349
  20.2 1.3 %collective-permute-start.3 = (f32[62,8,128]{2,1,0:T(8,128)S(1)}, f32[62,8,128]{2,1,0:T(8,128)S(1)}, u32[]{:S(2)}, u32[]{:S(2)}) collective-permute-start(f32[62,8,128]{2,1,0:T(8,128)S(1)} %get-tuple-element.17), channel_id=1, source_target_pairs={{32,0},{64,32},{96,64},{33,1},{65,33},{97,65},{34,2},{66,34},{98,6... | collective-permute-start | bytes 761864 | tf_op jit(solution)/shard_map/ppermute | solution.py:349
  21.5 1.9 %collective-permute-done.2.below = f32[62,8,128]{2,1,0:T(8,128)S(1)} collective-permute-done((f32[62,8,128]{2,1,0:T(8,128)S(1)}, f32[62,8,128]{2,1,0:T(8,128)S(1)}, u32[]{:S(2)}, u32[]{:S(2)}) %collective-permute-start.2) | collective-permute-done | bytes 253984 | tf_op jit(solution)/shard_map/ppermute | solution.py:349
  23.4 3.8 %collective-permute-done.3.above = f32[62,8,128]{2,1,0:T(8,128)S(1)} collective-permute-done((f32[62,8,128]{2,1,0:T(8,128)S(1)}, f32[62,8,128]{2,1,0:T(8,128)S(1)}, u32[]{:S(2)}, u32[]{:S(2)}) %collective-permute-start.3) | collective-permute-done | bytes 253984 | tf_op jit(solution)/shard_map/ppermute | solution.py:349
  27.2 0.4 shard_map.61
  27.6 4.4 %collective-permute-start.4 = (f32[19,8,128]{2,1,0:T(8,128)S(1)}, f32[19,8,128]{2,1,0:T(8,128)S(1)}, u32[]{:S(2)}, u32[]{:S(2)}) collective-permute-start(f32[19,8,128]{2,1,0:T(8,128)S(1)} %get-tuple-element.19.edge), channel_id=1, source_target_pairs={{0,128},{128,256},{256,384},{384,512},{512,640},{640,768},{768,896... | collective-permute-start | bytes 233480 | tf_op jit(solution)/shard_map/ppermute | solution.py:349
  32.0 1.9 %collective-permute-start.5 = (f32[19,8,128]{2,1,0:T(8,128)S(1)}, f32[19,8,128]{2,1,0:T(8,128)S(1)}, u32[]{:S(2)}, u32[]{:S(2)}) collective-permute-start(f32[19,8,128]{2,1,0:T(8,128)S(1)} %get-tuple-element.19.edge), channel_id=1, source_target_pairs={{128,0},{256,128},{384,256},{512,384},{640,512},{768,640},{896,768... | collective-permute-start | bytes 233480 | tf_op jit(solution)/shard_map/ppermute | solution.py:349
  33.9 0.0 copy-start.2
  33.9 2.9 %shard_map.62.inner = f32[19,12,8,128]{3,2,1,0:T(8,128)S(1)} custom-call(f32[19,16,8,128]{3,2,1,0:T(8,128)S(1)} %get-tuple-element.18.main), custom_call_target="tpu_custom_call" | custom-call | tf_op jit(solution)/shard_map/pallas_call | solution.py:384
  36.8 0.0 collective-permute-done.4.left
  36.8 1.5 %collective-permute-done.5.right = f32[19,8,128]{2,1,0:T(8,128)S(1)} collective-permute-done((f32[19,8,128]{2,1,0:T(8,128)S(1)}, f32[19,8,128]{2,1,0:T(8,128)S(1)}, u32[]{:S(2)}, u32[]{:S(2)}) %collective-permute-start.5) | collective-permute-done | bytes 77856 | tf_op jit(solution)/shard_map/ppermute | solution.py:349
  38.3 0.6 shard_map.63
  38.9 7.1 %collective-permute-start.6 = (f32[62,8,128]{2,1,0:T(8,128)S(1)}, f32[62,8,128]{2,1,0:T(8,128)S(1)}, u32[]{:S(2)}, u32[]{:S(2)}) collective-permute-start(f32[62,8,128]{2,1,0:T(8,128)S(1)} %get-tuple-element.22), channel_id=1, source_target_pairs={{0,1},{1,2},{2,3},{3,4},{4,5},{5,6},{6,7},{7,8},{8,9},{9,10},{10,1... | collective-permute-start | bytes 761864 | tf_op jit(solution)/shard_map/ppermute | solution.py:349
  46.1 1.9 %collective-permute-start.7 = (f32[62,8,128]{2,1,0:T(8,128)S(1)}, f32[62,8,128]{2,1,0:T(8,128)S(1)}, u32[]{:S(2)}, u32[]{:S(2)}) collective-permute-start(f32[62,8,128]{2,1,0:T(8,128)S(1)} %get-tuple-element.23), channel_id=1, source_target_pairs={{1,0},{2,1},{3,2},{4,3},{5,4},{6,5},{7,6},{8,7},{9,8},{10,9},{11,1... | collective-permute-start | bytes 761864 | tf_op jit(solution)/shard_map/ppermute | solution.py:349
  48.0 0.0 copy-done.2
  48.0 0.1 copy.7.block_fluid
  48.1 1.2 %collective-permute-done.6.below = f32[62,8,128]{2,1,0:T(8,128)S(1)} collective-permute-done((f32[62,8,128]{2,1,0:T(8,128)S(1)}, f32[62,8,128]{2,1,0:T(8,128)S(1)}, u32[]{:S(2)}, u32[]{:S(2)}) %collective-permute-start.6) | collective-permute-done | bytes 253984 | tf_op jit(solution)/shard_map/ppermute | solution.py:349
  49.3 5.6 %collective-permute-done.7.above = f32[62,8,128]{2,1,0:T(8,128)S(1)} collective-permute-done((f32[62,8,128]{2,1,0:T(8,128)S(1)}, f32[62,8,128]{2,1,0:T(8,128)S(1)}, u32[]{:S(2)}, u32[]{:S(2)}) %collective-permute-start.7) | collective-permute-done | bytes 253984 | tf_op jit(solution)/shard_map/ppermute | solution.py:349
  54.9 3.2 %shard_map.64 = (f32[19,4,8,128]{3,2,1,0:T(8,128)}, f32[2,1,1]{2,1,0:T(1,128)S(1)}) custom-call(f32[19,12,8,128]{3,2,1,0:T(8,128)S(1)} %get-tuple-element.20.main, f32[19,8,128]{2,1,0:T(8,128)S(1)} %get-tuple-element.21.halo, f32[62,8,128]{2,1,0:T(8,128)S(1)} %collective-permute-done.6.below, f32[62,8,128]{2,1,0:T(8,128)S(1)} %collective-permute-done.7.above, ...), custom_call_target="tpu_custom_call" | custom-call | tf_op jit(solution)/shard_map/pallas_call | solution.py:396
  58.1 0.6 %copy.8 = f32[2,1,1]{0,2,1:T(1,128)} copy(f32[2,1,1]{2,1,0:T(1,128)S(1)} %get-tuple-element.25) | data formatting | bytes 16 | tf_op jit(solution)/shard_map/pallas_call | solution.py:396
Async XLA Ops:
  0.6 1.0 %copy-start = (f32[19,4,8,128]{3,2,1,0:T(8,128)S(1)}, f32[19,4,8,128]{3,2,1,0:T(8,128)}, u32[]{:S(2)}) copy-start(f32[19,4,8,128]{3,2,1,0:T(8,128)} %relative.1) | copy-start | bytes 933892
  1.6 0.7 %copy-start.1 = (s32[4,8,128]{2,1,0:T(8,128)S(1)}, s32[4,8,128]{2,1,0:T(8,128)}, u32[]{:S(2)}) copy-start(s32[4,8,128]{2,1,0:T(8,128)} %fluid.1) | copy-start | bytes 49156
  2.4 8.5 %collective-permute-start = (f32[20,2,8,128]{3,2,1,0:T(8,128)S(1)}, f32[20,2,8,128]{3,2,1,0:T(8,128)S(1)}, u32[]{:S(2)}, u32[]{:S(2)}) collective-permute-start(f32[20,2,8,128]{3,2,1,0:T(8,128)S(1)} %get-tuple-element.14.high), channel_id=1, source_target_pairs={{0,1},{1,2},{2,3},{3,4},{4,5},{5,6},{6,7},{7,8},{8,9},{9,10},{10,1... | collective-permute-start | bytes 491528 | tf_op jit(solution)/shard_map/ppermute | solution.py:349
  8.2 7.8 %collective-permute-start.1 = (f32[20,2,8,128]{3,2,1,0:T(8,128)S(1)}, f32[20,2,8,128]{3,2,1,0:T(8,128)S(1)}, u32[]{:S(2)}, u32[]{:S(2)}) collective-permute-start(f32[20,2,8,128]{3,2,1,0:T(8,128)S(1)} %get-tuple-element.13.low), channel_id=1, source_target_pairs={{1,0},{2,1},{3,2},{4,3},{5,4},{6,5},{7,6},{8,7},{9,8},{10,9},{11,1... | collective-permute-start | bytes 491528 | tf_op jit(solution)/shard_map/ppermute | solution.py:349
  17.0 6.3 %collective-permute-start.2 = (f32[62,8,128]{2,1,0:T(8,128)S(1)}, f32[62,8,128]{2,1,0:T(8,128)S(1)}, u32[]{:S(2)}, u32[]{:S(2)}) collective-permute-start(f32[62,8,128]{2,1,0:T(8,128)S(1)} %get-tuple-element.16), channel_id=1, source_target_pairs={{0,32},{32,64},{64,96},{1,33},{33,65},{65,97},{2,34},{34,66},{66,9... | collective-permute-start | bytes 761864 | tf_op jit(solution)/shard_map/ppermute | solution.py:349
  20.2 7.0 %collective-permute-start.3 = (f32[62,8,128]{2,1,0:T(8,128)S(1)}, f32[62,8,128]{2,1,0:T(8,128)S(1)}, u32[]{:S(2)}, u32[]{:S(2)}) collective-permute-start(f32[62,8,128]{2,1,0:T(8,128)S(1)} %get-tuple-element.17), channel_id=1, source_target_pairs={{32,0},{64,32},{96,64},{33,1},{65,33},{97,65},{34,2},{66,34},{98,6... | collective-permute-start | bytes 761864 | tf_op jit(solution)/shard_map/ppermute | solution.py:349
  27.6 9.2 %collective-permute-start.4 = (f32[19,8,128]{2,1,0:T(8,128)S(1)}, f32[19,8,128]{2,1,0:T(8,128)S(1)}, u32[]{:S(2)}, u32[]{:S(2)}) collective-permute-start(f32[19,8,128]{2,1,0:T(8,128)S(1)} %get-tuple-element.19.edge), channel_id=1, source_target_pairs={{0,128},{128,256},{256,384},{384,512},{512,640},{640,768},{768,896... | collective-permute-start | bytes 233480 | tf_op jit(solution)/shard_map/ppermute | solution.py:349
  32.0 6.4 %collective-permute-start.5 = (f32[19,8,128]{2,1,0:T(8,128)S(1)}, f32[19,8,128]{2,1,0:T(8,128)S(1)}, u32[]{:S(2)}, u32[]{:S(2)}) collective-permute-start(f32[19,8,128]{2,1,0:T(8,128)S(1)} %get-tuple-element.19.edge), channel_id=1, source_target_pairs={{128,0},{256,128},{384,256},{512,384},{640,512},{768,640},{896,768... | collective-permute-start | bytes 233480 | tf_op jit(solution)/shard_map/ppermute | solution.py:349
  33.9 14.1 %copy-start.2 = (s32[2,1,1]{0,2,1:T(1,128)S(1)}, s32[2,1,1]{0,2,1:T(1,128)}, u32[]{:S(2)}) copy-start(s32[2,1,1]{0,2,1:T(1,128)} %param.6) | copy-start | bytes 28
  38.9 10.4 %collective-permute-start.6 = (f32[62,8,128]{2,1,0:T(8,128)S(1)}, f32[62,8,128]{2,1,0:T(8,128)S(1)}, u32[]{:S(2)}, u32[]{:S(2)}) collective-permute-start(f32[62,8,128]{2,1,0:T(8,128)S(1)} %get-tuple-element.22), channel_id=1, source_target_pairs={{0,1},{1,2},{2,3},{3,4},{4,5},{5,6},{6,7},{7,8},{8,9},{9,10},{10,1... | collective-permute-start | bytes 761864 | tf_op jit(solution)/shard_map/ppermute | solution.py:349
  46.1 8.8 %collective-permute-start.7 = (f32[62,8,128]{2,1,0:T(8,128)S(1)}, f32[62,8,128]{2,1,0:T(8,128)S(1)}, u32[]{:S(2)}, u32[]{:S(2)}) collective-permute-start(f32[62,8,128]{2,1,0:T(8,128)S(1)} %get-tuple-element.23), channel_id=1, source_target_pairs={{1,0},{2,1},{3,2},{4,3},{5,4},{6,5},{7,6},{8,7},{9,8},{10,9},{11,1... | collective-permute-start | bytes 761864 | tf_op jit(solution)/shard_map/ppermute | solution.py:349

commit v2 on v1

v2 whole, which is shorter than its diff:
```python
import functools

import jax
import jax.numpy as jnp
from jax import lax
from jax.experimental import pallas as pl
from jax.experimental.pallas import tpu as pltpu
from jax.sharding import PartitionSpec as P


VELOCITIES = [
    (0, 0, 0),
    (1, 0, 0),
    (-1, 0, 0),
    (0, 1, 0),
    (0, -1, 0),
    (0, 0, 1),
    (0, 0, -1),
    (1, 1, 0),
    (-1, -1, 0),
    (1, -1, 0),
    (-1, 1, 0),
    (1, 0, 1),
    (-1, 0, -1),
    (1, 0, -1),
    (-1, 0, 1),
    (0, 1, 1),
    (0, -1, -1),
    (0, 1, -1),
    (0, -1, 1),
]
OPPOSITE = [0, 2, 1, 4, 3, 6, 5, 8, 7, 10, 9, 12, 11, 14, 13, 16, 15, 18, 17]
Q = 19
UP_Y = [i for i in range(Q) if VELOCITIES[i][1] == 1]
DOWN_Y = [i for i in range(Q) if VELOCITIES[i][1] == -1]
SOLID = 3.0e38
Z_ORDER = sorted(range(Q), key=lambda i: {1: 0, -1: 1, 0: 2}[VELOCITIES[i][0]])
SLOT = [Z_ORDER.index(i) for i in range(Q)]
PER_SLOT = 14
NEAR = 34
FAR = 9
FLAT_ROWS = 8 * 8 * NEAR
F32 = jnp.float32
UNROLL = 2
VMEM = pl.BlockSpec(memory_space=pltpu.VMEM)
SMEM = pl.BlockSpec(memory_space=pltpu.SMEM)
HBM = pl.BlockSpec(memory_space=pltpu.HBM)


def shape(*dims):
    return jax.ShapeDtypeStruct(dims, F32)


def lanes():
    return lax.broadcasted_iota(jnp.int32, (8, 128), 1)


def sublanes():
    return lax.broadcasted_iota(jnp.int32, (8, 128), 0)


def roll(value, sublane_shift, lane_shift):
    if sublane_shift % 8:
        value = pltpu.roll(value, sublane_shift % 8, 0)
    if lane_shift % 128:
        value = pltpu.roll(value, lane_shift % 128, 1)
    return value


def relax(g):
    sums = [g[k] + g[k + 1] for k in range(1, Q, 2)]
    diffs = [g[k] - g[k + 1] for k in range(1, Q, 2)]
    axis_sum = sums[0] + sums[1] + sums[2]
    edge_sum = (sums[3] + sums[4]) + (sums[5] + sums[6]) + (sums[7] + sums[8])
    density = 12.0 * g[0] + 2.0 * axis_sum + edge_sum
    moment_z = 2.0 * diffs[0] + ((diffs[3] + diffs[4]) + (diffs[5] + diffs[6]))
    moment_y = 2.0 * diffs[1] + ((diffs[3] - diffs[4]) + (diffs[7] + diffs[8]))
    moment_x = 2.0 * diffs[2] + ((diffs[5] - diffs[6]) + (diffs[7] - diffs[8]))
    inverse = 1.0 / density
    speed = [moment_z * inverse, moment_y * inverse, moment_x * inverse]
    square = speed[0] * speed[0] + speed[1] * speed[1] + speed[2] * speed[2]
    scaled = density * (1.5 / 36.0)
    base = scaled * (1.0 - 1.5 * square)
    linear = [(4.5 / 36.0) * m for m in (moment_z, moment_y, moment_x)]
    speed = [1.5 * s for s in speed]
    out = [base - 0.5 * g[0]]
    for pair in range(9):
        velocity = VELOCITIES[1 + 2 * pair]
        along = None
        twice = None
        for axis in range(3):
            if velocity[axis] == 0:
                continue
            if along is None:
                along, twice = linear[axis], speed[axis]
            elif velocity[axis] > 0:
                along, twice = along + linear[axis], twice + speed[axis]
            else:
                along, twice = along - linear[axis], twice - speed[axis]
        even = base + along * twice - 0.25 * sums[pair]
        odd = along - 0.25 * diffs[pair]
        out += [even + odd, even - odd]
    return out


def relax_wet(g, wet):
    return [jnp.where(wet, value, SOLID) for value in relax(g)]


def stream_row(tile, at):
    own = [tile(i, at) for i in range(Q)]
    out = [own[0]]
    for i in range(1, Q):
        step_z, step_y, step_x = VELOCITIES[i]
        source = own[i] if step_y == 0 else tile(i, at - step_y)
        source = roll(source, step_z, step_x)
        out.append(jnp.where(source == SOLID, own[OPPOSITE[i]], source))
    return out


def relax_row(tile, at):
    wet = tile(0, at) != SOLID
    return relax_wet(stream_row(tile, at), wet)


def stream_patch(values):
    out = [values[0]]
    for i in range(1, Q):
        step_z, step_y, step_x = VELOCITIES[i]
        source = roll(values[i], step_z, 8 * step_y + step_x)
        out.append(jnp.where(source == SOLID, values[OPPOSITE[i]], source))
    return out


def over_rows(first, last, body):
    def step(row, carry):
        body(row)
        return carry

    lax.fori_loop(first, last, step, 0, unroll=UNROLL)


def gather_columns(values, rows):
    lane_row = lanes() // 8
    tile = jnp.full((8, 128), SOLID, F32)
    for row, value in zip(rows, values):
        tile = jnp.where(lane_row == row, roll(value, 0, 8 * row + 4), tile)
    return tile


def split_slabs(relative, fluid, new_owner, low, high, moved, kinds, owner, sems):
    copies = [
        pltpu.make_async_copy(fluid, kinds, sems.at[0]),
        pltpu.make_async_copy(relative.at[:, 2:4], high.at[0:Q], sems.at[1]),
        pltpu.make_async_copy(relative.at[:, 0:2], low.at[0:Q], sems.at[2]),
        pltpu.make_async_copy(new_owner, owner, sems.at[3]),
    ]
    for copy in copies:
        copy.start()
    copies[3].wait()
    place = lax.axis_index("gz")
    moved[0] = jnp.full((8, 128), jnp.where((owner[0, 0] == place - 1) & (place > 0), 1.0, 0.0), F32)
    inside = place < lax.axis_size("gz") - 1
    moved[1] = jnp.full((8, 128), jnp.where((owner[0, 1] == place + 1) & inside, 1.0, 0.0), F32)
    copies[0].wait()
    low[Q] = kinds[0:2].astype(F32)
    high[Q] = kinds[2:4].astype(F32)
    copies[1].wait()
    copies[2].wait()


def first_relax(low, high, below, above, moved, own, y_low, y_high, turn):
    place = lax.axis_index("gz")
    at_low = place == 0
    at_high = place == lax.axis_size("gz") - 1
    swap_low = moved[0] > 0.5
    swap_high = moved[1] > 0.5
    for k in range(2):
        turn[Q, 8 * k : 8 * k + 8] = jnp.where(at_low, 0.0, below[Q, k])
        turn[Q, 8 * (k + 2) : 8 * (k + 3)] = low[Q, k]
        turn[Q, 8 * (k + 4) : 8 * (k + 5)] = high[Q, k]
        turn[Q, 8 * (k + 6) : 8 * (k + 7)] = jnp.where(at_high, 0.0, above[Q, k])
    for i in range(Q):
        for k in range(2):
            mine, other = low[i, k], below[i, k]
            turn[i, 8 * k : 8 * k + 8] = jnp.where(swap_low, mine, other)
            turn[i, 8 * (k + 2) : 8 * (k + 3)] = jnp.where(swap_low, other, mine)
            mine, other = high[i, k], above[i, k]
            turn[i, 8 * (k + 4) : 8 * (k + 5)] = jnp.where(swap_high, other, mine)
            turn[i, 8 * (k + 6) : 8 * (k + 7)] = jnp.where(swap_high, mine, other)
    for row in range(8):
        wet = turn[Q, pl.ds(row, 8, stride=8)] > 0.5
        values = relax_wet([turn[i, pl.ds(row, 8, stride=8)] for i in range(Q)], wet)
        for i in range(Q):
            own[i, row] = values[i]
            if row < 3:
                y_low[3 * i + row] = values[i]
            if row > 4:
                y_high[3 * i + row - 5] = values[i]
        if row == 3:
            for k, i in enumerate(DOWN_Y):
                y_low[3 * Q + k] = values[i]
        if row == 4:
            for k, i in enumerate(UP_Y):
                y_high[3 * Q + k] = values[i]


def join_rows(own, below, above, main, edge, x_low, x_high):
    place = lax.axis_index("gy")
    at_low = place == 0
    at_high = place == lax.axis_size("gy") - 1
    edges = []
    for i in range(Q):
        rows = []
        if i in UP_Y:
            rows.append(jnp.where(at_low, SOLID, below[3 * Q + UP_Y.index(i)]))
        else:
            rows.append(jnp.full((8, 128), SOLID, F32))
        for k in range(3):
            rows.append(jnp.where(at_low, SOLID, below[3 * i + k]))
        for k in range(8):
            rows.append(own[i, k])
        for k in range(3):
            rows.append(jnp.where(at_high, SOLID, above[3 * i + k]))
        if i in DOWN_Y:
            rows.append(jnp.where(at_high, SOLID, above[3 * Q + DOWN_Y.index(i)]))
        else:
            rows.append(jnp.full((8, 128), SOLID, F32))
        for k in range(16):
            main[i, k] = rows[k]
        edges.append(gather_columns(rows, range(16)))
        edge[i] = edges[i]
    low_side = lanes() % 8 < 4
    for i in range(10):
        if i + 10 < Q:
            x_low[i] = jnp.where(low_side, roll(edges[i + 10], 0, -4), edges[i])
            x_high[i] = jnp.where(low_side, edges[i], roll(edges[i + 10], 0, 4))
        else:
            x_low[i] = edges[i]
            x_high[i] = edges[i]


def two_steps(main, out, edge, middle):
    def first(row):
        values = relax_row(lambda i, at: main[i, at], row)
        for i in range(Q):
            middle[i, row - 1] = values[i]

    def second(row):
        values = relax_row(lambda i, at: middle[i, at], row - 1)
        for i in range(Q):
            out[i, row - 2] = values[i]

    over_rows(1, 15, first)
    over_rows(2, 14, second)
    for i in range(Q):
        edge[i] = gather_columns([out[i, k] for k in range(12)], range(2, 14))


def patch_two_steps(inner, inner_edge, edge, left, right, flat, below, above):
    place = lax.axis_index("gx")
    at_low = place == 0
    at_high = place == lax.axis_size("gx") - 1
    column = lanes() % 8
    low_side = column < 4
    sides = []
    for side in range(2):
        values = []
        for i in range(Q):
            message = (left, right)[side][i % 10]
            if i >= 10:
                message = roll(message, 0, (-4, 4)[side])
            message = jnp.where((at_low, at_high)[side], SOLID, message)
            if side == 0:
                values.append(jnp.where(low_side, message, edge[i]))
            else:
                values.append(jnp.where(low_side, edge[i], message))
        for step in range(2):
            wet = values[0] != SOLID
            values = relax_wet(stream_patch(values), wet)
        sides.append(values)
    lane = lanes()
    seam = (lane < 2) | (lane >= 126)
    for i in range(Q):
        own_columns = jnp.where(low_side, sides[1][i], sides[0][i])
        first = PER_SLOT * SLOT[i]
        for row in range(12):
            value = jnp.where(seam, roll(own_columns, 0, -(8 * (row + 2) + 4)), inner[i, row])
            flat[8 * (first + row) : 8 * (first + row) + 8] = value
        fresh = inner_edge[i]
        for side in range(2):
            stale = (column < 6) if side == 0 else (column >= 2)
            at = 8 * (first + 12 + side)
            flat[at : at + 8] = jnp.where(stale, sides[side][i], fresh)
    flat[8 * PER_SLOT * Q :] = jnp.full((FLAT_ROWS - 8 * PER_SLOT * Q, 128), SOLID, F32)
    for group in range(NEAR):
        above[group] = flat[pl.ds(64 * group + 5, 8, stride=8)]
        below[group] = flat[pl.ds(64 * group + 2, 8, stride=8)]
    for group in range(FAR):
        above[NEAR + group] = flat[pl.ds(64 * group + 4, 8, stride=8)]
        below[NEAR + group] = flat[pl.ds(8 * 5 * PER_SLOT + 64 * group + 3, 8, stride=8)]


def last_two_steps(
    flat_in, below, above, block_fluid, out, block_density, flat, middle, turn, final, wet_count, sems
):
    count_copy = pltpu.make_async_copy(block_fluid, wet_count, sems.at[2])
    count_copy.start()
    place = lax.axis_index("gz")
    at_low = place == 0
    at_high = place == lax.axis_size("gz") - 1
    lane = lanes()
    low_side = lane % 8 < 4
    for group in range(NEAR):
        flat[pl.ds(64 * group + 1, 8, stride=8)] = jnp.where(at_low, SOLID, below[group])
        flat[pl.ds(64 * group + 6, 8, stride=8)] = jnp.where(at_high, SOLID, above[group])
    for group in range(FAR):
        flat[pl.ds(64 * group, 8, stride=8)] = jnp.where(at_low, SOLID, below[NEAR + group])
        flat[pl.ds(8 * 5 * PER_SLOT + 64 * group + 7, 8, stride=8)] = jnp.where(
            at_high, SOLID, above[NEAR + group]
        )

    def joined(i, at):
        return flat[pl.ds(pl.multiple_of(8 * (PER_SLOT * SLOT[i] + at), 8), 8)]

    def third(row):
        values = relax_row(joined, row - 2)
        for i in range(Q):
            middle[i, row - 3] = values[i]

    over_rows(3, 13, third)
    patches = []
    for side in range(2):
        values = [joined(i, 12 + side) for i in range(Q)]
        wet = values[0] != SOLID
        values = relax_wet(stream_patch(values), wet)
        patches.append(stream_patch(values))
    own_columns = [jnp.where(low_side, patches[1][i], patches[0][i]) for i in range(Q)]
    seam = (lane < 2) | (lane >= 126)
    for row in range(8):
        wet = middle[0, row + 1] != SOLID
        values = stream_row(lambda i, at: middle[i, at], row + 1)
        for i in range(Q):
            value = jnp.where(seam, roll(own_columns[i], 0, -(8 * (row + 4) + 4)), values[i])
            turn[i, 8 * row : 8 * row + 8] = jnp.where(wet, value, 0.0)
    copies = []
    masses = []
    for slot in range(2):
        mass = None
        for k in range(2):
            layer = 2 * slot + k
            values = [turn[i, pl.ds(layer + 2, 8, stride=8)] for i in range(Q)]
            for i in range(Q):
                final[i, layer] = values[i]
            axis_sum = functools.reduce(jnp.add, values[1:7])
            edge_sum = functools.reduce(jnp.add, values[7:])
            density = values[0] * (1.0 / 3.0) + axis_sum * (1.0 / 18.0) + edge_sum * (1.0 / 36.0)
            mass = density if mass is None else mass + density
        masses.append(mass)
        layers = slice(2 * slot, 2 * slot + 2)
        copies.append(pltpu.make_async_copy(final.at[:, layers], out.at[:, layers], sems.at[slot]))
        copies[slot].start()
    count_copy.wait()
    for slot in range(2):
        count = jnp.maximum(wet_count[0, slot], 1).astype(F32)
        block_density[0, slot] = jnp.sum(masses[slot]) / count
    for copy in copies:
        copy.wait()


def exchange(to_low, to_high, axis, ring=False):
    count = lax.axis_size(axis)
    up = [(i, (i + 1) % count) for i in range(count if ring else count - 1)]
    down = [(target, source) for source, target in up]
    return lax.ppermute(to_high, axis, up), lax.ppermute(to_low, axis, down)


def call(kernel, outs, in_specs, out_specs=None, scratch=(), aliases=None, vmem=32):
    if out_specs is None:
        out_specs = [VMEM] * len(outs)
    return pl.pallas_call(
        kernel,
        out_shape=outs,
        in_specs=in_specs,
        out_specs=out_specs,
        scratch_shapes=list(scratch),
        input_output_aliases=aliases or {},
        compiler_params=pltpu.CompilerParams(vmem_limit_bytes=vmem * 1024 * 1024),
    )


def in_hbm(array):
    return pltpu.with_memory_space_constraint(array, pltpu.HBM)


def on_device(relative, fluid, block_fluid, new_owner):
    low, high, moved = call(
        split_slabs,
        [shape(Q + 1, 2, 8, 128), shape(Q + 1, 2, 8, 128), shape(2, 8, 128)],
        [HBM] * 3,
        scratch=[
            pltpu.VMEM((4, 8, 128), jnp.int32),
            pltpu.SMEM((1, 2), jnp.int32),
            pltpu.SemaphoreType.DMA((4,)),
        ],
    )(in_hbm(relative), in_hbm(fluid), in_hbm(new_owner.transpose(1, 2, 0).reshape(1, 2)))
    below, above = exchange(low, high, "gz", ring=True)
    own, y_low, y_high = call(
        first_relax,
        [shape(Q, 8, 8, 128), shape(3 * Q + 5, 8, 128), shape(3 * Q + 5, 8, 128)],
        [VMEM] * 5,
        scratch=[pltpu.VMEM((Q + 1, 64, 128), F32)],
    )(low, high, below, above, moved)
    below, above = exchange(y_low, y_high, "gy")
    main, edge, x_low, x_high = call(
        join_rows,
        [shape(Q, 16, 8, 128), shape(Q, 8, 128), shape(10, 8, 128), shape(10, 8, 128)],
        [VMEM] * 3,
    )(own, below, above)
    left, right = exchange(x_low, x_high, "gx")
    inner, inner_edge = call(
        two_steps,
        [shape(Q, 12, 8, 128), shape(Q, 8, 128)],
        [VMEM],
        scratch=[pltpu.VMEM((Q, 14, 8, 128), F32)],
    )(main)
    flat, z_low, z_high = call(
        patch_two_steps,
        [shape(FLAT_ROWS, 128), shape(NEAR + FAR, 8, 128), shape(NEAR + FAR, 8, 128)],
        [VMEM] * 5,
    )(inner, inner_edge, edge, left, right)
    below, above = exchange(z_low, z_high, "gz", ring=True)
    out, block_density, _ = call(
        last_two_steps,
        [shape(Q, 4, 8, 128), shape(1, 2), shape(FLAT_ROWS, 128)],
        [VMEM] * 3 + [HBM],
        [HBM, SMEM, VMEM],
        scratch=[
            pltpu.VMEM((Q, 10, 8, 128), F32),
            pltpu.VMEM((Q, 64, 128), F32),
            pltpu.VMEM((Q, 4, 8, 128), F32),
            pltpu.SMEM((1, 2), jnp.int32),
            pltpu.SemaphoreType.DMA((3,)),
        ],
        aliases={0: 2},
    )(flat, below, above, in_hbm(block_fluid.transpose(1, 2, 0).reshape(1, 2)))
    return out, block_density.reshape(1, 1, 2).transpose(2, 0, 1)


def solution(mesh):
    return jax.shard_map(
        on_device,
        mesh=mesh,
        in_specs=(
            P(None, "gz", "gy", "gx"),
            P("gz", "gy", "gx"),
            P("gz", "gy", "gx"),
            P("gz", "gy", "gx"),
        ),
        out_specs=(P(None, "gz", "gy", "gx"), P("gz", "gy", "gx")),
        check_vma=False,
    )
```

time: 59.1 us -> 57.1 us (0.966)
  the two profiles are of different devices: /device:TPU:217 before, /device:TPU:26 now
where the time goes in v2:
time: 57.1 us; the launch traced here: 56.9 us
  starting transfers between devices  31.2 us (55%)
  waiting for transfers between devices  17.9 us (31%)
  Pallas kernels  7.07 us (12%)
  between operations  0.7 us (1%)
    ppermute x8, starting transfers between devices, exchange(): return (lax.ppermute(to_high, axis, up), lax.ppermute(to_low, axis, down))  31.2 us
    ppermute x8, waiting for transfers between devices, exchange(): return (lax.ppermute(to_high, axis, up), lax.ppermute(to_low, axis, down))  17.9 us
    pallas_call x1, Pallas kernels, on_device(): call(last_two_steps, [shape(Q, 4, 8, 128), shape(1, 2), shape(FLAT_ROWS,...  2.49 us
    pallas_call x1, Pallas kernels, on_device(): call(two_steps, [shape(Q, 12, 8, 128), shape(Q, 8, 128)], [VMEM], scratch...  2.04 us
  transfers between devices with their start and end apart: 8, of which 6 were waited for; matrix products, arithmetic and copies ran while one was open for 0% of the time, Pallas kernels for 4%

profile of v2, /device:TPU:26, one launch (start us, length us, event | category | flops | bytes accessed | tf_op | source)
XLA Modules:
  0.0 56.9 jit_solution(13663724646643441881)
XLA Ops:
  0.6 1.0 %shard_map.59 = (f32[20,2,8,128]{3,2,1,0:T(8,128)S(1)}, f32[20,2,8,128]{3,2,1,0:T(8,128)S(1)}, f32[2,8,128]{2,1,0:T(8,128)S(1)}) custom-call(f32[19,4,8,128]{3,2,1,0:T(8,128)} %relative.1, s32[4,8,128]{2,1,0:T(8,128)} %fluid.1, s32[1,2]{1,0:T(1,128)} %bitcast.3), custom_call_target="tpu_custom_call" | custom-call | tf_op jit(solution)/shard_map/pallas_call | solution.py:397
  1.7 15.8 %collective-permute-start.1 = (f32[20,2,8,128]{3,2,1,0:T(8,128)S(1)}, f32[20,2,8,128]{3,2,1,0:T(8,128)S(1)}, u32[]{:S(2)}, u32[]{:S(2)}) collective-permute-start(f32[20,2,8,128]{3,2,1,0:T(8,128)S(1)} %get-tuple-element.19.low), channel_id=1, source_target_pairs={{1,0},{2,1},{3,2},{4,3},{5,4},{6,5},{7,6},{8,7},{9,8},{10,9},{11,1... | collective-permute-start | bytes 491528 | tf_op jit(solution)/shard_map/ppermute | solution.py:375
  17.4 0.0 collective-permute-start
  17.4 2.8 %collective-permute-done.1.above = f32[20,2,8,128]{3,2,1,0:T(8,128)S(1)} collective-permute-done((f32[20,2,8,128]{3,2,1,0:T(8,128)S(1)}, f32[20,2,8,128]{3,2,1,0:T(8,128)S(1)}, u32[]{:S(2)}, u32[]{:S(2)}) %collective-permute-start.1) | collective-permute-done | bytes 163872 | tf_op jit(solution)/shard_map/ppermute | solution.py:375
  20.3 3.1 %collective-permute-done.below = f32[20,2,8,128]{3,2,1,0:T(8,128)S(1)} collective-permute-done((f32[20,2,8,128]{3,2,1,0:T(8,128)S(1)}, f32[20,2,8,128]{3,2,1,0:T(8,128)S(1)}, u32[]{:S(2)}, u32[]{:S(2)}) %collective-permute-start) | collective-permute-done | bytes 163872 | tf_op jit(solution)/shard_map/ppermute | solution.py:375
  23.4 0.3 shard_map.60
  23.8 3.4 %collective-permute-start.2 = (f32[62,8,128]{2,1,0:T(8,128)S(1)}, f32[62,8,128]{2,1,0:T(8,128)S(1)}, u32[]{:S(2)}, u32[]{:S(2)}) collective-permute-start(f32[62,8,128]{2,1,0:T(8,128)S(1)} %get-tuple-element.23), channel_id=1, source_target_pairs={{0,32},{32,64},{64,96},{1,33},{33,65},{65,97},{2,34},{34,66},{66,9... | collective-permute-start | bytes 761864 | tf_op jit(solution)/shard_map/ppermute | solution.py:375
  27.2 2.5 %collective-permute-start.3 = (f32[62,8,128]{2,1,0:T(8,128)S(1)}, f32[62,8,128]{2,1,0:T(8,128)S(1)}, u32[]{:S(2)}, u32[]{:S(2)}) collective-permute-start(f32[62,8,128]{2,1,0:T(8,128)S(1)} %get-tuple-element.24), channel_id=1, source_target_pairs={{32,0},{64,32},{96,64},{33,1},{65,33},{97,65},{34,2},{66,34},{98,6... | collective-permute-start | bytes 761864 | tf_op jit(solution)/shard_map/ppermute | solution.py:375
  29.6 2.3 %collective-permute-done.2.below = f32[62,8,128]{2,1,0:T(8,128)S(1)} collective-permute-done((f32[62,8,128]{2,1,0:T(8,128)S(1)}, f32[62,8,128]{2,1,0:T(8,128)S(1)}, u32[]{:S(2)}, u32[]{:S(2)}) %collective-permute-start.2) | collective-permute-done | bytes 253984 | tf_op jit(solution)/shard_map/ppermute | solution.py:375
  31.9 3.4 %collective-permute-done.3.above = f32[62,8,128]{2,1,0:T(8,128)S(1)} collective-permute-done((f32[62,8,128]{2,1,0:T(8,128)S(1)}, f32[62,8,128]{2,1,0:T(8,128)S(1)}, u32[]{:S(2)}, u32[]{:S(2)}) %collective-permute-start.3) | collective-permute-done | bytes 253984 | tf_op jit(solution)/shard_map/ppermute | solution.py:375
  35.3 0.4 shard_map.61
  35.8 4.7 %collective-permute-start.4 = (f32[10,8,128]{2,1,0:T(8,128)S(1)}, f32[10,8,128]{2,1,0:T(8,128)S(1)}, u32[]{:S(2)}, u32[]{:S(2)}) collective-permute-start(f32[10,8,128]{2,1,0:T(8,128)S(1)} %get-tuple-element.29), channel_id=1, source_target_pairs={{0,128},{128,256},{256,384},{384,512},{512,640},{640,768},{768,896... | collective-permute-start | bytes 122888 | tf_op jit(solution)/shard_map/ppermute | solution.py:375
  40.5 1.9 %collective-permute-start.5 = (f32[10,8,128]{2,1,0:T(8,128)S(1)}, f32[10,8,128]{2,1,0:T(8,128)S(1)}, u32[]{:S(2)}, u32[]{:S(2)}) collective-permute-start(f32[10,8,128]{2,1,0:T(8,128)S(1)} %get-tuple-element.30), channel_id=1, source_target_pairs={{128,0},{256,128},{384,256},{512,384},{640,512},{768,640},{896,768... | collective-permute-start | bytes 122888 | tf_op jit(solution)/shard_map/ppermute | solution.py:375
  42.4 2.0 %shard_map.62 = (f32[19,12,8,128]{3,2,1,0:T(8,128)S(1)}, f32[19,8,128]{2,1,0:T(8,128)S(1)}) custom-call(f32[19,16,8,128]{3,2,1,0:T(8,128)S(1)} %get-tuple-element.25.main), custom_call_target="tpu_custom_call" | custom-call | tf_op jit(solution)/shard_map/pallas_call | solution.py:421
  44.4 0.0 collective-permute-done.4.left
  44.5 3.1 %collective-permute-done.5.right = f32[10,8,128]{2,1,0:T(8,128)S(1)} collective-permute-done((f32[10,8,128]{2,1,0:T(8,128)S(1)}, f32[10,8,128]{2,1,0:T(8,128)S(1)}, u32[]{:S(2)}, u32[]{:S(2)}) %collective-permute-start.5) | collective-permute-done | bytes 40992 | tf_op jit(solution)/shard_map/ppermute | solution.py:375
  47.6 0.7 %shard_map.63 = (f32[2176,128]{1,0:T(8,128)S(1)}, f32[43,8,128]{2,1,0:T(8,128)S(1)}, f32[43,8,128]{2,1,0:T(8,128)S(1)}) custom-call(f32[19,12,8,128]{3,2,1,0:T(8,128)S(1)} %get-tuple-element.26.inner, f32[19,8,128]{2,1,0:T(8,128)S(1)} %get-tuple-element.27.inner_edge, f32[19,8,128]{2,1,0:T(8,128)S(1)} %get-tuple-element.28.edge, ...), custom_call_target="tpu_custom_call" | custom-call | tf_op jit(solution)/shard_map/pallas_call | solution.py:427
  48.3 0.0 collective-permute-start.6
  48.3 2.9 %collective-permute-start.7 = (f32[43,8,128]{2,1,0:T(8,128)S(1)}, f32[43,8,128]{2,1,0:T(8,128)S(1)}, u32[]{:S(2)}, u32[]{:S(2)}) collective-permute-start(f32[43,8,128]{2,1,0:T(8,128)S(1)} %get-tuple-element.33), channel_id=1, source_target_pairs={{1,0},{2,1},{3,2},{4,3},{5,4},{6,5},{7,6},{8,7},{9,8},{10,9},{11,1... | collective-permute-start | bytes 528392 | tf_op jit(solution)/shard_map/ppermute | solution.py:375
  51.3 3.1 %collective-permute-done.6.below = f32[43,8,128]{2,1,0:T(8,128)S(1)} collective-permute-done((f32[43,8,128]{2,1,0:T(8,128)S(1)}, f32[43,8,128]{2,1,0:T(8,128)S(1)}, u32[]{:S(2)}, u32[]{:S(2)}) %collective-permute-start.6) | collective-permute-done | bytes 176160 | tf_op jit(solution)/shard_map/ppermute | solution.py:375
  54.4 0.0 collective-permute-done.7.above
  54.4 2.5 %shard_map.64 = (f32[19,4,8,128]{3,2,1,0:T(8,128)}, f32[1,2]{1,0:T(1,128)}, f32[2176,128]{1,0:T(8,128)S(1)}) custom-call(f32[2176,128]{1,0:T(8,128)S(1)} %get-tuple-element.31.flat_in, f32[43,8,128]{2,1,0:T(8,128)S(1)} %collective-permute-done.6.below, f32[43,8,128]{2,1,0:T(8,128)S(1)} %collective-permute-done.7.above, ...), custom_call_target="tpu_custom_call", output_to_operand_aliasing={{2}: (0, {})} | custom-call | tf_op jit(solution)/shard_map/pallas_call | solution.py:433
Async XLA Ops:
  1.7 18.6 %collective-permute-start.1 = (f32[20,2,8,128]{3,2,1,0:T(8,128)S(1)}, f32[20,2,8,128]{3,2,1,0:T(8,128)S(1)}, u32[]{:S(2)}, u32[]{:S(2)}) collective-permute-start(f32[20,2,8,128]{3,2,1,0:T(8,128)S(1)} %get-tuple-element.19.low), channel_id=1, source_target_pairs={{1,0},{2,1},{3,2},{4,3},{5,4},{6,5},{7,6},{8,7},{9,8},{10,9},{11,1... | collective-permute-start | bytes 491528 | tf_op jit(solution)/shard_map/ppermute | solution.py:375
  17.4 6.0 %collective-permute-start = (f32[20,2,8,128]{3,2,1,0:T(8,128)S(1)}, f32[20,2,8,128]{3,2,1,0:T(8,128)S(1)}, u32[]{:S(2)}, u32[]{:S(2)}) collective-permute-start(f32[20,2,8,128]{3,2,1,0:T(8,128)S(1)} %get-tuple-element.20.high), channel_id=1, source_target_pairs={{0,1},{1,2},{2,3},{3,4},{4,5},{5,6},{6,7},{7,8},{8,9},{9,10},{10,1... | collective-permute-start | bytes 491528 | tf_op jit(solution)/shard_map/ppermute | solution.py:375
  23.8 8.2 %collective-permute-start.2 = (f32[62,8,128]{2,1,0:T(8,128)S(1)}, f32[62,8,128]{2,1,0:T(8,128)S(1)}, u32[]{:S(2)}, u32[]{:S(2)}) collective-permute-start(f32[62,8,128]{2,1,0:T(8,128)S(1)} %get-tuple-element.23), channel_id=1, source_target_pairs={{0,32},{32,64},{64,96},{1,33},{33,65},{65,97},{2,34},{34,66},{66,9... | collective-permute-start | bytes 761864 | tf_op jit(solution)/shard_map/ppermute | solution.py:375
  27.2 8.2 %collective-permute-start.3 = (f32[62,8,128]{2,1,0:T(8,128)S(1)}, f32[62,8,128]{2,1,0:T(8,128)S(1)}, u32[]{:S(2)}, u32[]{:S(2)}) collective-permute-start(f32[62,8,128]{2,1,0:T(8,128)S(1)} %get-tuple-element.24), channel_id=1, source_target_pairs={{32,0},{64,32},{96,64},{33,1},{65,33},{97,65},{34,2},{66,34},{98,6... | collective-permute-start | bytes 761864 | tf_op jit(solution)/shard_map/ppermute | solution.py:375
  35.8 8.7 %collective-permute-start.4 = (f32[10,8,128]{2,1,0:T(8,128)S(1)}, f32[10,8,128]{2,1,0:T(8,128)S(1)}, u32[]{:S(2)}, u32[]{:S(2)}) collective-permute-start(f32[10,8,128]{2,1,0:T(8,128)S(1)} %get-tuple-element.29), channel_id=1, source_target_pairs={{0,128},{128,256},{256,384},{384,512},{512,640},{640,768},{768,896... | collective-permute-start | bytes 122888 | tf_op jit(solution)/shard_map/ppermute | solution.py:375
  40.5 7.1 %collective-permute-start.5 = (f32[10,8,128]{2,1,0:T(8,128)S(1)}, f32[10,8,128]{2,1,0:T(8,128)S(1)}, u32[]{:S(2)}, u32[]{:S(2)}) collective-permute-start(f32[10,8,128]{2,1,0:T(8,128)S(1)} %get-tuple-element.30), channel_id=1, source_target_pairs={{128,0},{256,128},{384,256},{512,384},{640,512},{768,640},{896,768... | collective-permute-start | bytes 122888 | tf_op jit(solution)/shard_map/ppermute | solution.py:375
  48.3 6.1 %collective-permute-start.6 = (f32[43,8,128]{2,1,0:T(8,128)S(1)}, f32[43,8,128]{2,1,0:T(8,128)S(1)}, u32[]{:S(2)}, u32[]{:S(2)}) collective-permute-start(f32[43,8,128]{2,1,0:T(8,128)S(1)} %get-tuple-element.32), channel_id=1, source_target_pairs={{0,1},{1,2},{2,3},{3,4},{4,5},{5,6},{6,7},{7,8},{8,9},{9,10},{10,1... | collective-permute-start | bytes 528392 | tf_op jit(solution)/shard_map/ppermute | solution.py:375
  48.3 6.1 %collective-permute-start.7 = (f32[43,8,128]{2,1,0:T(8,128)S(1)}, f32[43,8,128]{2,1,0:T(8,128)S(1)}, u32[]{:S(2)}, u32[]{:S(2)}) collective-permute-start(f32[43,8,128]{2,1,0:T(8,128)S(1)} %get-tuple-element.33), channel_id=1, source_target_pairs={{1,0},{2,1},{3,2},{4,3},{5,4},{6,5},{7,6},{8,7},{9,8},{10,9},{11,1... | collective-permute-start | bytes 528392 | tf_op jit(solution)/shard_map/ppermute | solution.py:375

commit v3 on v2

--- a/solution.py
+++ b/solution.py
@@ -169,7 +169,7 @@
     copies[2].wait()
 
 
-def first_relax(low, high, below, above, moved, own, y_low, y_high, turn):
+def first_relax(low, high, below, above, moved, own, ahead, back, turn):
     place = lax.axis_index("gz")
     at_low = place == 0
     at_high = place == lax.axis_size("gz") - 1
@@ -193,51 +193,53 @@
         values = relax_wet([turn[i, pl.ds(row, 8, stride=8)] for i in range(Q)], wet)
         for i in range(Q):
             own[i, row] = values[i]
-            if row < 3:
-                y_low[3 * i + row] = values[i]
-            if row > 4:
-                y_high[3 * i + row - 5] = values[i]
-        if row == 3:
-            for k, i in enumerate(DOWN_Y):
-                y_low[3 * Q + k] = values[i]
-        if row == 4:
-            for k, i in enumerate(UP_Y):
-                y_high[3 * Q + k] = values[i]
-
-
-def join_rows(own, below, above, main, edge, x_low, x_high):
+    up = place % 2 == 0
+    for message, high_rows in ((ahead, up), (back, jnp.logical_not(up))):
+        first = jnp.where(high_rows, 5, 0)
+        far = jnp.where(high_rows, 4, 3)
+        for i in range(Q):
+            for k in range(3):
+                message[3 * i + k] = own[i, first + k]
+        for k in range(5):
+            message[3 * Q + k] = own[jnp.where(high_rows, UP_Y[k], DOWN_Y[k]), far]
+
+
+def join_rows(own, ahead, back, main, edge, x_ahead, x_back):
     place = lax.axis_index("gy")
-    at_low = place == 0
-    at_high = place == lax.axis_size("gy") - 1
+    up = lax.axis_index("gz") % 2 == 0
+    outside_low = place == 0
+    outside_high = place == lax.axis_size("gy") - 1
+    for i in range(Q):
+        main[i, 0] = jnp.full((8, 128), SOLID, F32)
+        main[i, 15] = jnp.full((8, 128), SOLID, F32)
+    for message, low_rows in ((ahead, up), (back, jnp.logical_not(up))):
+        outside = jnp.where(low_rows, outside_low, outside_high)
+        first = jnp.where(low_rows, 1, 12)
+        far = jnp.where(low_rows, 0, 15)
+        for i in range(Q):
+            for k in range(3):
+                main[i, first + k] = jnp.where(outside, SOLID, message[3 * i + k])
+        for k in range(5):
+            value = jnp.where(outside, SOLID, message[3 * Q + k])
+            main[jnp.where(low_rows, UP_Y[k], DOWN_Y[k]), far] = value
     edges = []
     for i in range(Q):
-        rows = []
-        if i in UP_Y:
-            rows.append(jnp.where(at_low, SOLID, below[3 * Q + UP_Y.index(i)]))
-        else:
-            rows.append(jnp.full((8, 128), SOLID, F32))
-        for k in range(3):
-            rows.append(jnp.where(at_low, SOLID, below[3 * i + k]))
+        rows = [own[i, k] for k in range(8)]
         for k in range(8):
-            rows.append(own[i, k])
-        for k in range(3):
-            rows.append(jnp.where(at_high, SOLID, above[3 * i + k]))
-        if i in DOWN_Y:
-            rows.append(jnp.where(at_high, SOLID, above[3 * Q + DOWN_Y.index(i)]))
-        else:
-            rows.append(jnp.full((8, 128), SOLID, F32))
-        for k in range(16):
-            main[i, k] = rows[k]
+            main[i, 4 + k] = rows[k]
+        rows = [main[i, k] for k in range(4)] + rows + [main[i, k] for k in range(12, 16)]
         edges.append(gather_columns(rows, range(16)))
         edge[i] = edges[i]
     low_side = lanes() % 8 < 4
     for i in range(10):
         if i + 10 < Q:
-            x_low[i] = jnp.where(low_side, roll(edges[i + 10], 0, -4), edges[i])
-            x_high[i] = jnp.where(low_side, edges[i], roll(edges[i + 10], 0, 4))
+            to_low = jnp.where(low_side, roll(edges[i + 10], 0, -4), edges[i])
+            to_high = jnp.where(low_side, edges[i], roll(edges[i + 10], 0, 4))
+            x_ahead[i] = jnp.where(up, to_high, to_low)
+            x_back[i] = jnp.where(up, to_low, to_high)
         else:
-            x_low[i] = edges[i]
-            x_high[i] = edges[i]
+            x_ahead[i] = edges[i]
+            x_back[i] = edges[i]
 
 
 def two_steps(main, out, edge, middle):
@@ -257,7 +259,8 @@
         edge[i] = gather_columns([out[i, k] for k in range(12)], range(2, 14))
 
 
-def patch_two_steps(inner, inner_edge, edge, left, right, flat, below, above):
+def patch_two_steps(inner, inner_edge, edge, ahead, back, flat, below, above):
+    up = lax.axis_index("gz") % 2 == 0
     place = lax.axis_index("gx")
     at_low = place == 0
     at_high = place == lax.axis_size("gx") - 1
@@ -267,7 +270,7 @@
     for side in range(2):
         values = []
         for i in range(Q):
-            message = (left, right)[side][i % 10]
+            message = jnp.where(up == (side == 0), ahead[i % 10], back[i % 10])
             if i >= 10:
                 message = roll(message, 0, (-4, 4)[side])
             message = jnp.where((at_low, at_high)[side], SOLID, message)
@@ -368,11 +371,27 @@
         copy.wait()
 
 
-def exchange(to_low, to_high, axis, ring=False):
+def ring_exchange(to_low, to_high, axis):
     count = lax.axis_size(axis)
-    up = [(i, (i + 1) % count) for i in range(count if ring else count - 1)]
+    up = [(i, (i + 1) % count) for i in range(count)]
     down = [(target, source) for source, target in up]
     return lax.ppermute(to_high, axis, up), lax.ppermute(to_low, axis, down)
+
+
+def loop_exchange(ahead, back, axis):
+    count = lax.axis_size(axis)
+    layers = lax.axis_size("gz")
+    pairs = []
+    for i in range(count):
+        for layer in range(layers):
+            if layer % 2 == 0:
+                target = (i + 1, layer) if i < count - 1 else (i, layer + 1)
+            else:
+                target = (i - 1, layer) if i > 0 else (i, layer - 1)
+            pairs.append((i * layers + layer, target[0] * layers + target[1]))
+    inverse = [(target, source) for source, target in pairs]
+    axes = (axis, "gz")
+    return lax.ppermute(ahead, axes, pairs), lax.ppermute(back, axes, inverse)
 
 
 def call(kernel, outs, in_specs, out_specs=None, scratch=(), aliases=None, vmem=32):
@@ -404,20 +423,20 @@
             pltpu.SemaphoreType.DMA((4,)),
         ],
     )(in_hbm(relative), in_hbm(fluid), in_hbm(new_owner.transpose(1, 2, 0).reshape(1, 2)))
-    below, above = exchange(low, high, "gz", ring=True)
-    own, y_low, y_high = call(
+    below, above = ring_exchange(low, high, "gz")
+    own, ahead, back = call(
         first_relax,
         [shape(Q, 8, 8, 128), shape(3 * Q + 5, 8, 128), shape(3 * Q + 5, 8, 128)],
         [VMEM] * 5,
         scratch=[pltpu.VMEM((Q + 1, 64, 128), F32)],
     )(low, high, below, above, moved)
-    below, above = exchange(y_low, y_high, "gy")
-    main, edge, x_low, x_high = call(
+    ahead, back = loop_exchange(ahead, back, "gy")
+    main, edge, x_ahead, x_back = call(
         join_rows,
         [shape(Q, 16, 8, 128), shape(Q, 8, 128), shape(10, 8, 128), shape(10, 8, 128)],
         [VMEM] * 3,
-    )(own, below, above)
-    left, right = exchange(x_low, x_high, "gx")
+    )(own, ahead, back)
+    x_ahead, x_back = loop_exchange(x_ahead, x_back, "gx")
     inner, inner_edge = call(
         two_steps,
         [shape(Q, 12, 8, 128), shape(Q, 8, 128)],
@@ -428,8 +447,8 @@
         patch_two_steps,
         [shape(FLAT_ROWS, 128), shape(NEAR + FAR, 8, 128), shape(NEAR + FAR, 8, 128)],
         [VMEM] * 5,
-    )(inner, inner_edge, edge, left, right)
-    below, above = exchange(z_low, z_high, "gz", ring=True)
+    )(inner, inner_edge, edge, x_ahead, x_back)
+    below, above = ring_exchange(z_low, z_high, "gz")
     out, block_density, _ = call(
         last_two_steps,
         [shape(Q, 4, 8, 128), shape(1, 2), shape(FLAT_ROWS, 128)],

time: 57.1 us -> 49.6 us (0.87)
  starting transfers between devices: 31.2 us -> 23.6 us
    ppermute x8, starting transfers between devices: 31.2 us -> 23.6 us  [the longest x4 18.7 us: ring_exchange(): return (lax.ppermute(to_high, axis, up), lax.ppermute(to_low, axis, down))]
where the time goes in v3:
time: 49.6 us; the launch traced here: 49.4 us
  starting transfers between devices  23.6 us (48%)
  waiting for transfers between devices  18 us (36%)
  Pallas kernels  7.21 us (15%)
  between operations  0.67 us (1%)
    ppermute x4, starting transfers between devices, ring_exchange(): return (lax.ppermute(to_high, axis, up), lax.ppermute(to_low, axis, down))  18.7 us
    ppermute x4, waiting for transfers between devices, ring_exchange(): return (lax.ppermute(to_high, axis, up), lax.ppermute(to_low, axis, down))  9.08 us
    ppermute x4, waiting for transfers between devices, loop_exchange(): return (lax.ppermute(ahead, axes, pairs), lax.ppermute(back, axes, inverse))  8.91 us
    ppermute x4, starting transfers between devices, loop_exchange(): return (lax.ppermute(ahead, axes, pairs), lax.ppermute(back, axes, inverse))  4.83 us
    pallas_call x1, Pallas kernels, on_device(): call(last_two_steps, [shape(Q, 4, 8, 128), shape(1, 2), shape(FLAT_ROWS,...  2.49 us
    pallas_call x1, Pallas kernels, on_device(): call(two_steps, [shape(Q, 12, 8, 128), shape(Q, 8, 128)], [VMEM], scratch...  2.04 us
    pallas_call x1, Pallas kernels, on_device(): call(split_slabs, [shape(Q + 1, 2, 8, 128), shape(Q + 1, 2, 8, 128), shap...  1.04 us
  transfers between devices with their start and end apart: 8, of which 6 were waited for; matrix products, arithmetic and copies ran while one was open for 0% of the time, Pallas kernels for 4%

profile of v3, /device:TPU:26, one launch (start us, length us, event | category | flops | bytes accessed | tf_op | source)
XLA Modules:
  0.0 49.4 jit_solution(4546568146612831879)
XLA Ops:
  0.6 1.0 %shard_map.59 = (f32[20,2,8,128]{3,2,1,0:T(8,128)S(1)}, f32[20,2,8,128]{3,2,1,0:T(8,128)S(1)}, f32[2,8,128]{2,1,0:T(8,128)S(1)}) custom-call(f32[19,4,8,128]{3,2,1,0:T(8,128)} %relative.1, s32[4,8,128]{2,1,0:T(8,128)} %fluid.1, s32[1,2]{1,0:T(1,128)} %bitcast.3), custom_call_target="tpu_custom_call" | custom-call | tf_op jit(solution)/shard_map/pallas_call | solution.py:416
  1.7 15.8 %collective-permute-start.1 = (f32[20,2,8,128]{3,2,1,0:T(8,128)S(1)}, f32[20,2,8,128]{3,2,1,0:T(8,128)S(1)}, u32[]{:S(2)}, u32[]{:S(2)}) collective-permute-start(f32[20,2,8,128]{3,2,1,0:T(8,128)S(1)} %get-tuple-element.19.low), channel_id=1, source_target_pairs={{1,0},{2,1},{3,2},{4,3},{5,4},{6,5},{7,6},{8,7},{9,8},{10,9},{11,1... | collective-permute-start | bytes 491528 | tf_op jit(solution)/shard_map/ppermute | solution.py:378
  17.4 0.0 collective-permute-start
  17.4 2.8 %collective-permute-done.1.above = f32[20,2,8,128]{3,2,1,0:T(8,128)S(1)} collective-permute-done((f32[20,2,8,128]{3,2,1,0:T(8,128)S(1)}, f32[20,2,8,128]{3,2,1,0:T(8,128)S(1)}, u32[]{:S(2)}, u32[]{:S(2)}) %collective-permute-start.1) | collective-permute-done | bytes 163872 | tf_op jit(solution)/shard_map/ppermute | solution.py:378
  20.3 3.1 %collective-permute-done.below = f32[20,2,8,128]{3,2,1,0:T(8,128)S(1)} collective-permute-done((f32[20,2,8,128]{3,2,1,0:T(8,128)S(1)}, f32[20,2,8,128]{3,2,1,0:T(8,128)S(1)}, u32[]{:S(2)}, u32[]{:S(2)}) %collective-permute-start) | collective-permute-done | bytes 163872 | tf_op jit(solution)/shard_map/ppermute | solution.py:378
  23.4 0.4 shard_map.60
  23.8 1.5 %collective-permute-start.2 = (f32[62,8,128]{2,1,0:T(8,128)S(1)}, f32[62,8,128]{2,1,0:T(8,128)S(1)}, u32[]{:S(2)}, u32[]{:S(2)}) collective-permute-start(f32[62,8,128]{2,1,0:T(8,128)S(1)} %get-tuple-element.23), channel_id=1, source_target_pairs={{0,32},{1,0},{2,34},{3,2},{4,36},{5,4},{6,38},{7,6},{8,40},{9,8},{... | collective-permute-start | bytes 761864 | tf_op jit(solution)/shard_map/ppermute | solution.py:394
  25.3 0.5 %collective-permute-start.3 = (f32[62,8,128]{2,1,0:T(8,128)S(1)}, f32[62,8,128]{2,1,0:T(8,128)S(1)}, u32[]{:S(2)}, u32[]{:S(2)}) collective-permute-start(f32[62,8,128]{2,1,0:T(8,128)S(1)} %get-tuple-element.24), channel_id=1, source_target_pairs={{32,0},{0,1},{34,2},{2,3},{36,4},{4,5},{38,6},{6,7},{40,8},{8,9},{... | collective-permute-start | bytes 761864 | tf_op jit(solution)/shard_map/ppermute | solution.py:394
  25.8 5.3 %collective-permute-done.2.ahead = f32[62,8,128]{2,1,0:T(8,128)S(1)} collective-permute-done((f32[62,8,128]{2,1,0:T(8,128)S(1)}, f32[62,8,128]{2,1,0:T(8,128)S(1)}, u32[]{:S(2)}, u32[]{:S(2)}) %collective-permute-start.2) | collective-permute-done | bytes 253984 | tf_op jit(solution)/shard_map/ppermute | solution.py:394
  31.2 0.4 collective-permute-done.3.back
  31.6 0.5 %shard_map.61 = (f32[19,16,8,128]{3,2,1,0:T(8,128)S(1)}, f32[19,8,128]{2,1,0:T(8,128)S(1)}, f32[10,8,128]{2,1,0:T(8,128)S(1)}, f32[10,8,128]{2,1,0:T(8,128)S(1)}) custom-call(f32[19,8,8,128]{3,2,1,0:T(8,128)S(1)} %get-tuple-element.22.own, f32[62,8,128]{2,1,0:T(8,128)S(1)} %collective-permute-done.2.ahead, f32[62,8,128]{2,1,0:T(8,128)S(1)} %collective-permute-done.3.back), custom_call_target="tpu_custom_call" | custom-call | tf_op jit(solution)/shard_map/pallas_call | solution.py:434
  32.1 2.8 %collective-permute-start.4 = (f32[10,8,128]{2,1,0:T(8,128)S(1)}, f32[10,8,128]{2,1,0:T(8,128)S(1)}, u32[]{:S(2)}, u32[]{:S(2)}) collective-permute-start(f32[10,8,128]{2,1,0:T(8,128)S(1)} %get-tuple-element.29), channel_id=1, source_target_pairs={{0,128},{1,0},{2,130},{3,2},{4,132},{5,4},{6,134},{7,6},{8,136},{9... | collective-permute-start | bytes 122888 | tf_op jit(solution)/shard_map/ppermute | solution.py:394
  34.9 0.0 collective-permute-start.5
  34.9 2.0 %shard_map.62 = (f32[19,12,8,128]{3,2,1,0:T(8,128)S(1)}, f32[19,8,128]{2,1,0:T(8,128)S(1)}) custom-call(f32[19,16,8,128]{3,2,1,0:T(8,128)S(1)} %get-tuple-element.25.main), custom_call_target="tpu_custom_call" | custom-call | tf_op jit(solution)/shard_map/pallas_call | solution.py:440
  37.0 0.0 collective-permute-done.4.ahead
  37.0 3.2 %collective-permute-done.5.back = f32[10,8,128]{2,1,0:T(8,128)S(1)} collective-permute-done((f32[10,8,128]{2,1,0:T(8,128)S(1)}, f32[10,8,128]{2,1,0:T(8,128)S(1)}, u32[]{:S(2)}, u32[]{:S(2)}) %collective-permute-start.5) | collective-permute-done | bytes 40992 | tf_op jit(solution)/shard_map/ppermute | solution.py:394
  40.1 0.7 %shard_map.63 = (f32[2176,128]{1,0:T(8,128)S(1)}, f32[43,8,128]{2,1,0:T(8,128)S(1)}, f32[43,8,128]{2,1,0:T(8,128)S(1)}) custom-call(f32[19,12,8,128]{3,2,1,0:T(8,128)S(1)} %get-tuple-element.26.inner, f32[19,8,128]{2,1,0:T(8,128)S(1)} %get-tuple-element.27.inner_edge, f32[19,8,128]{2,1,0:T(8,128)S(1)} %get-tuple-element.28.edge, ...), custom_call_target="tpu_custom_call" | custom-call | tf_op jit(solution)/shard_map/pallas_call | solution.py:446
  40.9 0.0 collective-permute-start.6
  40.9 2.9 %collective-permute-start.7 = (f32[43,8,128]{2,1,0:T(8,128)S(1)}, f32[43,8,128]{2,1,0:T(8,128)S(1)}, u32[]{:S(2)}, u32[]{:S(2)}) collective-permute-start(f32[43,8,128]{2,1,0:T(8,128)S(1)} %get-tuple-element.33), channel_id=1, source_target_pairs={{1,0},{2,1},{3,2},{4,3},{5,4},{6,5},{7,6},{8,7},{9,8},{10,9},{11,1... | collective-permute-start | bytes 528392 | tf_op jit(solution)/shard_map/ppermute | solution.py:378
  43.8 3.1 %collective-permute-done.6.below = f32[43,8,128]{2,1,0:T(8,128)S(1)} collective-permute-done((f32[43,8,128]{2,1,0:T(8,128)S(1)}, f32[43,8,128]{2,1,0:T(8,128)S(1)}, u32[]{:S(2)}, u32[]{:S(2)}) %collective-permute-start.6) | collective-permute-done | bytes 176160 | tf_op jit(solution)/shard_map/ppermute | solution.py:378
  47.0 0.0 collective-permute-done.7.above
  47.0 2.5 %shard_map.64 = (f32[19,4,8,128]{3,2,1,0:T(8,128)}, f32[1,2]{1,0:T(1,128)}, f32[2176,128]{1,0:T(8,128)S(1)}) custom-call(f32[2176,128]{1,0:T(8,128)S(1)} %get-tuple-element.31.flat_in, f32[43,8,128]{2,1,0:T(8,128)S(1)} %collective-permute-done.6.below, f32[43,8,128]{2,1,0:T(8,128)S(1)} %collective-permute-done.7.above, ...), custom_call_target="tpu_custom_call", output_to_operand_aliasing={{2}: (0, {})} | custom-call | tf_op jit(solution)/shard_map/pallas_call | solution.py:452
Async XLA Ops:
  1.7 18.6 %collective-permute-start.1 = (f32[20,2,8,128]{3,2,1,0:T(8,128)S(1)}, f32[20,2,8,128]{3,2,1,0:T(8,128)S(1)}, u32[]{:S(2)}, u32[]{:S(2)}) collective-permute-start(f32[20,2,8,128]{3,2,1,0:T(8,128)S(1)} %get-tuple-element.19.low), channel_id=1, source_target_pairs={{1,0},{2,1},{3,2},{4,3},{5,4},{6,5},{7,6},{8,7},{9,8},{10,9},{11,1... | collective-permute-start | bytes 491528 | tf_op jit(solution)/shard_map/ppermute | solution.py:378
  17.4 6.0 %collective-permute-start = (f32[20,2,8,128]{3,2,1,0:T(8,128)S(1)}, f32[20,2,8,128]{3,2,1,0:T(8,128)S(1)}, u32[]{:S(2)}, u32[]{:S(2)}) collective-permute-start(f32[20,2,8,128]{3,2,1,0:T(8,128)S(1)} %get-tuple-element.20.high), channel_id=1, source_target_pairs={{0,1},{1,2},{2,3},{3,4},{4,5},{5,6},{6,7},{7,8},{8,9},{9,10},{10,1... | collective-permute-start | bytes 491528 | tf_op jit(solution)/shard_map/ppermute | solution.py:378
  23.8 7.4 %collective-permute-start.2 = (f32[62,8,128]{2,1,0:T(8,128)S(1)}, f32[62,8,128]{2,1,0:T(8,128)S(1)}, u32[]{:S(2)}, u32[]{:S(2)}) collective-permute-start(f32[62,8,128]{2,1,0:T(8,128)S(1)} %get-tuple-element.23), channel_id=1, source_target_pairs={{0,32},{1,0},{2,34},{3,2},{4,36},{5,4},{6,38},{7,6},{8,40},{9,8},{... | collective-permute-start | bytes 761864 | tf_op jit(solution)/shard_map/ppermute | solution.py:394
  25.3 6.3 %collective-permute-start.3 = (f32[62,8,128]{2,1,0:T(8,128)S(1)}, f32[62,8,128]{2,1,0:T(8,128)S(1)}, u32[]{:S(2)}, u32[]{:S(2)}) collective-permute-start(f32[62,8,128]{2,1,0:T(8,128)S(1)} %get-tuple-element.24), channel_id=1, source_target_pairs={{32,0},{0,1},{34,2},{2,3},{36,4},{4,5},{38,6},{6,7},{40,8},{8,9},{... | collective-permute-start | bytes 761864 | tf_op jit(solution)/shard_map/ppermute | solution.py:394
  32.1 4.8 %collective-permute-start.4 = (f32[10,8,128]{2,1,0:T(8,128)S(1)}, f32[10,8,128]{2,1,0:T(8,128)S(1)}, u32[]{:S(2)}, u32[]{:S(2)}) collective-permute-start(f32[10,8,128]{2,1,0:T(8,128)S(1)} %get-tuple-element.29), channel_id=1, source_target_pairs={{0,128},{1,0},{2,130},{3,2},{4,132},{5,4},{6,134},{7,6},{8,136},{9... | collective-permute-start | bytes 122888 | tf_op jit(solution)/shard_map/ppermute | solution.py:394
  34.9 5.2 %collective-permute-start.5 = (f32[10,8,128]{2,1,0:T(8,128)S(1)}, f32[10,8,128]{2,1,0:T(8,128)S(1)}, u32[]{:S(2)}, u32[]{:S(2)}) collective-permute-start(f32[10,8,128]{2,1,0:T(8,128)S(1)} %get-tuple-element.30), channel_id=1, source_target_pairs={{128,0},{0,1},{130,2},{2,3},{132,4},{4,5},{134,6},{6,7},{136,8},{8... | collective-permute-start | bytes 122888 | tf_op jit(solution)/shard_map/ppermute | solution.py:394
  40.9 6.1 %collective-permute-start.6 = (f32[43,8,128]{2,1,0:T(8,128)S(1)}, f32[43,8,128]{2,1,0:T(8,128)S(1)}, u32[]{:S(2)}, u32[]{:S(2)}) collective-permute-start(f32[43,8,128]{2,1,0:T(8,128)S(1)} %get-tuple-element.32), channel_id=1, source_target_pairs={{0,1},{1,2},{2,3},{3,4},{4,5},{5,6},{6,7},{7,8},{8,9},{9,10},{10,1... | collective-permute-start | bytes 528392 | tf_op jit(solution)/shard_map/ppermute | solution.py:378
  40.9 6.1 %collective-permute-start.7 = (f32[43,8,128]{2,1,0:T(8,128)S(1)}, f32[43,8,128]{2,1,0:T(8,128)S(1)}, u32[]{:S(2)}, u32[]{:S(2)}) collective-permute-start(f32[43,8,128]{2,1,0:T(8,128)S(1)} %get-tuple-element.33), channel_id=1, source_target_pairs={{1,0},{2,1},{3,2},{4,3},{5,4},{6,5},{7,6},{8,7},{9,8},{10,9},{11,1... | collective-permute-start | bytes 528392 | tf_op jit(solution)/shard_map/ppermute | solution.py:378

commit v4 on v3

--- a/solution.py
+++ b/solution.py
@@ -31,17 +31,19 @@
 ]
 OPPOSITE = [0, 2, 1, 4, 3, 6, 5, 8, 7, 10, 9, 12, 11, 14, 13, 16, 15, 18, 17]
 Q = 19
-UP_Y = [i for i in range(Q) if VELOCITIES[i][1] == 1]
-DOWN_Y = [i for i in range(Q) if VELOCITIES[i][1] == -1]
 SOLID = 3.0e38
 Z_ORDER = sorted(range(Q), key=lambda i: {1: 0, -1: 1, 0: 2}[VELOCITIES[i][0]])
 SLOT = [Z_ORDER.index(i) for i in range(Q)]
+UP_Y = [i for i in Z_ORDER if VELOCITIES[i][1] == 1]
+DOWN_Y = [i for i in Z_ORDER if VELOCITIES[i][1] == -1]
+Y_FIRST = [3 * s + min(s // 5, 2) for s in SLOT]
+Y_FAR = [15, 31, 59, 60, 61]
+Y_TILES = 52
 PER_SLOT = 14
 NEAR = 34
 FAR = 9
 FLAT_ROWS = 8 * 8 * NEAR
 F32 = jnp.float32
-UNROLL = 2
 VMEM = pl.BlockSpec(memory_space=pltpu.VMEM)
 SMEM = pl.BlockSpec(memory_space=pltpu.SMEM)
 HBM = pl.BlockSpec(memory_space=pltpu.HBM)
@@ -132,14 +134,6 @@
     return out
 
 
-def over_rows(first, last, body):
-    def step(row, carry):
-        body(row)
-        return carry
-
-    lax.fori_loop(first, last, step, 0, unroll=UNROLL)
-
-
 def gather_columns(values, rows):
     lane_row = lanes() // 8
     tile = jnp.full((8, 128), SOLID, F32)
@@ -169,7 +163,7 @@
     copies[2].wait()
 
 
-def first_relax(low, high, below, above, moved, own, ahead, back, turn):
+def first_relax(high, low, above, below, moved, own, ahead, back, turn, stage):
     place = lax.axis_index("gz")
     at_low = place == 0
     at_high = place == lax.axis_size("gz") - 1
@@ -194,17 +188,26 @@
         for i in range(Q):
             own[i, row] = values[i]
     up = place % 2 == 0
-    for message, high_rows in ((ahead, up), (back, jnp.logical_not(up))):
+    for side, (message, high_rows) in enumerate(((ahead, up), (back, jnp.logical_not(up)))):
         first = jnp.where(high_rows, 5, 0)
         far = jnp.where(high_rows, 4, 3)
         for i in range(Q):
             for k in range(3):
-                message[3 * i + k] = own[i, first + k]
+                at = 8 * (Y_FIRST[i] + k)
+                stage[side, at : at + 8] = own[i, first + k]
         for k in range(5):
-            message[3 * Q + k] = own[jnp.where(high_rows, UP_Y[k], DOWN_Y[k]), far]
-
-
-def join_rows(own, ahead, back, main, edge, x_ahead, x_back):
+            at = 8 * Y_FAR[k]
+            stage[side, at : at + 8] = own[jnp.where(high_rows, UP_Y[k], DOWN_Y[k]), far]
+        stage[side, 8 * 62 :] = jnp.full((16, 128), SOLID, F32)
+        for group in range(8):
+            for layer in range(1, 7):
+                message[6 * group + layer - 1] = stage[side, pl.ds(64 * group + layer, 8, stride=8)]
+        for group in range(2):
+            message[48 + group] = stage[side, pl.ds(64 * group, 8, stride=8)]
+            message[50 + group] = stage[side, pl.ds(64 * (group + 2) + 7, 8, stride=8)]
+
+
+def join_rows(own, ahead, back, main, edge, x_ahead, x_back, stage):
     place = lax.axis_index("gy")
     up = lax.axis_index("gz") % 2 == 0
     outside_low = place == 0
@@ -212,15 +215,24 @@
     for i in range(Q):
         main[i, 0] = jnp.full((8, 128), SOLID, F32)
         main[i, 15] = jnp.full((8, 128), SOLID, F32)
-    for message, low_rows in ((ahead, up), (back, jnp.logical_not(up))):
+    for side, (message, low_rows) in enumerate(((ahead, up), (back, jnp.logical_not(up)))):
         outside = jnp.where(low_rows, outside_low, outside_high)
         first = jnp.where(low_rows, 1, 12)
         far = jnp.where(low_rows, 0, 15)
+        stage[side] = jnp.full((512, 128), SOLID, F32)
+        for group in range(8):
+            for layer in range(1, 7):
+                stage[side, pl.ds(64 * group + layer, 8, stride=8)] = message[6 * group + layer - 1]
+        for group in range(2):
+            stage[side, pl.ds(64 * group, 8, stride=8)] = message[48 + group]
+            stage[side, pl.ds(64 * (group + 2) + 7, 8, stride=8)] = message[50 + group]
         for i in range(Q):
             for k in range(3):
-                main[i, first + k] = jnp.where(outside, SOLID, message[3 * i + k])
+                at = 8 * (Y_FIRST[i] + k)
+                main[i, first + k] = jnp.where(outside, SOLID, stage[side, at : at + 8])
         for k in range(5):
-            value = jnp.where(outside, SOLID, message[3 * Q + k])
+            at = 8 * Y_FAR[k]
+            value = jnp.where(outside, SOLID, stage[side, at : at + 8])
             main[jnp.where(low_rows, UP_Y[k], DOWN_Y[k]), far] = value
     edges = []
     for i in range(Q):
@@ -253,8 +265,10 @@
         for i in range(Q):
             out[i, row - 2] = values[i]
 
-    over_rows(1, 15, first)
-    over_rows(2, 14, second)
+    for row in range(1, 15):
+        first(row)
+    for row in range(2, 14):
+        second(row)
     for i in range(Q):
         edge[i] = gather_columns([out[i, k] for k in range(12)], range(2, 14))
 
@@ -324,14 +338,15 @@
         )
 
     def joined(i, at):
-        return flat[pl.ds(pl.multiple_of(8 * (PER_SLOT * SLOT[i] + at), 8), 8)]
+        return flat[pl.ds(8 * (PER_SLOT * SLOT[i] + at), 8)]
 
     def third(row):
         values = relax_row(joined, row - 2)
         for i in range(Q):
             middle[i, row - 3] = values[i]
 
-    over_rows(3, 13, third)
+    for row in range(3, 13):
+        third(row)
     patches = []
     for side in range(2):
         values = [joined(i, 12 + side) for i in range(Q)]
@@ -426,15 +441,16 @@
     below, above = ring_exchange(low, high, "gz")
     own, ahead, back = call(
         first_relax,
-        [shape(Q, 8, 8, 128), shape(3 * Q + 5, 8, 128), shape(3 * Q + 5, 8, 128)],
+        [shape(Q, 8, 8, 128), shape(Y_TILES, 8, 128), shape(Y_TILES, 8, 128)],
         [VMEM] * 5,
-        scratch=[pltpu.VMEM((Q + 1, 64, 128), F32)],
-    )(low, high, below, above, moved)
+        scratch=[pltpu.VMEM((Q + 1, 64, 128), F32), pltpu.VMEM((2, 512, 128), F32)],
+    )(high, low, above, below, moved)
     ahead, back = loop_exchange(ahead, back, "gy")
     main, edge, x_ahead, x_back = call(
         join_rows,
         [shape(Q, 16, 8, 128), shape(Q, 8, 128), shape(10, 8, 128), shape(10, 8, 128)],
         [VMEM] * 3,
+        scratch=[pltpu.VMEM((2, 512, 128), F32)],
     )(own, ahead, back)
     x_ahead, x_back = loop_exchange(x_ahead, x_back, "gx")
     inner, inner_edge = call(

time: 49.6 us -> 45.9 us (0.925)
  waiting for transfers between devices: 18 us -> 15.5 us
  Pallas kernels: 7.21 us -> 6.03 us
    ppermute x4, waiting for transfers between devices: 9.08 us -> 6.11 us  [ring_exchange(): return (lax.ppermute(to_high, axis, up), lax.ppermute(to_low, axis, down))]
    pallas_call x1, Pallas kernels: 2.04 us -> 1.14 us  [on_device(): call(two_steps, [shape(Q, 12, 8, 128), shape(Q, 8, 128)], [VMEM], scratch...]
  transfers between devices with their start and end apart: 8 -> 8, of which waited for: 6 -> 6; matrix products, arithmetic and copies ran while one was open for 0% -> 0% of each run, Pallas kernels for 4% -> 2%
where the time goes in v4:
time: 45.9 us; the launch traced here: 45.8 us
  starting transfers between devices  23.6 us (51%)
  waiting for transfers between devices  15.5 us (34%)
  Pallas kernels  6.03 us (13%)
  between operations  0.67 us (1%)
    ppermute x4, starting transfers between devices, ring_exchange(): return (lax.ppermute(to_high, axis, up), lax.ppermute(to_low, axis, down))  18.7 us
    ppermute x4, waiting for transfers between devices, loop_exchange(): return (lax.ppermute(ahead, axes, pairs), lax.ppermute(back, axes, inverse))  9.37 us
    ppermute x4, waiting for transfers between devices, ring_exchange(): return (lax.ppermute(to_high, axis, up), lax.ppermute(to_low, axis, down))  6.11 us
    ppermute x4, starting transfers between devices, loop_exchange(): return (lax.ppermute(ahead, axes, pairs), lax.ppermute(back, axes, inverse))  4.83 us
    pallas_call x1, Pallas kernels, on_device(): call(last_two_steps, [shape(Q, 4, 8, 128), shape(1, 2), shape(FLAT_ROWS,...  2.05 us
    pallas_call x1, Pallas kernels, on_device(): call(two_steps, [shape(Q, 12, 8, 128), shape(Q, 8, 128)], [VMEM], scratch...  1.14 us
    pallas_call x1, Pallas kernels, on_device(): call(split_slabs, [shape(Q + 1, 2, 8, 128), shape(Q + 1, 2, 8, 128), shap...  1.04 us
  transfers between devices with their start and end apart: 8, of which 6 were waited for; matrix products, arithmetic and copies ran while one was open for 0% of the time, Pallas kernels for 2%

profile of v4, /device:TPU:26, one launch (start us, length us, event | category | flops | bytes accessed | tf_op | source)
XLA Modules:
  0.0 45.8 jit_solution(16067809450840647138)
XLA Ops:
  0.6 1.0 %shard_map.59 = (f32[20,2,8,128]{3,2,1,0:T(8,128)S(1)}, f32[20,2,8,128]{3,2,1,0:T(8,128)S(1)}, f32[2,8,128]{2,1,0:T(8,128)S(1)}) custom-call(f32[19,4,8,128]{3,2,1,0:T(8,128)} %relative.1, s32[4,8,128]{2,1,0:T(8,128)} %fluid.1, s32[1,2]{1,0:T(1,128)} %bitcast.3), custom_call_target="tpu_custom_call" | custom-call | tf_op jit(solution)/shard_map/pallas_call | solution.py:431
  1.7 0.0 collective-permute-start.1
  1.7 15.8 %collective-permute-start = (f32[20,2,8,128]{3,2,1,0:T(8,128)S(1)}, f32[20,2,8,128]{3,2,1,0:T(8,128)S(1)}, u32[]{:S(2)}, u32[]{:S(2)}) collective-permute-start(f32[20,2,8,128]{3,2,1,0:T(8,128)S(1)} %get-tuple-element.20.low), channel_id=1, source_target_pairs={{1,0},{2,1},{3,2},{4,3},{5,4},{6,5},{7,6},{8,7},{9,8},{10,9},{11,1... | collective-permute-start | bytes 491528 | tf_op jit(solution)/shard_map/ppermute | solution.py:393
  17.5 3.0 %collective-permute-done.1.below = f32[20,2,8,128]{3,2,1,0:T(8,128)S(1)} collective-permute-done((f32[20,2,8,128]{3,2,1,0:T(8,128)S(1)}, f32[20,2,8,128]{3,2,1,0:T(8,128)S(1)}, u32[]{:S(2)}, u32[]{:S(2)}) %collective-permute-start.1) | collective-permute-done | bytes 163872 | tf_op jit(solution)/shard_map/ppermute | solution.py:393
  20.5 0.0 collective-permute-done.above
  20.5 0.5 %shard_map.60 = (f32[19,8,8,128]{3,2,1,0:T(8,128)S(1)}, f32[52,8,128]{2,1,0:T(8,128)S(1)}, f32[52,8,128]{2,1,0:T(8,128)S(1)}) custom-call(f32[20,2,8,128]{3,2,1,0:T(8,128)S(1)} %get-tuple-element.19.high, f32[20,2,8,128]{3,2,1,0:T(8,128)S(1)} %get-tuple-element.20.low, f32[20,2,8,128]{3,2,1,0:T(8,128)S(1)} %collective-permute-done.above, ...), custom_call_target="tpu_custom_call" | custom-call | tf_op jit(solution)/shard_map/pallas_call | solution.py:442
  20.9 1.5 %collective-permute-start.2 = (f32[52,8,128]{2,1,0:T(8,128)S(1)}, f32[52,8,128]{2,1,0:T(8,128)S(1)}, u32[]{:S(2)}, u32[]{:S(2)}) collective-permute-start(f32[52,8,128]{2,1,0:T(8,128)S(1)} %get-tuple-element.23), channel_id=1, source_target_pairs={{0,32},{1,0},{2,34},{3,2},{4,36},{5,4},{6,38},{7,6},{8,40},{9,8},{... | collective-permute-start | bytes 638984 | tf_op jit(solution)/shard_map/ppermute | solution.py:409
  22.4 0.5 %collective-permute-start.3 = (f32[52,8,128]{2,1,0:T(8,128)S(1)}, f32[52,8,128]{2,1,0:T(8,128)S(1)}, u32[]{:S(2)}, u32[]{:S(2)}) collective-permute-start(f32[52,8,128]{2,1,0:T(8,128)S(1)} %get-tuple-element.24), channel_id=1, source_target_pairs={{32,0},{0,1},{34,2},{2,3},{36,4},{4,5},{38,6},{6,7},{40,8},{8,9},{... | collective-permute-start | bytes 638984 | tf_op jit(solution)/shard_map/ppermute | solution.py:409
  23.0 4.4 %collective-permute-done.2.ahead = f32[52,8,128]{2,1,0:T(8,128)S(1)} collective-permute-done((f32[52,8,128]{2,1,0:T(8,128)S(1)}, f32[52,8,128]{2,1,0:T(8,128)S(1)}, u32[]{:S(2)}, u32[]{:S(2)}) %collective-permute-start.2) | collective-permute-done | bytes 213024 | tf_op jit(solution)/shard_map/ppermute | solution.py:409
  27.4 0.9 %collective-permute-done.3.back = f32[52,8,128]{2,1,0:T(8,128)S(1)} collective-permute-done((f32[52,8,128]{2,1,0:T(8,128)S(1)}, f32[52,8,128]{2,1,0:T(8,128)S(1)}, u32[]{:S(2)}, u32[]{:S(2)}) %collective-permute-start.3) | collective-permute-done | bytes 213024 | tf_op jit(solution)/shard_map/ppermute | solution.py:409
  28.3 0.6 %shard_map.61 = (f32[19,16,8,128]{3,2,1,0:T(8,128)S(1)}, f32[19,8,128]{2,1,0:T(8,128)S(1)}, f32[10,8,128]{2,1,0:T(8,128)S(1)}, f32[10,8,128]{2,1,0:T(8,128)S(1)}) custom-call(f32[19,8,8,128]{3,2,1,0:T(8,128)S(1)} %get-tuple-element.22.own, f32[52,8,128]{2,1,0:T(8,128)S(1)} %collective-permute-done.2.ahead, f32[52,8,128]{2,1,0:T(8,128)S(1)} %collective-permute-done.3.back), custom_call_target="tpu_custom_call" | custom-call | tf_op jit(solution)/shard_map/pallas_call | solution.py:449
  28.9 2.8 %collective-permute-start.4 = (f32[10,8,128]{2,1,0:T(8,128)S(1)}, f32[10,8,128]{2,1,0:T(8,128)S(1)}, u32[]{:S(2)}, u32[]{:S(2)}) collective-permute-start(f32[10,8,128]{2,1,0:T(8,128)S(1)} %get-tuple-element.29), channel_id=1, source_target_pairs={{0,128},{1,0},{2,130},{3,2},{4,132},{5,4},{6,134},{7,6},{8,136},{9... | collective-permute-start | bytes 122888 | tf_op jit(solution)/shard_map/ppermute | solution.py:409
  31.7 0.0 collective-permute-start.5
  31.7 1.1 %shard_map.62 = (f32[19,12,8,128]{3,2,1,0:T(8,128)S(1)}, f32[19,8,128]{2,1,0:T(8,128)S(1)}) custom-call(f32[19,16,8,128]{3,2,1,0:T(8,128)S(1)} %get-tuple-element.25.main), custom_call_target="tpu_custom_call" | custom-call | tf_op jit(solution)/shard_map/pallas_call | solution.py:456
  32.8 0.5 %collective-permute-done.4.ahead = f32[10,8,128]{2,1,0:T(8,128)S(1)} collective-permute-done((f32[10,8,128]{2,1,0:T(8,128)S(1)}, f32[10,8,128]{2,1,0:T(8,128)S(1)}, u32[]{:S(2)}, u32[]{:S(2)}) %collective-permute-start.4) | collective-permute-done | bytes 40992 | tf_op jit(solution)/shard_map/ppermute | solution.py:409
  33.4 3.5 %collective-permute-done.5.back = f32[10,8,128]{2,1,0:T(8,128)S(1)} collective-permute-done((f32[10,8,128]{2,1,0:T(8,128)S(1)}, f32[10,8,128]{2,1,0:T(8,128)S(1)}, u32[]{:S(2)}, u32[]{:S(2)}) %collective-permute-start.5) | collective-permute-done | bytes 40992 | tf_op jit(solution)/shard_map/ppermute | solution.py:409
  36.9 0.7 %shard_map.63 = (f32[2176,128]{1,0:T(8,128)S(1)}, f32[43,8,128]{2,1,0:T(8,128)S(1)}, f32[43,8,128]{2,1,0:T(8,128)S(1)}) custom-call(f32[19,12,8,128]{3,2,1,0:T(8,128)S(1)} %get-tuple-element.26.inner, f32[19,8,128]{2,1,0:T(8,128)S(1)} %get-tuple-element.27.inner_edge, f32[19,8,128]{2,1,0:T(8,128)S(1)} %get-tuple-element.28.edge, ...), custom_call_target="tpu_custom_call" | custom-call | tf_op jit(solution)/shard_map/pallas_call | solution.py:462
  37.6 0.0 collective-permute-start.6
  37.6 2.9 %collective-permute-start.7 = (f32[43,8,128]{2,1,0:T(8,128)S(1)}, f32[43,8,128]{2,1,0:T(8,128)S(1)}, u32[]{:S(2)}, u32[]{:S(2)}) collective-permute-start(f32[43,8,128]{2,1,0:T(8,128)S(1)} %get-tuple-element.33), channel_id=1, source_target_pairs={{1,0},{2,1},{3,2},{4,3},{5,4},{6,5},{7,6},{8,7},{9,8},{10,9},{11,1... | collective-permute-start | bytes 528392 | tf_op jit(solution)/shard_map/ppermute | solution.py:393
  40.6 3.1 %collective-permute-done.6.below = f32[43,8,128]{2,1,0:T(8,128)S(1)} collective-permute-done((f32[43,8,128]{2,1,0:T(8,128)S(1)}, f32[43,8,128]{2,1,0:T(8,128)S(1)}, u32[]{:S(2)}, u32[]{:S(2)}) %collective-permute-start.6) | collective-permute-done | bytes 176160 | tf_op jit(solution)/shard_map/ppermute | solution.py:393
  43.7 0.0 collective-permute-done.7.above
  43.7 2.1 %shard_map.64 = (f32[19,4,8,128]{3,2,1,0:T(8,128)}, f32[1,2]{1,0:T(1,128)}, f32[2176,128]{1,0:T(8,128)S(1)}) custom-call(f32[2176,128]{1,0:T(8,128)S(1)} %get-tuple-element.31.flat_in, f32[43,8,128]{2,1,0:T(8,128)S(1)} %collective-permute-done.6.below, f32[43,8,128]{2,1,0:T(8,128)S(1)} %collective-permute-done.7.above, ...), custom_call_target="tpu_custom_call", output_to_operand_aliasing={{2}: (0, {})} | custom-call | tf_op jit(solution)/shard_map/pallas_call | solution.py:468
Async XLA Ops:
  1.7 18.8 %collective-permute-start.1 = (f32[20,2,8,128]{3,2,1,0:T(8,128)S(1)}, f32[20,2,8,128]{3,2,1,0:T(8,128)S(1)}, u32[]{:S(2)}, u32[]{:S(2)}) collective-permute-start(f32[20,2,8,128]{3,2,1,0:T(8,128)S(1)} %get-tuple-element.19.high), channel_id=1, source_target_pairs={{0,1},{1,2},{2,3},{3,4},{4,5},{5,6},{6,7},{7,8},{8,9},{9,10},{10,1... | collective-permute-start | bytes 491528 | tf_op jit(solution)/shard_map/ppermute | solution.py:393
  1.7 18.7 %collective-permute-start = (f32[20,2,8,128]{3,2,1,0:T(8,128)S(1)}, f32[20,2,8,128]{3,2,1,0:T(8,128)S(1)}, u32[]{:S(2)}, u32[]{:S(2)}) collective-permute-start(f32[20,2,8,128]{3,2,1,0:T(8,128)S(1)} %get-tuple-element.20.low), channel_id=1, source_target_pairs={{1,0},{2,1},{3,2},{4,3},{5,4},{6,5},{7,6},{8,7},{9,8},{10,9},{11,1... | collective-permute-start | bytes 491528 | tf_op jit(solution)/shard_map/ppermute | solution.py:393
  20.9 6.5 %collective-permute-start.2 = (f32[52,8,128]{2,1,0:T(8,128)S(1)}, f32[52,8,128]{2,1,0:T(8,128)S(1)}, u32[]{:S(2)}, u32[]{:S(2)}) collective-permute-start(f32[52,8,128]{2,1,0:T(8,128)S(1)} %get-tuple-element.23), channel_id=1, source_target_pairs={{0,32},{1,0},{2,34},{3,2},{4,36},{5,4},{6,38},{7,6},{8,40},{9,8},{... | collective-permute-start | bytes 638984 | tf_op jit(solution)/shard_map/ppermute | solution.py:409
  22.4 5.8 %collective-permute-start.3 = (f32[52,8,128]{2,1,0:T(8,128)S(1)}, f32[52,8,128]{2,1,0:T(8,128)S(1)}, u32[]{:S(2)}, u32[]{:S(2)}) collective-permute-start(f32[52,8,128]{2,1,0:T(8,128)S(1)} %get-tuple-element.24), channel_id=1, source_target_pairs={{32,0},{0,1},{34,2},{2,3},{36,4},{4,5},{38,6},{6,7},{40,8},{8,9},{... | collective-permute-start | bytes 638984 | tf_op jit(solution)/shard_map/ppermute | solution.py:409
  28.9 4.5 %collective-permute-start.4 = (f32[10,8,128]{2,1,0:T(8,128)S(1)}, f32[10,8,128]{2,1,0:T(8,128)S(1)}, u32[]{:S(2)}, u32[]{:S(2)}) collective-permute-start(f32[10,8,128]{2,1,0:T(8,128)S(1)} %get-tuple-element.29), channel_id=1, source_target_pairs={{0,128},{1,0},{2,130},{3,2},{4,132},{5,4},{6,134},{7,6},{8,136},{9... | collective-permute-start | bytes 122888 | tf_op jit(solution)/shard_map/ppermute | solution.py:409
  31.7 5.2 %collective-permute-start.5 = (f32[10,8,128]{2,1,0:T(8,128)S(1)}, f32[10,8,128]{2,1,0:T(8,128)S(1)}, u32[]{:S(2)}, u32[]{:S(2)}) collective-permute-start(f32[10,8,128]{2,1,0:T(8,128)S(1)} %get-tuple-element.30), channel_id=1, source_target_pairs={{128,0},{0,1},{130,2},{2,3},{132,4},{4,5},{134,6},{6,7},{136,8},{8... | collective-permute-start | bytes 122888 | tf_op jit(solution)/shard_map/ppermute | solution.py:409
  37.6 6.1 %collective-permute-start.6 = (f32[43,8,128]{2,1,0:T(8,128)S(1)}, f32[43,8,128]{2,1,0:T(8,128)S(1)}, u32[]{:S(2)}, u32[]{:S(2)}) collective-permute-start(f32[43,8,128]{2,1,0:T(8,128)S(1)} %get-tuple-element.32), channel_id=1, source_target_pairs={{0,1},{1,2},{2,3},{3,4},{4,5},{5,6},{6,7},{7,8},{8,9},{9,10},{10,1... | collective-permute-start | bytes 528392 | tf_op jit(solution)/shard_map/ppermute | solution.py:393
  37.6 6.1 %collective-permute-start.7 = (f32[43,8,128]{2,1,0:T(8,128)S(1)}, f32[43,8,128]{2,1,0:T(8,128)S(1)}, u32[]{:S(2)}, u32[]{:S(2)}) collective-permute-start(f32[43,8,128]{2,1,0:T(8,128)S(1)} %get-tuple-element.33), channel_id=1, source_target_pairs={{1,0},{2,1},{3,2},{4,3},{5,4},{6,5},{7,6},{8,7},{9,8},{10,9},{11,1... | collective-permute-start | bytes 528392 | tf_op jit(solution)/shard_map/ppermute | solution.py:393

commit v5 on v4

--- a/solution.py
+++ b/solution.py
@@ -142,52 +142,63 @@
     return tile
 
 
-def split_slabs(relative, fluid, new_owner, low, high, moved, kinds, owner, sems):
+def split_slabs(relative, fluid, new_owner, far, near, moved, kinds, owner, sems):
+    place = lax.axis_index("gz")
+    far_first = 2 * lax.rem(place, 2)
+    near_first = 2 - far_first
     copies = [
         pltpu.make_async_copy(fluid, kinds, sems.at[0]),
-        pltpu.make_async_copy(relative.at[:, 2:4], high.at[0:Q], sems.at[1]),
-        pltpu.make_async_copy(relative.at[:, 0:2], low.at[0:Q], sems.at[2]),
+        pltpu.make_async_copy(relative.at[:, pl.ds(far_first, 2)], far.at[0:Q], sems.at[1]),
+        pltpu.make_async_copy(relative.at[:, pl.ds(near_first, 2)], near.at[0:Q], sems.at[2]),
         pltpu.make_async_copy(new_owner, owner, sems.at[3]),
     ]
     for copy in copies:
         copy.start()
     copies[3].wait()
-    place = lax.axis_index("gz")
     moved[0] = jnp.full((8, 128), jnp.where((owner[0, 0] == place - 1) & (place > 0), 1.0, 0.0), F32)
     inside = place < lax.axis_size("gz") - 1
     moved[1] = jnp.full((8, 128), jnp.where((owner[0, 1] == place + 1) & inside, 1.0, 0.0), F32)
     copies[0].wait()
-    low[Q] = kinds[0:2].astype(F32)
-    high[Q] = kinds[2:4].astype(F32)
+    far[Q] = kinds[pl.ds(far_first, 2)].astype(F32)
+    near[Q] = kinds[pl.ds(near_first, 2)].astype(F32)
     copies[1].wait()
     copies[2].wait()
 
 
-def first_relax(high, low, above, below, moved, own, ahead, back, turn, stage):
+def first_relax(far, near, got_far, got_near, moved, own, ahead, back, turn, stage):
     place = lax.axis_index("gz")
     at_low = place == 0
     at_high = place == lax.axis_size("gz") - 1
+    even = lax.rem(place, 2) == 0
     swap_low = moved[0] > 0.5
     swap_high = moved[1] > 0.5
+
+    def slabs(i, k):
+        low = jnp.where(even, far[i, k], near[i, k])
+        high = jnp.where(even, near[i, k], far[i, k])
+        below = jnp.where(even, got_far[i, k], got_near[i, k])
+        above = jnp.where(even, got_near[i, k], got_far[i, k])
+        return low, high, below, above
+
     for k in range(2):
-        turn[Q, 8 * k : 8 * k + 8] = jnp.where(at_low, 0.0, below[Q, k])
-        turn[Q, 8 * (k + 2) : 8 * (k + 3)] = low[Q, k]
-        turn[Q, 8 * (k + 4) : 8 * (k + 5)] = high[Q, k]
-        turn[Q, 8 * (k + 6) : 8 * (k + 7)] = jnp.where(at_high, 0.0, above[Q, k])
+        low, high, below, above = slabs(Q, k)
+        turn[Q, 8 * k : 8 * k + 8] = jnp.where(at_low, 0.0, below)
+        turn[Q, 8 * (k + 2) : 8 * (k + 3)] = low
+        turn[Q, 8 * (k + 4) : 8 * (k + 5)] = high
+        turn[Q, 8 * (k + 6) : 8 * (k + 7)] = jnp.where(at_high, 0.0, above)
     for i in range(Q):
         for k in range(2):
-            mine, other = low[i, k], below[i, k]
-            turn[i, 8 * k : 8 * k + 8] = jnp.where(swap_low, mine, other)
-            turn[i, 8 * (k + 2) : 8 * (k + 3)] = jnp.where(swap_low, other, mine)
-            mine, other = high[i, k], above[i, k]
-            turn[i, 8 * (k + 4) : 8 * (k + 5)] = jnp.where(swap_high, other, mine)
-            turn[i, 8 * (k + 6) : 8 * (k + 7)] = jnp.where(swap_high, mine, other)
+            low, high, below, above = slabs(i, k)
+            turn[i, 8 * k : 8 * k + 8] = jnp.where(swap_low, low, below)
+            turn[i, 8 * (k + 2) : 8 * (k + 3)] = jnp.where(swap_low, below, low)
+            turn[i, 8 * (k + 4) : 8 * (k + 5)] = jnp.where(swap_high, above, high)
+            turn[i, 8 * (k + 6) : 8 * (k + 7)] = jnp.where(swap_high, high, above)
     for row in range(8):
         wet = turn[Q, pl.ds(row, 8, stride=8)] > 0.5
         values = relax_wet([turn[i, pl.ds(row, 8, stride=8)] for i in range(Q)], wet)
         for i in range(Q):
             own[i, row] = values[i]
-    up = place % 2 == 0
+    up = even
     for side, (message, high_rows) in enumerate(((ahead, up), (back, jnp.logical_not(up)))):
         first = jnp.where(high_rows, 5, 0)
         far = jnp.where(high_rows, 4, 3)
@@ -273,7 +284,7 @@
         edge[i] = gather_columns([out[i, k] for k in range(12)], range(2, 14))
 
 
-def patch_two_steps(inner, inner_edge, edge, ahead, back, flat, below, above):
+def patch_two_steps(inner, inner_edge, edge, ahead, back, flat, far, near):
     up = lax.axis_index("gz") % 2 == 0
     place = lax.axis_index("gx")
     at_low = place == 0
@@ -310,16 +321,19 @@
             at = 8 * (first + 12 + side)
             flat[at : at + 8] = jnp.where(stale, sides[side][i], fresh)
     flat[8 * PER_SLOT * Q :] = jnp.full((FLAT_ROWS - 8 * PER_SLOT * Q, 128), SOLID, F32)
-    for group in range(NEAR):
-        above[group] = flat[pl.ds(64 * group + 5, 8, stride=8)]
-        below[group] = flat[pl.ds(64 * group + 2, 8, stride=8)]
-    for group in range(FAR):
-        above[NEAR + group] = flat[pl.ds(64 * group + 4, 8, stride=8)]
-        below[NEAR + group] = flat[pl.ds(8 * 5 * PER_SLOT + 64 * group + 3, 8, stride=8)]
+    for group in range(NEAR + FAR):
+        if group < NEAR:
+            to_low = flat[pl.ds(64 * group + 2, 8, stride=8)]
+            to_high = flat[pl.ds(64 * group + 5, 8, stride=8)]
+        else:
+            to_low = flat[pl.ds(8 * 5 * PER_SLOT + 64 * (group - NEAR) + 3, 8, stride=8)]
+            to_high = flat[pl.ds(64 * (group - NEAR) + 4, 8, stride=8)]
+        far[group] = jnp.where(up, to_low, to_high)
+        near[group] = jnp.where(up, to_high, to_low)
 
 
 def last_two_steps(
-    flat_in, below, above, block_fluid, out, block_density, flat, middle, turn, final, wet_count, sems
+    flat_in, far, near, block_fluid, out, block_density, flat, middle, turn, final, wet_count, sems
 ):
     count_copy = pltpu.make_async_copy(block_fluid, wet_count, sems.at[2])
     count_copy.start()
@@ -328,14 +342,16 @@
     at_high = place == lax.axis_size("gz") - 1
     lane = lanes()
     low_side = lane % 8 < 4
-    for group in range(NEAR):
-        flat[pl.ds(64 * group + 1, 8, stride=8)] = jnp.where(at_low, SOLID, below[group])
-        flat[pl.ds(64 * group + 6, 8, stride=8)] = jnp.where(at_high, SOLID, above[group])
-    for group in range(FAR):
-        flat[pl.ds(64 * group, 8, stride=8)] = jnp.where(at_low, SOLID, below[NEAR + group])
-        flat[pl.ds(8 * 5 * PER_SLOT + 64 * group + 7, 8, stride=8)] = jnp.where(
-            at_high, SOLID, above[NEAR + group]
-        )
+    even = lax.rem(place, 2) == 0
+    for group in range(NEAR + FAR):
+        below = jnp.where(at_low, SOLID, jnp.where(even, far[group], near[group]))
+        above = jnp.where(at_high, SOLID, jnp.where(even, near[group], far[group]))
+        if group < NEAR:
+            flat[pl.ds(64 * group + 1, 8, stride=8)] = below
+            flat[pl.ds(64 * group + 6, 8, stride=8)] = above
+        else:
+            flat[pl.ds(64 * (group - NEAR), 8, stride=8)] = below
+            flat[pl.ds(8 * 5 * PER_SLOT + 64 * (group - NEAR) + 7, 8, stride=8)] = above
 
     def joined(i, at):
         return flat[pl.ds(8 * (PER_SLOT * SLOT[i] + at), 8)]
@@ -386,11 +402,20 @@
         copy.wait()
 
 
-def ring_exchange(to_low, to_high, axis):
-    count = lax.axis_size(axis)
-    up = [(i, (i + 1) % count) for i in range(count)]
-    down = [(target, source) for source, target in up]
-    return lax.ppermute(to_high, axis, up), lax.ppermute(to_low, axis, down)
+def layer_exchange(far, near):
+    count = lax.axis_size("gz")
+    swap = [(i, i + 1 - 2 * (i % 2)) for i in range(count)]
+    cycle = []
+    for i in range(count):
+        if i % 2 == 0:
+            cycle.append((i, i + 2 if i + 2 < count else i + 1))
+        else:
+            cycle.append((i, i - 2 if i - 2 >= 0 else i - 1))
+    far = lax.ppermute(far, "gz", swap)
+    far, near = lax.optimization_barrier((far, near))
+    far = lax.ppermute(far, "gz", cycle)
+    near = lax.ppermute(near, "gz", swap)
+    return far, near
 
 
 def loop_exchange(ahead, back, axis):
@@ -428,7 +453,7 @@
 
 
 def on_device(relative, fluid, block_fluid, new_owner):
-    low, high, moved = call(
+    far, near, moved = call(
         split_slabs,
         [shape(Q + 1, 2, 8, 128), shape(Q + 1, 2, 8, 128), shape(2, 8, 128)],
         [HBM] * 3,
@@ -438,13 +463,13 @@
             pltpu.SemaphoreType.DMA((4,)),
         ],
     )(in_hbm(relative), in_hbm(fluid), in_hbm(new_owner.transpose(1, 2, 0).reshape(1, 2)))
-    below, above = ring_exchange(low, high, "gz")
+    got_far, got_near = layer_exchange(far, near)
     own, ahead, back = call(
         first_relax,
         [shape(Q, 8, 8, 128), shape(Y_TILES, 8, 128), shape(Y_TILES, 8, 128)],
         [VMEM] * 5,
         scratch=[pltpu.VMEM((Q + 1, 64, 128), F32), pltpu.VMEM((2, 512, 128), F32)],
-    )(high, low, above, below, moved)
+    )(far, near, got_far, got_near, moved)
     ahead, back = loop_exchange(ahead, back, "gy")
     main, edge, x_ahead, x_back = call(
         join_rows,
@@ -459,12 +484,12 @@
         [VMEM],
         scratch=[pltpu.VMEM((Q, 14, 8, 128), F32)],
     )(main)
-    flat, z_low, z_high = call(
+    flat, far, near = call(
         patch_two_steps,
         [shape(FLAT_ROWS, 128), shape(NEAR + FAR, 8, 128), shape(NEAR + FAR, 8, 128)],
         [VMEM] * 5,
     )(inner, inner_edge, edge, x_ahead, x_back)
-    below, above = ring_exchange(z_low, z_high, "gz")
+    far, near = layer_exchange(far, near)
     out, block_density, _ = call(
         last_two_steps,
         [shape(Q, 4, 8, 128), shape(1, 2), shape(FLAT_ROWS, 128)],
@@ -478,7 +503,7 @@
             pltpu.SemaphoreType.DMA((3,)),
         ],
         aliases={0: 2},
-    )(flat, below, above, in_hbm(block_fluid.transpose(1, 2, 0).reshape(1, 2)))
+    )(flat, far, near, in_hbm(block_fluid.transpose(1, 2, 0).reshape(1, 2)))
     return out, block_density.reshape(1, 1, 2).transpose(2, 0, 1)
 
 

time: 45.9 us -> 46 us (level)
  the two profiles are of different devices: /device:TPU:26 before, /device:TPU:1 now
where the time goes in v5:
time: 46 us; the launch traced here: 45.8 us
  starting transfers between devices  28 us (61%)
  waiting for transfers between devices  11 us (24%)
  Pallas kernels  6.05 us (13%)
  between operations  0.7 us (2%)
    ppermute x2, starting transfers between devices, layer_exchange(): far = lax.ppermute(far, 'gz', swap)  19.7 us
    ppermute x4, waiting for transfers between devices, loop_exchange(): return (lax.ppermute(ahead, axes, pairs), lax.ppermute(back, axes, inverse))  5.93 us
    ppermute x2, starting transfers between devices, layer_exchange(): near = lax.ppermute(near, 'gz', swap)  4.65 us
    ppermute x2, waiting for transfers between devices, layer_exchange(): far = lax.ppermute(far, 'gz', cycle)  3.07 us
    ppermute x4, starting transfers between devices, loop_exchange(): return (lax.ppermute(ahead, axes, pairs), lax.ppermute(back, axes, inverse))  2.94 us
    pallas_call x1, Pallas kernels, on_device(): call(last_two_steps, [shape(Q, 4, 8, 128), shape(1, 2), shape(FLAT_ROWS,...  2.06 us
    ppermute x2, waiting for transfers between devices, layer_exchange(): far = lax.ppermute(far, 'gz', swap)  2.03 us
    pallas_call x1, Pallas kernels, on_device(): call(two_steps, [shape(Q, 12, 8, 128), shape(Q, 8, 128)], [VMEM], scratch...  1.14 us
  transfers between devices with their start and end apart: 10, of which 6 were waited for; matrix products, arithmetic and copies ran while one was open for 0% of the time, Pallas kernels for 2%

profile of v5, /device:TPU:1, one launch (start us, length us, event | category | flops | bytes accessed | tf_op | source)
XLA Modules:
  0.0 45.8 jit_solution(8109702304843265897)
XLA Ops:
  0.6 1.0 %shard_map.59 = (f32[20,2,8,128]{3,2,1,0:T(8,128)S(1)}, f32[20,2,8,128]{3,2,1,0:T(8,128)S(1)}, f32[2,8,128]{2,1,0:T(8,128)S(1)}) custom-call(f32[19,4,8,128]{3,2,1,0:T(8,128)} %relative.1, s32[4,8,128]{2,1,0:T(8,128)} %fluid.1, s32[1,2]{1,0:T(1,128)} %bitcast.3), custom_call_target="tpu_custom_call" | custom-call | tf_op jit(solution)/shard_map/pallas_call | solution.py:456
  1.7 16.1 %collective-permute-start = (f32[20,2,8,128]{3,2,1,0:T(8,128)S(1)}, f32[20,2,8,128]{3,2,1,0:T(8,128)S(1)}, u32[]{:S(2)}, u32[]{:S(2)}) collective-permute-start(f32[20,2,8,128]{3,2,1,0:T(8,128)S(1)} %get-tuple-element.23.far), channel_id=1, source_target_pairs={{0,1},{1,0},{2,3},{3,2},{4,5},{5,4},{6,7},{7,6},{8,9},{9,8},{10,11... | collective-permute-start | bytes 491528 | tf_op jit(solution)/shard_map/ppermute | solution.py:414
  17.7 1.0 %collective-permute-done = f32[20,2,8,128]{3,2,1,0:T(8,128)S(1)} collective-permute-done((f32[20,2,8,128]{3,2,1,0:T(8,128)S(1)}, f32[20,2,8,128]{3,2,1,0:T(8,128)S(1)}, u32[]{:S(2)}, u32[]{:S(2)}) %collective-permute-start) | collective-permute-done | bytes 163872 | tf_op jit(solution)/shard_map/ppermute | solution.py:414
  18.8 0.4 collective-permute-start.1
  19.1 1.9 %collective-permute-start.2 = (f32[20,2,8,128]{3,2,1,0:T(8,128)S(1)}, f32[20,2,8,128]{3,2,1,0:T(8,128)S(1)}, u32[]{:S(2)}, u32[]{:S(2)}) collective-permute-start(f32[20,2,8,128]{3,2,1,0:T(8,128)S(1)} %get-tuple-element.26.near), channel_id=1, source_target_pairs={{0,1},{1,0},{2,3},{3,2},{4,5},{5,4},{6,7},{7,6},{8,9},{9,8},{10,11... | collective-permute-start | bytes 491528 | tf_op jit(solution)/shard_map/ppermute | solution.py:417
  21.0 1.9 %collective-permute-done.1.got_far = f32[20,2,8,128]{3,2,1,0:T(8,128)S(1)} collective-permute-done((f32[20,2,8,128]{3,2,1,0:T(8,128)S(1)}, f32[20,2,8,128]{3,2,1,0:T(8,128)S(1)}, u32[]{:S(2)}, u32[]{:S(2)}) %collective-permute-start.1) | collective-permute-done | bytes 163872 | tf_op jit(solution)/shard_map/ppermute | solution.py:416
  22.9 0.0 collective-permute-done.2.got_near
  22.9 0.5 %shard_map.60 = (f32[19,8,8,128]{3,2,1,0:T(8,128)S(1)}, f32[52,8,128]{2,1,0:T(8,128)S(1)}, f32[52,8,128]{2,1,0:T(8,128)S(1)}) custom-call(f32[20,2,8,128]{3,2,1,0:T(8,128)S(1)} %get-tuple-element.23.far, f32[20,2,8,128]{3,2,1,0:T(8,128)S(1)} %get-tuple-element.26.near, f32[20,2,8,128]{3,2,1,0:T(8,128)S(1)} %collective-permute-done.1.got_far, ...), custom_call_target="tpu_custom_call" | custom-call | tf_op jit(solution)/shard_map/pallas_call | solution.py:467
  23.4 0.0 collective-permute-start.3
  23.4 1.5 %collective-permute-start.4 = (f32[52,8,128]{2,1,0:T(8,128)S(1)}, f32[52,8,128]{2,1,0:T(8,128)S(1)}, u32[]{:S(2)}, u32[]{:S(2)}) collective-permute-start(f32[52,8,128]{2,1,0:T(8,128)S(1)} %get-tuple-element.30), channel_id=1, source_target_pairs={{32,0},{0,1},{34,2},{2,3},{36,4},{4,5},{38,6},{6,7},{40,8},{8,9},{... | collective-permute-start | bytes 638984 | tf_op jit(solution)/shard_map/ppermute | solution.py:434
  24.9 5.7 %collective-permute-done.3.ahead = f32[52,8,128]{2,1,0:T(8,128)S(1)} collective-permute-done((f32[52,8,128]{2,1,0:T(8,128)S(1)}, f32[52,8,128]{2,1,0:T(8,128)S(1)}, u32[]{:S(2)}, u32[]{:S(2)}) %collective-permute-start.3) | collective-permute-done | bytes 213024 | tf_op jit(solution)/shard_map/ppermute | solution.py:434
  30.6 0.0 collective-permute-done.4.back
  30.6 0.6 %shard_map.61 = (f32[19,16,8,128]{3,2,1,0:T(8,128)S(1)}, f32[19,8,128]{2,1,0:T(8,128)S(1)}, f32[10,8,128]{2,1,0:T(8,128)S(1)}, f32[10,8,128]{2,1,0:T(8,128)S(1)}) custom-call(f32[19,8,8,128]{3,2,1,0:T(8,128)S(1)} %get-tuple-element.28.own, f32[52,8,128]{2,1,0:T(8,128)S(1)} %collective-permute-done.3.ahead, f32[52,8,128]{2,1,0:T(8,128)S(1)} %collective-permute-done.4.back), custom_call_target="tpu_custom_call" | custom-call | tf_op jit(solution)/shard_map/pallas_call | solution.py:474
  31.2 0.5 %collective-permute-start.5 = (f32[10,8,128]{2,1,0:T(8,128)S(1)}, f32[10,8,128]{2,1,0:T(8,128)S(1)}, u32[]{:S(2)}, u32[]{:S(2)}) collective-permute-start(f32[10,8,128]{2,1,0:T(8,128)S(1)} %get-tuple-element.35), channel_id=1, source_target_pairs={{0,128},{1,0},{2,130},{3,2},{4,132},{5,4},{6,134},{7,6},{8,136},{9... | collective-permute-start | bytes 122888 | tf_op jit(solution)/shard_map/ppermute | solution.py:434
  31.7 1.0 %collective-permute-start.6 = (f32[10,8,128]{2,1,0:T(8,128)S(1)}, f32[10,8,128]{2,1,0:T(8,128)S(1)}, u32[]{:S(2)}, u32[]{:S(2)}) collective-permute-start(f32[10,8,128]{2,1,0:T(8,128)S(1)} %get-tuple-element.36), channel_id=1, source_target_pairs={{128,0},{0,1},{130,2},{2,3},{132,4},{4,5},{134,6},{6,7},{136,8},{8... | collective-permute-start | bytes 122888 | tf_op jit(solution)/shard_map/ppermute | solution.py:434
  32.7 1.1 %shard_map.62 = (f32[19,12,8,128]{3,2,1,0:T(8,128)S(1)}, f32[19,8,128]{2,1,0:T(8,128)S(1)}) custom-call(f32[19,16,8,128]{3,2,1,0:T(8,128)S(1)} %get-tuple-element.31.main), custom_call_target="tpu_custom_call" | custom-call | tf_op jit(solution)/shard_map/pallas_call | solution.py:481
  33.8 0.2 collective-permute-done.5.ahead
  34.0 0.0 collective-permute-done.6.back
  34.0 0.7 %shard_map.63 = (f32[2176,128]{1,0:T(8,128)S(1)}, f32[43,8,128]{2,1,0:T(8,128)S(1)}, f32[43,8,128]{2,1,0:T(8,128)S(1)}) custom-call(f32[19,12,8,128]{3,2,1,0:T(8,128)S(1)} %get-tuple-element.32.inner, f32[19,8,128]{2,1,0:T(8,128)S(1)} %get-tuple-element.33.inner_edge, f32[19,8,128]{2,1,0:T(8,128)S(1)} %get-tuple-element.34.edge, ...), custom_call_target="tpu_custom_call" | custom-call | tf_op jit(solution)/shard_map/pallas_call | solution.py:487
  34.8 3.6 %collective-permute-start.7 = (f32[43,8,128]{2,1,0:T(8,128)S(1)}, f32[43,8,128]{2,1,0:T(8,128)S(1)}, u32[]{:S(2)}, u32[]{:S(2)}) collective-permute-start(f32[43,8,128]{2,1,0:T(8,128)S(1)} %get-tuple-element.38), channel_id=1, source_target_pairs={{0,1},{1,0},{2,3},{3,2},{4,5},{5,4},{6,7},{7,6},{8,9},{9,8},{10,11... | collective-permute-start | bytes 528392 | tf_op jit(solution)/shard_map/ppermute | solution.py:414
  38.4 1.0 %collective-permute-done.7 = f32[43,8,128]{2,1,0:T(8,128)S(1)} collective-permute-done((f32[43,8,128]{2,1,0:T(8,128)S(1)}, f32[43,8,128]{2,1,0:T(8,128)S(1)}, u32[]{:S(2)}, u32[]{:S(2)}) %collective-permute-start.7) | collective-permute-done | bytes 176160 | tf_op jit(solution)/shard_map/ppermute | solution.py:414
  39.4 0.4 collective-permute-start.8
  39.8 2.7 %collective-permute-start.9 = (f32[43,8,128]{2,1,0:T(8,128)S(1)}, f32[43,8,128]{2,1,0:T(8,128)S(1)}, u32[]{:S(2)}, u32[]{:S(2)}) collective-permute-start(f32[43,8,128]{2,1,0:T(8,128)S(1)} %get-tuple-element.41), channel_id=1, source_target_pairs={{0,1},{1,0},{2,3},{3,2},{4,5},{5,4},{6,7},{7,6},{8,9},{9,8},{10,11... | collective-permute-start | bytes 528392 | tf_op jit(solution)/shard_map/ppermute | solution.py:417
  42.5 1.2 %collective-permute-done.8.far = f32[43,8,128]{2,1,0:T(8,128)S(1)} collective-permute-done((f32[43,8,128]{2,1,0:T(8,128)S(1)}, f32[43,8,128]{2,1,0:T(8,128)S(1)}, u32[]{:S(2)}, u32[]{:S(2)}) %collective-permute-start.8) | collective-permute-done | bytes 176160 | tf_op jit(solution)/shard_map/ppermute | solution.py:416
  43.7 0.0 collective-permute-done.9.near
  43.7 2.1 %shard_map.64 = (f32[19,4,8,128]{3,2,1,0:T(8,128)}, f32[1,2]{1,0:T(1,128)}, f32[2176,128]{1,0:T(8,128)S(1)}) custom-call(f32[2176,128]{1,0:T(8,128)S(1)} %get-tuple-element.37.flat_in, f32[43,8,128]{2,1,0:T(8,128)S(1)} %collective-permute-done.8.far, f32[43,8,128]{2,1,0:T(8,128)S(1)} %collective-permute-done.9.near, ...), custom_call_target="tpu_custom_call", output_to_operand_aliasing={{2}: (0, {})} | custom-call | tf_op jit(solution)/shard_map/pallas_call | solution.py:493
Async XLA Ops:
  1.7 17.1 %collective-permute-start = (f32[20,2,8,128]{3,2,1,0:T(8,128)S(1)}, f32[20,2,8,128]{3,2,1,0:T(8,128)S(1)}, u32[]{:S(2)}, u32[]{:S(2)}) collective-permute-start(f32[20,2,8,128]{3,2,1,0:T(8,128)S(1)} %get-tuple-element.23.far), channel_id=1, source_target_pairs={{0,1},{1,0},{2,3},{3,2},{4,5},{5,4},{6,7},{7,6},{8,9},{9,8},{10,11... | collective-permute-start | bytes 491528 | tf_op jit(solution)/shard_map/ppermute | solution.py:414
  18.8 4.2 %collective-permute-start.1 = (f32[20,2,8,128]{3,2,1,0:T(8,128)S(1)}, f32[20,2,8,128]{3,2,1,0:T(8,128)S(1)}, u32[]{:S(2)}, u32[]{:S(2)}) collective-permute-start(f32[20,2,8,128]{3,2,1,0:T(8,128)S(1)} %collective-permute-done), channel_id=1, source_target_pairs={{0,2},{1,0},{2,4},{3,1},{4,6},{5,3},{6,8},{7,5},{8,10},{9,7},{10,1... | collective-permute-start | bytes 491528 | tf_op jit(solution)/shard_map/ppermute | solution.py:416
  19.1 3.8 %collective-permute-start.2 = (f32[20,2,8,128]{3,2,1,0:T(8,128)S(1)}, f32[20,2,8,128]{3,2,1,0:T(8,128)S(1)}, u32[]{:S(2)}, u32[]{:S(2)}) collective-permute-start(f32[20,2,8,128]{3,2,1,0:T(8,128)S(1)} %get-tuple-element.26.near), channel_id=1, source_target_pairs={{0,1},{1,0},{2,3},{3,2},{4,5},{5,4},{6,7},{7,6},{8,9},{9,8},{10,11... | collective-permute-start | bytes 491528 | tf_op jit(solution)/shard_map/ppermute | solution.py:417
  23.4 7.2 %collective-permute-start.3 = (f32[52,8,128]{2,1,0:T(8,128)S(1)}, f32[52,8,128]{2,1,0:T(8,128)S(1)}, u32[]{:S(2)}, u32[]{:S(2)}) collective-permute-start(f32[52,8,128]{2,1,0:T(8,128)S(1)} %get-tuple-element.29), channel_id=1, source_target_pairs={{0,32},{1,0},{2,34},{3,2},{4,36},{5,4},{6,38},{7,6},{8,40},{9,8},{... | collective-permute-start | bytes 638984 | tf_op jit(solution)/shard_map/ppermute | solution.py:434
  23.4 7.1 %collective-permute-start.4 = (f32[52,8,128]{2,1,0:T(8,128)S(1)}, f32[52,8,128]{2,1,0:T(8,128)S(1)}, u32[]{:S(2)}, u32[]{:S(2)}) collective-permute-start(f32[52,8,128]{2,1,0:T(8,128)S(1)} %get-tuple-element.30), channel_id=1, source_target_pairs={{32,0},{0,1},{34,2},{2,3},{36,4},{4,5},{38,6},{6,7},{40,8},{8,9},{... | collective-permute-start | bytes 638984 | tf_op jit(solution)/shard_map/ppermute | solution.py:434
  31.2 2.9 %collective-permute-start.5 = (f32[10,8,128]{2,1,0:T(8,128)S(1)}, f32[10,8,128]{2,1,0:T(8,128)S(1)}, u32[]{:S(2)}, u32[]{:S(2)}) collective-permute-start(f32[10,8,128]{2,1,0:T(8,128)S(1)} %get-tuple-element.35), channel_id=1, source_target_pairs={{0,128},{1,0},{2,130},{3,2},{4,132},{5,4},{6,134},{7,6},{8,136},{9... | collective-permute-start | bytes 122888 | tf_op jit(solution)/shard_map/ppermute | solution.py:434
  31.7 2.3 %collective-permute-start.6 = (f32[10,8,128]{2,1,0:T(8,128)S(1)}, f32[10,8,128]{2,1,0:T(8,128)S(1)}, u32[]{:S(2)}, u32[]{:S(2)}) collective-permute-start(f32[10,8,128]{2,1,0:T(8,128)S(1)} %get-tuple-element.36), channel_id=1, source_target_pairs={{128,0},{0,1},{130,2},{2,3},{132,4},{4,5},{134,6},{6,7},{136,8},{8... | collective-permute-start | bytes 122888 | tf_op jit(solution)/shard_map/ppermute | solution.py:434
  34.8 4.6 %collective-permute-start.7 = (f32[43,8,128]{2,1,0:T(8,128)S(1)}, f32[43,8,128]{2,1,0:T(8,128)S(1)}, u32[]{:S(2)}, u32[]{:S(2)}) collective-permute-start(f32[43,8,128]{2,1,0:T(8,128)S(1)} %get-tuple-element.38), channel_id=1, source_target_pairs={{0,1},{1,0},{2,3},{3,2},{4,5},{5,4},{6,7},{7,6},{8,9},{9,8},{10,11... | collective-permute-start | bytes 528392 | tf_op jit(solution)/shard_map/ppermute | solution.py:414
  39.4 4.3 %collective-permute-start.8 = (f32[43,8,128]{2,1,0:T(8,128)S(1)}, f32[43,8,128]{2,1,0:T(8,128)S(1)}, u32[]{:S(2)}, u32[]{:S(2)}) collective-permute-start(f32[43,8,128]{2,1,0:T(8,128)S(1)} %collective-permute-done.7), channel_id=1, source_target_pairs={{0,2},{1,0},{2,4},{3,1},{4,6},{5,3},{6,8},{7,5},{8,10},{9,7},{10,1... | collective-permute-start | bytes 528392 | tf_op jit(solution)/shard_map/ppermute | solution.py:416
  39.8 3.9 %collective-permute-start.9 = (f32[43,8,128]{2,1,0:T(8,128)S(1)}, f32[43,8,128]{2,1,0:T(8,128)S(1)}, u32[]{:S(2)}, u32[]{:S(2)}) collective-permute-start(f32[43,8,128]{2,1,0:T(8,128)S(1)} %get-tuple-element.41), channel_id=1, source_target_pairs={{0,1},{1,0},{2,3},{3,2},{4,5},{5,4},{6,7},{7,6},{8,9},{9,8},{10,11... | collective-permute-start | bytes 528392 | tf_op jit(solution)/shard_map/ppermute | solution.py:417

commit v6 on v4

--- a/solution.py
+++ b/solution.py
@@ -39,10 +39,8 @@
 Y_FIRST = [3 * s + min(s // 5, 2) for s in SLOT]
 Y_FAR = [15, 31, 59, 60, 61]
 Y_TILES = 52
-PER_SLOT = 14
-NEAR = 34
-FAR = 9
-FLAT_ROWS = 8 * 8 * NEAR
+MAIN = (12, 29, 8)
+PATCH = (4, 10, 3)
 F32 = jnp.float32
 VMEM = pl.BlockSpec(memory_space=pltpu.VMEM)
 SMEM = pl.BlockSpec(memory_space=pltpu.SMEM)
@@ -126,19 +124,60 @@
 
 
 def stream_patch(values):
+    lane = lanes()
     out = [values[0]]
     for i in range(1, Q):
         step_z, step_y, step_x = VELOCITIES[i]
-        source = roll(values[i], step_z, 8 * step_y + step_x)
-        out.append(jnp.where(source == SOLID, values[OPPOSITE[i]], source))
+        low, high = (roll(value, step_z, 16 * step_y + step_x) for value in values[i])
+        if step_y == 1:
+            high = jnp.where(lane < 16, low, high)
+        elif step_y == -1:
+            low = jnp.where(lane >= 112, high, low)
+        bounce = values[OPPOSITE[i]]
+        out.append(
+            (jnp.where(low == SOLID, bounce[0], low), jnp.where(high == SOLID, bounce[1], high))
+        )
     return out
 
 
-def gather_columns(values, rows):
-    lane_row = lanes() // 8
-    tile = jnp.full((8, 128), SOLID, F32)
-    for row, value in zip(rows, values):
-        tile = jnp.where(lane_row == row, roll(value, 0, 8 * row + 4), tile)
+def relax_patch(values):
+    halves = []
+    streamed = stream_patch(values)
+    for half in range(2):
+        wet = values[0][half] != SOLID
+        halves.append(relax_wet([value[half] for value in streamed], wet))
+    return list(zip(*halves))
+
+
+def layers_to_send(flat, sizes, low, high):
+    tiles, near, far = sizes
+    for group in range(near):
+        high[group] = flat[pl.ds(64 * group + 5, 8, stride=8)]
+        low[group] = flat[pl.ds(64 * group + 2, 8, stride=8)]
+    for group in range(far):
+        high[near + group] = flat[pl.ds(64 * group + 4, 8, stride=8)]
+        low[near + group] = flat[pl.ds(8 * 5 * tiles + 64 * group + 3, 8, stride=8)]
+
+
+def layers_to_place(flat, sizes, below, above):
+    tiles, near, far = sizes
+    place = lax.axis_index("gz")
+    at_low = place == 0
+    at_high = place == lax.axis_size("gz") - 1
+    for group in range(near):
+        flat[pl.ds(64 * group + 1, 8, stride=8)] = jnp.where(at_low, SOLID, below[group])
+        flat[pl.ds(64 * group + 6, 8, stride=8)] = jnp.where(at_high, SOLID, above[group])
+    for group in range(far):
+        flat[pl.ds(64 * group, 8, stride=8)] = jnp.where(at_low, SOLID, below[near + group])
+        first = 8 * 5 * tiles + 64 * group + 7
+        flat[pl.ds(first, 8, stride=8)] = jnp.where(at_high, SOLID, above[near + group])
+
+
+def gather_columns(values):
+    lane_row = lanes() // 16
+    tile = roll(values[0], 0, 8)
+    for row in range(1, 8):
+        tile = jnp.where(lane_row == row, roll(values[row], 0, 16 * row + 8), tile)
     return tile
 
 
@@ -163,7 +202,7 @@
     copies[2].wait()
 
 
-def first_relax(high, low, above, below, moved, own, ahead, back, turn, stage):
+def first_relax(low, high, below, above, moved, own, ahead, back, turn, stage):
     place = lax.axis_index("gz")
     at_low = place == 0
     at_high = place == lax.axis_size("gz") - 1
@@ -240,127 +279,101 @@
         for k in range(8):
             main[i, 4 + k] = rows[k]
         rows = [main[i, k] for k in range(4)] + rows + [main[i, k] for k in range(12, 16)]
-        edges.append(gather_columns(rows, range(16)))
-        edge[i] = edges[i]
-    low_side = lanes() % 8 < 4
-    for i in range(10):
-        if i + 10 < Q:
-            to_low = jnp.where(low_side, roll(edges[i + 10], 0, -4), edges[i])
-            to_high = jnp.where(low_side, edges[i], roll(edges[i + 10], 0, 4))
-            x_ahead[i] = jnp.where(up, to_high, to_low)
-            x_back[i] = jnp.where(up, to_low, to_high)
-        else:
-            x_ahead[i] = edges[i]
-            x_back[i] = edges[i]
-
-
-def two_steps(main, out, edge, middle):
-    def first(row):
+        for half in range(2):
+            edges.append(gather_columns(rows[8 * half : 8 * half + 8]))
+            edge[i, half] = edges[-1]
+    part = lanes() % 16 // 4
+    for group in range(10):
+        to_low = jnp.full((8, 128), SOLID, F32)
+        to_high = to_low
+        for k, tile in enumerate(edges[4 * group : 4 * group + 4]):
+            to_low = jnp.where(part == k, roll(tile, 0, 4 * (k - 2)), to_low)
+            to_high = jnp.where(part == k, roll(tile, 0, 4 * (k - 1)), to_high)
+        x_ahead[group] = jnp.where(up, to_high, to_low)
+        x_back[group] = jnp.where(up, to_low, to_high)
+
+
+def two_steps(main, flat, z_low, z_high, middle):
+    for row in range(1, 15):
         values = relax_row(lambda i, at: main[i, at], row)
         for i in range(Q):
             middle[i, row - 1] = values[i]
-
-    def second(row):
+    for row in range(2, 14):
         values = relax_row(lambda i, at: middle[i, at], row - 1)
         for i in range(Q):
-            out[i, row - 2] = values[i]
-
-    for row in range(1, 15):
-        first(row)
-    for row in range(2, 14):
-        second(row)
-    for i in range(Q):
-        edge[i] = gather_columns([out[i, k] for k in range(12)], range(2, 14))
-
-
-def patch_two_steps(inner, inner_edge, edge, ahead, back, flat, below, above):
+            at = 8 * (12 * SLOT[i] + row - 2)
+            flat[at : at + 8] = values[i]
+    flat[8 * 12 * Q :] = jnp.full((32, 128), SOLID, F32)
+    layers_to_send(flat, MAIN, z_low, z_high)
+
+
+def patch_two_steps(edge, ahead, back, flat, z_low, z_high):
     up = lax.axis_index("gz") % 2 == 0
     place = lax.axis_index("gx")
-    at_low = place == 0
-    at_high = place == lax.axis_size("gx") - 1
-    column = lanes() % 8
-    low_side = column < 4
-    sides = []
+    outside = (place == 0, place == lax.axis_size("gx") - 1)
+    own_part = (lanes() % 16 >= 8, lanes() % 16 < 8)
     for side in range(2):
         values = []
         for i in range(Q):
-            message = jnp.where(up == (side == 0), ahead[i % 10], back[i % 10])
-            if i >= 10:
-                message = roll(message, 0, (-4, 4)[side])
-            message = jnp.where((at_low, at_high)[side], SOLID, message)
-            if side == 0:
-                values.append(jnp.where(low_side, message, edge[i]))
-            else:
-                values.append(jnp.where(low_side, edge[i], message))
-        for step in range(2):
-            wet = values[0] != SOLID
-            values = relax_wet(stream_patch(values), wet)
-        sides.append(values)
-    lane = lanes()
-    seam = (lane < 2) | (lane >= 126)
-    for i in range(Q):
-        own_columns = jnp.where(low_side, sides[1][i], sides[0][i])
-        first = PER_SLOT * SLOT[i]
-        for row in range(12):
-            value = jnp.where(seam, roll(own_columns, 0, -(8 * (row + 2) + 4)), inner[i, row])
-            flat[8 * (first + row) : 8 * (first + row) + 8] = value
-        fresh = inner_edge[i]
-        for side in range(2):
-            stale = (column < 6) if side == 0 else (column >= 2)
-            at = 8 * (first + 12 + side)
-            flat[at : at + 8] = jnp.where(stale, sides[side][i], fresh)
-    flat[8 * PER_SLOT * Q :] = jnp.full((FLAT_ROWS - 8 * PER_SLOT * Q, 128), SOLID, F32)
-    for group in range(NEAR):
-        above[group] = flat[pl.ds(64 * group + 5, 8, stride=8)]
-        below[group] = flat[pl.ds(64 * group + 2, 8, stride=8)]
-    for group in range(FAR):
-        above[NEAR + group] = flat[pl.ds(64 * group + 4, 8, stride=8)]
-        below[NEAR + group] = flat[pl.ds(8 * 5 * PER_SLOT + 64 * group + 3, 8, stride=8)]
-
-
-def last_two_steps(
-    flat_in, below, above, block_fluid, out, block_density, flat, middle, turn, final, wet_count, sems
+            tiles = []
+            for half in range(2):
+                group, k = divmod(2 * i + half, 4)
+                message = jnp.where(up == (side == 0), ahead[group], back[group])
+                message = roll(message, 0, -4 * (k - 1 - side))
+                message = jnp.where(outside[side], SOLID, message)
+                tiles.append(jnp.where(own_part[side], edge[i, half], message))
+            values.append(tiles)
+        values = relax_patch(relax_patch(values))
+        for i in range(Q):
+            for half in range(2):
+                at = 8 * (4 * SLOT[i] + 2 * side + half)
+                flat[at : at + 8] = values[i][half]
+    flat[8 * 4 * Q :] = jnp.full((32, 128), SOLID, F32)
+    layers_to_send(flat, PATCH, z_low, z_high)
+
+
+def last_two_steps(flat_in, below, above, out, flat, middle):
+    layers_to_place(flat, MAIN, below, above)
+
+    def joined(i, at):
+        return flat[pl.ds(8 * (12 * SLOT[i] + at), 8)]
+
+    for row in range(3, 13):
+        values = relax_row(joined, row - 2)
+        for i in range(Q):
+            middle[i, row - 3] = values[i]
+    for row in range(8):
+        wet = middle[0, row + 1] != SOLID
+        values = stream_row(lambda i, at: middle[i, at], row + 1)
+        for i in range(Q):
+            out[i, row] = jnp.where(wet, values[i], 0.0)
+
+
+def patch_last_two_steps(
+    flat_in, below, above, inner, block_fluid, out, block_density, flat, turn, final, wet_count, sems
 ):
     count_copy = pltpu.make_async_copy(block_fluid, wet_count, sems.at[2])
     count_copy.start()
-    place = lax.axis_index("gz")
-    at_low = place == 0
-    at_high = place == lax.axis_size("gz") - 1
-    lane = lanes()
-    low_side = lane % 8 < 4
-    for group in range(NEAR):
-        flat[pl.ds(64 * group + 1, 8, stride=8)] = jnp.where(at_low, SOLID, below[group])
-        flat[pl.ds(64 * group + 6, 8, stride=8)] = jnp.where(at_high, SOLID, above[group])
-    for group in range(FAR):
-        flat[pl.ds(64 * group, 8, stride=8)] = jnp.where(at_low, SOLID, below[NEAR + group])
-        flat[pl.ds(8 * 5 * PER_SLOT + 64 * group + 7, 8, stride=8)] = jnp.where(
-            at_high, SOLID, above[NEAR + group]
-        )
-
-    def joined(i, at):
-        return flat[pl.ds(8 * (PER_SLOT * SLOT[i] + at), 8)]
-
-    def third(row):
-        values = relax_row(joined, row - 2)
-        for i in range(Q):
-            middle[i, row - 3] = values[i]
-
-    for row in range(3, 13):
-        third(row)
+    layers_to_place(flat, PATCH, below, above)
     patches = []
     for side in range(2):
-        values = [joined(i, 12 + side) for i in range(Q)]
-        wet = values[0] != SOLID
-        values = relax_wet(stream_patch(values), wet)
-        patches.append(stream_patch(values))
-    own_columns = [jnp.where(low_side, patches[1][i], patches[0][i]) for i in range(Q)]
-    seam = (lane < 2) | (lane >= 126)
-    for row in range(8):
-        wet = middle[0, row + 1] != SOLID
-        values = stream_row(lambda i, at: middle[i, at], row + 1)
-        for i in range(Q):
-            value = jnp.where(seam, roll(own_columns[i], 0, -(8 * (row + 4) + 4)), values[i])
-            turn[i, 8 * row : 8 * row + 8] = jnp.where(wet, value, 0.0)
+        values = []
+        for i in range(Q):
+            at = 8 * (4 * SLOT[i] + 2 * side)
+            values.append((flat[at : at + 8], flat[at + 8 : at + 16]))
+        values = relax_patch(values)
+        wet = [value != SOLID for value in values[0]]
+        values = stream_patch(values)
+        patches.append([[jnp.where(wet[half], v[half], 0.0) for half in range(2)] for v in values])
+    lane = lanes()
+    seam = (lane < 4) | (lane >= 124)
+    low_part = lane % 16 < 8
+    for i in range(Q):
+        columns = [jnp.where(low_part, patches[1][i][half], patches[0][i][half]) for half in range(2)]
+        for row in range(8):
+            half, at = divmod(row + 4, 8)
+            value = jnp.where(seam, roll(columns[half], 0, -(16 * at + 8)), inner[i, row])
+            turn[i, 8 * row : 8 * row + 8] = value
     copies = []
     masses = []
     for slot in range(2):
@@ -409,7 +422,7 @@
     return lax.ppermute(ahead, axes, pairs), lax.ppermute(back, axes, inverse)
 
 
-def call(kernel, outs, in_specs, out_specs=None, scratch=(), aliases=None, vmem=32):
+def call(kernel, outs, in_specs, out_specs=None, scratch=(), aliases=None):
     if out_specs is None:
         out_specs = [VMEM] * len(outs)
     return pl.pallas_call(
@@ -419,7 +432,7 @@
         out_specs=out_specs,
         scratch_shapes=list(scratch),
         input_output_aliases=aliases or {},
-        compiler_params=pltpu.CompilerParams(vmem_limit_bytes=vmem * 1024 * 1024),
+        compiler_params=pltpu.CompilerParams(vmem_limit_bytes=32 * 1024 * 1024),
     )
 
 
@@ -444,41 +457,48 @@
         [shape(Q, 8, 8, 128), shape(Y_TILES, 8, 128), shape(Y_TILES, 8, 128)],
         [VMEM] * 5,
         scratch=[pltpu.VMEM((Q + 1, 64, 128), F32), pltpu.VMEM((2, 512, 128), F32)],
-    )(high, low, above, below, moved)
+    )(low, high, below, above, moved)
     ahead, back = loop_exchange(ahead, back, "gy")
     main, edge, x_ahead, x_back = call(
         join_rows,
-        [shape(Q, 16, 8, 128), shape(Q, 8, 128), shape(10, 8, 128), shape(10, 8, 128)],
+        [shape(Q, 16, 8, 128), shape(Q, 2, 8, 128), shape(10, 8, 128), shape(10, 8, 128)],
         [VMEM] * 3,
         scratch=[pltpu.VMEM((2, 512, 128), F32)],
     )(own, ahead, back)
     x_ahead, x_back = loop_exchange(x_ahead, x_back, "gx")
-    inner, inner_edge = call(
+    flat, z_low, z_high = call(
         two_steps,
-        [shape(Q, 12, 8, 128), shape(Q, 8, 128)],
+        [shape(64 * MAIN[1], 128)] + [shape(sum(MAIN[1:]), 8, 128)] * 2,
         [VMEM],
         scratch=[pltpu.VMEM((Q, 14, 8, 128), F32)],
     )(main)
-    flat, z_low, z_high = call(
+    below, above = ring_exchange(z_low, z_high, "gz")
+    patch, z_low, z_high = call(
         patch_two_steps,
-        [shape(FLAT_ROWS, 128), shape(NEAR + FAR, 8, 128), shape(NEAR + FAR, 8, 128)],
-        [VMEM] * 5,
-    )(inner, inner_edge, edge, x_ahead, x_back)
-    below, above = ring_exchange(z_low, z_high, "gz")
+        [shape(64 * PATCH[1], 128)] + [shape(sum(PATCH[1:]), 8, 128)] * 2,
+        [VMEM] * 3,
+    )(edge, x_ahead, x_back)
+    patch_below, patch_above = ring_exchange(z_low, z_high, "gz")
+    inner, _ = call(
+        last_two_steps,
+        [shape(Q, 8, 8, 128), shape(64 * MAIN[1], 128)],
+        [VMEM] * 3,
+        scratch=[pltpu.VMEM((Q, 10, 8, 128), F32)],
+        aliases={0: 1},
+    )(flat, below, above)
     out, block_density, _ = call(
-        last_two_steps,
-        [shape(Q, 4, 8, 128), shape(1, 2), shape(FLAT_ROWS, 128)],
-        [VMEM] * 3 + [HBM],
+        patch_last_two_steps,
+        [shape(Q, 4, 8, 128), shape(1, 2), shape(64 * PATCH[1], 128)],
+        [VMEM] * 4 + [HBM],
         [HBM, SMEM, VMEM],
         scratch=[
-            pltpu.VMEM((Q, 10, 8, 128), F32),
             pltpu.VMEM((Q, 64, 128), F32),
             pltpu.VMEM((Q, 4, 8, 128), F32),
             pltpu.SMEM((1, 2), jnp.int32),
             pltpu.SemaphoreType.DMA((3,)),
         ],
         aliases={0: 2},
-    )(flat, below, above, in_hbm(block_fluid.transpose(1, 2, 0).reshape(1, 2)))
+    )(patch, patch_below, patch_above, inner, in_hbm(block_fluid.transpose(1, 2, 0).reshape(1, 2)))
     return out, block_density.reshape(1, 1, 2).transpose(2, 0, 1)
 
 

time: 45.9 us -> 48.1 us (1.048)
  starting transfers between devices: 23.6 us -> 26.5 us
  waiting for transfers between devices: 15.5 us -> 14.8 us
    ppermute x4 -> x6, starting transfers between devices: 18.7 us -> 21.7 us  [ring_exchange(): return (lax.ppermute(to_high, axis, up), lax.ppermute(to_low, axis, down))]
    ppermute x4 -> x6, waiting for transfers between devices: 6.11 us -> 4.27 us  [ring_exchange(): return (lax.ppermute(to_high, axis, up), lax.ppermute(to_low, axis, down))]
    ppermute x4, waiting for transfers between devices: 9.37 us -> 10.5 us  [loop_exchange(): return (lax.ppermute(ahead, axes, pairs), lax.ppermute(back, axes, inverse))]
    pallas_call x4 -> x5, Pallas kernels: 4.52 us -> 4.39 us  [the longest x1 1.8 us: on_device(): call(patch_last_two_steps, [shape(Q, 4, 8, 128), shape(1, 2), shape(64 *...]
  transfers between devices with their start and end apart: 8 -> 10, of which waited for: 6 -> 6; matrix products, arithmetic and copies ran while one was open for 0% -> 0% of each run, Pallas kernels for 2% -> 2%
where the time goes in v6:
time: 48.1 us; the launch traced here: 47.9 us
  starting transfers between devices  26.5 us (55%)
  waiting for transfers between devices  14.8 us (31%)
  Pallas kernels  5.9 us (12%)
  between operations  0.7 us (1%)
    ppermute x6, starting transfers between devices, ring_exchange(): return (lax.ppermute(to_high, axis, up), lax.ppermute(to_low, axis, down))  21.7 us
    ppermute x4, waiting for transfers between devices, loop_exchange(): return (lax.ppermute(ahead, axes, pairs), lax.ppermute(back, axes, inverse))  10.5 us
    ppermute x4, starting transfers between devices, loop_exchange(): return (lax.ppermute(ahead, axes, pairs), lax.ppermute(back, axes, inverse))  4.83 us
    ppermute x6, waiting for transfers between devices, ring_exchange(): return (lax.ppermute(to_high, axis, up), lax.ppermute(to_low, axis, down))  4.27 us
    pallas_call x1, Pallas kernels, on_device(): call(patch_last_two_steps, [shape(Q, 4, 8, 128), shape(1, 2), shape(64 *...  1.8 us
    pallas_call x1, Pallas kernels, on_device(): call(split_slabs, [shape(Q + 1, 2, 8, 128), shape(Q + 1, 2, 8, 128), shap...  1.04 us
  transfers between devices with their start and end apart: 10, of which 6 were waited for; matrix products, arithmetic and copies ran while one was open for 0% of the time, Pallas kernels for 2%

profile of v6, /device:TPU:26, one launch (start us, length us, event | category | flops | bytes accessed | tf_op | source)
XLA Modules:
  0.0 47.9 jit_solution(5797129176477454568)
XLA Ops:
  0.6 1.0 %shard_map.59 = (f32[20,2,8,128]{3,2,1,0:T(8,128)S(1)}, f32[20,2,8,128]{3,2,1,0:T(8,128)S(1)}, f32[2,8,128]{2,1,0:T(8,128)S(1)}) custom-call(f32[19,4,8,128]{3,2,1,0:T(8,128)} %relative.1, s32[4,8,128]{2,1,0:T(8,128)} %fluid.1, s32[1,2]{1,0:T(1,128)} %bitcast.3), custom_call_target="tpu_custom_call" | custom-call | tf_op jit(solution)/shard_map/pallas_call | solution.py:444
  1.7 0.0 collective-permute-start
  1.7 15.8 %collective-permute-start.1 = (f32[20,2,8,128]{3,2,1,0:T(8,128)S(1)}, f32[20,2,8,128]{3,2,1,0:T(8,128)S(1)}, u32[]{:S(2)}, u32[]{:S(2)}) collective-permute-start(f32[20,2,8,128]{3,2,1,0:T(8,128)S(1)} %get-tuple-element.21.low), channel_id=1, source_target_pairs={{1,0},{2,1},{3,2},{4,3},{5,4},{6,5},{7,6},{8,7},{9,8},{10,9},{11,1... | collective-permute-start | bytes 491528 | tf_op jit(solution)/shard_map/ppermute | solution.py:406
  17.5 3.0 %collective-permute-done.below = f32[20,2,8,128]{3,2,1,0:T(8,128)S(1)} collective-permute-done((f32[20,2,8,128]{3,2,1,0:T(8,128)S(1)}, f32[20,2,8,128]{3,2,1,0:T(8,128)S(1)}, u32[]{:S(2)}, u32[]{:S(2)}) %collective-permute-start) | collective-permute-done | bytes 163872 | tf_op jit(solution)/shard_map/ppermute | solution.py:406
  20.5 0.0 collective-permute-done.1.above
  20.5 0.5 shard_map.60
  20.9 1.5 %collective-permute-start.2 = (f32[52,8,128]{2,1,0:T(8,128)S(1)}, f32[52,8,128]{2,1,0:T(8,128)S(1)}, u32[]{:S(2)}, u32[]{:S(2)}) collective-permute-start(f32[52,8,128]{2,1,0:T(8,128)S(1)} %get-tuple-element.25), channel_id=1, source_target_pairs={{0,32},{1,0},{2,34},{3,2},{4,36},{5,4},{6,38},{7,6},{8,40},{9,8},{... | collective-permute-start | bytes 638984 | tf_op jit(solution)/shard_map/ppermute | solution.py:422
  22.4 0.5 %collective-permute-start.3 = (f32[52,8,128]{2,1,0:T(8,128)S(1)}, f32[52,8,128]{2,1,0:T(8,128)S(1)}, u32[]{:S(2)}, u32[]{:S(2)}) collective-permute-start(f32[52,8,128]{2,1,0:T(8,128)S(1)} %get-tuple-element.26), channel_id=1, source_target_pairs={{32,0},{0,1},{34,2},{2,3},{36,4},{4,5},{38,6},{6,7},{40,8},{8,9},{... | collective-permute-start | bytes 638984 | tf_op jit(solution)/shard_map/ppermute | solution.py:422
  23.0 4.4 %collective-permute-done.2.ahead = f32[52,8,128]{2,1,0:T(8,128)S(1)} collective-permute-done((f32[52,8,128]{2,1,0:T(8,128)S(1)}, f32[52,8,128]{2,1,0:T(8,128)S(1)}, u32[]{:S(2)}, u32[]{:S(2)}) %collective-permute-start.2) | collective-permute-done | bytes 213024 | tf_op jit(solution)/shard_map/ppermute | solution.py:422
  27.4 0.9 %collective-permute-done.3.back = f32[52,8,128]{2,1,0:T(8,128)S(1)} collective-permute-done((f32[52,8,128]{2,1,0:T(8,128)S(1)}, f32[52,8,128]{2,1,0:T(8,128)S(1)}, u32[]{:S(2)}, u32[]{:S(2)}) %collective-permute-start.3) | collective-permute-done | bytes 213024 | tf_op jit(solution)/shard_map/ppermute | solution.py:422
  28.3 0.6 %shard_map.61 = (f32[19,16,8,128]{3,2,1,0:T(8,128)S(1)}, f32[19,2,8,128]{3,2,1,0:T(8,128)S(1)}, f32[10,8,128]{2,1,0:T(8,128)S(1)}, f32[10,8,128]{2,1,0:T(8,128)S(1)}) custom-call(f32[19,8,8,128]{3,2,1,0:T(8,128)S(1)} %get-tuple-element.24.own, f32[52,8,128]{2,1,0:T(8,128)S(1)} %collective-permute-done.2.ahead, f32[52,8,128]{2,1,0:T(8,128)S(1)} %collective-permute-done.3.back), custom_call_target="tpu_custom_call" | custom-call | tf_op jit(solution)/shard_map/pallas_call | solution.py:462
  28.9 1.0 %shard_map.63 = (f32[1856,128]{1,0:T(8,128)S(1)}, f32[37,8,128]{2,1,0:T(8,128)S(1)}, f32[37,8,128]{2,1,0:T(8,128)S(1)}) custom-call(f32[19,16,8,128]{3,2,1,0:T(8,128)S(1)} %get-tuple-element.33.main), custom_call_target="tpu_custom_call" | custom-call | tf_op jit(solution)/shard_map/pallas_call | solution.py:469
  29.9 0.0 collective-permute-start.8
  29.9 2.9 %collective-permute-start.9 = (f32[37,8,128]{2,1,0:T(8,128)S(1)}, f32[37,8,128]{2,1,0:T(8,128)S(1)}, u32[]{:S(2)}, u32[]{:S(2)}) collective-permute-start(f32[37,8,128]{2,1,0:T(8,128)S(1)} %get-tuple-element.36), channel_id=1, source_target_pairs={{1,0},{2,1},{3,2},{4,3},{5,4},{6,5},{7,6},{8,7},{9,8},{10,9},{11,1... | collective-permute-start | bytes 454664 | tf_op jit(solution)/shard_map/ppermute | solution.py:406
  32.8 2.8 %collective-permute-start.4 = (f32[10,8,128]{2,1,0:T(8,128)S(1)}, f32[10,8,128]{2,1,0:T(8,128)S(1)}, u32[]{:S(2)}, u32[]{:S(2)}) collective-permute-start(f32[10,8,128]{2,1,0:T(8,128)S(1)} %get-tuple-element.28), channel_id=1, source_target_pairs={{0,128},{1,0},{2,130},{3,2},{4,132},{5,4},{6,134},{7,6},{8,136},{9... | collective-permute-start | bytes 122888 | tf_op jit(solution)/shard_map/ppermute | solution.py:422
  35.6 0.0 collective-permute-start.5
  35.6 1.7 %collective-permute-done.4.ahead = f32[10,8,128]{2,1,0:T(8,128)S(1)} collective-permute-done((f32[10,8,128]{2,1,0:T(8,128)S(1)}, f32[10,8,128]{2,1,0:T(8,128)S(1)}, u32[]{:S(2)}, u32[]{:S(2)}) %collective-permute-start.4) | collective-permute-done | bytes 40992 | tf_op jit(solution)/shard_map/ppermute | solution.py:422
  37.3 3.5 %collective-permute-done.5.back = f32[10,8,128]{2,1,0:T(8,128)S(1)} collective-permute-done((f32[10,8,128]{2,1,0:T(8,128)S(1)}, f32[10,8,128]{2,1,0:T(8,128)S(1)}, u32[]{:S(2)}, u32[]{:S(2)}) %collective-permute-start.5) | collective-permute-done | bytes 40992 | tf_op jit(solution)/shard_map/ppermute | solution.py:422
  40.8 0.5 %shard_map.62 = (f32[640,128]{1,0:T(8,128)S(1)}, f32[13,8,128]{2,1,0:T(8,128)S(1)}, f32[13,8,128]{2,1,0:T(8,128)S(1)}) custom-call(f32[19,2,8,128]{3,2,1,0:T(8,128)S(1)} %get-tuple-element.27.edge, f32[10,8,128]{2,1,0:T(8,128)S(1)} %collective-permute-done.4.ahead, f32[10,8,128]{2,1,0:T(8,128)S(1)} %collective-permute-done.5.back), custom_call_target="tpu_custom_call" | custom-call | tf_op jit(solution)/shard_map/pallas_call | solution.py:476
  41.3 0.0 collective-permute-start.6
  41.4 2.9 %collective-permute-start.7 = (f32[13,8,128]{2,1,0:T(8,128)S(1)}, f32[13,8,128]{2,1,0:T(8,128)S(1)}, u32[]{:S(2)}, u32[]{:S(2)}) collective-permute-start(f32[13,8,128]{2,1,0:T(8,128)S(1)} %get-tuple-element.32), channel_id=1, source_target_pairs={{1,0},{2,1},{3,2},{4,3},{5,4},{6,5},{7,6},{8,7},{9,8},{10,9},{11,1... | collective-permute-start | bytes 159752 | tf_op jit(solution)/shard_map/ppermute | solution.py:406
  44.3 0.0 collective-permute-done.8.below
  44.3 0.0 collective-permute-done.9.above
  44.3 0.5 %shard_map.64 = (f32[19,8,8,128]{3,2,1,0:T(8,128)S(1)}, f32[1856,128]{1,0:T(8,128)S(1)}) custom-call(f32[1856,128]{1,0:T(8,128)S(1)} %get-tuple-element.34.flat_in, f32[37,8,128]{2,1,0:T(8,128)S(1)} %collective-permute-done.8.below, f32[37,8,128]{2,1,0:T(8,128)S(1)} %collective-permute-done.9.above), custom_call_target="tpu_custom_call", output_to_operand_aliasing={{1}: (0, {})} | custom-call | tf_op jit(solution)/shard_map/pallas_call | solution.py:482
  44.8 1.3 %collective-permute-done.6.below = f32[13,8,128]{2,1,0:T(8,128)S(1)} collective-permute-done((f32[13,8,128]{2,1,0:T(8,128)S(1)}, f32[13,8,128]{2,1,0:T(8,128)S(1)}, u32[]{:S(2)}, u32[]{:S(2)}) %collective-permute-start.6) | collective-permute-done | bytes 53280 | tf_op jit(solution)/shard_map/ppermute | solution.py:406
  46.1 0.0 collective-permute-done.7.above
  46.1 1.8 %shard_map.65 = (f32[19,4,8,128]{3,2,1,0:T(8,128)}, f32[1,2]{1,0:T(1,128)}, f32[640,128]{1,0:T(8,128)S(1)}) custom-call(f32[640,128]{1,0:T(8,128)S(1)} %get-tuple-element.30.flat_in, f32[13,8,128]{2,1,0:T(8,128)S(1)} %collective-permute-done.6.below, f32[13,8,128]{2,1,0:T(8,128)S(1)} %collective-permute-done.7.above, ...), custom_call_target="tpu_custom_call", output_to_operand_aliasing={{2}: (0, {})} | custom-call | tf_op jit(solution)/shard_map/pallas_call | solution.py:489
Async XLA Ops:
  1.7 18.8 %collective-permute-start = (f32[20,2,8,128]{3,2,1,0:T(8,128)S(1)}, f32[20,2,8,128]{3,2,1,0:T(8,128)S(1)}, u32[]{:S(2)}, u32[]{:S(2)}) collective-permute-start(f32[20,2,8,128]{3,2,1,0:T(8,128)S(1)} %get-tuple-element.22.high), channel_id=1, source_target_pairs={{0,1},{1,2},{2,3},{3,4},{4,5},{5,6},{6,7},{7,8},{8,9},{9,10},{10,1... | collective-permute-start | bytes 491528 | tf_op jit(solution)/shard_map/ppermute | solution.py:406
  1.7 18.7 %collective-permute-start.1 = (f32[20,2,8,128]{3,2,1,0:T(8,128)S(1)}, f32[20,2,8,128]{3,2,1,0:T(8,128)S(1)}, u32[]{:S(2)}, u32[]{:S(2)}) collective-permute-start(f32[20,2,8,128]{3,2,1,0:T(8,128)S(1)} %get-tuple-element.21.low), channel_id=1, source_target_pairs={{1,0},{2,1},{3,2},{4,3},{5,4},{6,5},{7,6},{8,7},{9,8},{10,9},{11,1... | collective-permute-start | bytes 491528 | tf_op jit(solution)/shard_map/ppermute | solution.py:406
  20.9 6.5 %collective-permute-start.2 = (f32[52,8,128]{2,1,0:T(8,128)S(1)}, f32[52,8,128]{2,1,0:T(8,128)S(1)}, u32[]{:S(2)}, u32[]{:S(2)}) collective-permute-start(f32[52,8,128]{2,1,0:T(8,128)S(1)} %get-tuple-element.25), channel_id=1, source_target_pairs={{0,32},{1,0},{2,34},{3,2},{4,36},{5,4},{6,38},{7,6},{8,40},{9,8},{... | collective-permute-start | bytes 638984 | tf_op jit(solution)/shard_map/ppermute | solution.py:422
  22.4 5.8 %collective-permute-start.3 = (f32[52,8,128]{2,1,0:T(8,128)S(1)}, f32[52,8,128]{2,1,0:T(8,128)S(1)}, u32[]{:S(2)}, u32[]{:S(2)}) collective-permute-start(f32[52,8,128]{2,1,0:T(8,128)S(1)} %get-tuple-element.26), channel_id=1, source_target_pairs={{32,0},{0,1},{34,2},{2,3},{36,4},{4,5},{38,6},{6,7},{40,8},{8,9},{... | collective-permute-start | bytes 638984 | tf_op jit(solution)/shard_map/ppermute | solution.py:422
  29.9 14.5 %collective-permute-start.8 = (f32[37,8,128]{2,1,0:T(8,128)S(1)}, f32[37,8,128]{2,1,0:T(8,128)S(1)}, u32[]{:S(2)}, u32[]{:S(2)}) collective-permute-start(f32[37,8,128]{2,1,0:T(8,128)S(1)} %get-tuple-element.35), channel_id=1, source_target_pairs={{0,1},{1,2},{2,3},{3,4},{4,5},{5,6},{6,7},{7,8},{8,9},{9,10},{10,1... | collective-permute-start | bytes 454664 | tf_op jit(solution)/shard_map/ppermute | solution.py:406
  29.9 14.4 %collective-permute-start.9 = (f32[37,8,128]{2,1,0:T(8,128)S(1)}, f32[37,8,128]{2,1,0:T(8,128)S(1)}, u32[]{:S(2)}, u32[]{:S(2)}) collective-permute-start(f32[37,8,128]{2,1,0:T(8,128)S(1)} %get-tuple-element.36), channel_id=1, source_target_pairs={{1,0},{2,1},{3,2},{4,3},{5,4},{6,5},{7,6},{8,7},{9,8},{10,9},{11,1... | collective-permute-start | bytes 454664 | tf_op jit(solution)/shard_map/ppermute | solution.py:406
  32.8 4.5 %collective-permute-start.4 = (f32[10,8,128]{2,1,0:T(8,128)S(1)}, f32[10,8,128]{2,1,0:T(8,128)S(1)}, u32[]{:S(2)}, u32[]{:S(2)}) collective-permute-start(f32[10,8,128]{2,1,0:T(8,128)S(1)} %get-tuple-element.28), channel_id=1, source_target_pairs={{0,128},{1,0},{2,130},{3,2},{4,132},{5,4},{6,134},{7,6},{8,136},{9... | collective-permute-start | bytes 122888 | tf_op jit(solution)/shard_map/ppermute | solution.py:422
  35.6 5.2 %collective-permute-start.5 = (f32[10,8,128]{2,1,0:T(8,128)S(1)}, f32[10,8,128]{2,1,0:T(8,128)S(1)}, u32[]{:S(2)}, u32[]{:S(2)}) collective-permute-start(f32[10,8,128]{2,1,0:T(8,128)S(1)} %get-tuple-element.29), channel_id=1, source_target_pairs={{128,0},{0,1},{130,2},{2,3},{132,4},{4,5},{134,6},{6,7},{136,8},{8... | collective-permute-start | bytes 122888 | tf_op jit(solution)/shard_map/ppermute | solution.py:422
  41.3 4.8 %collective-permute-start.6 = (f32[13,8,128]{2,1,0:T(8,128)S(1)}, f32[13,8,128]{2,1,0:T(8,128)S(1)}, u32[]{:S(2)}, u32[]{:S(2)}) collective-permute-start(f32[13,8,128]{2,1,0:T(8,128)S(1)} %get-tuple-element.31), channel_id=1, source_target_pairs={{0,1},{1,2},{2,3},{3,4},{4,5},{5,6},{6,7},{7,8},{8,9},{9,10},{10,1... | collective-permute-start | bytes 159752 | tf_op jit(solution)/shard_map/ppermute | solution.py:406
  41.4 4.8 %collective-permute-start.7 = (f32[13,8,128]{2,1,0:T(8,128)S(1)}, f32[13,8,128]{2,1,0:T(8,128)S(1)}, u32[]{:S(2)}, u32[]{:S(2)}) collective-permute-start(f32[13,8,128]{2,1,0:T(8,128)S(1)} %get-tuple-element.32), channel_id=1, source_target_pairs={{1,0},{2,1},{3,2},{4,3},{5,4},{6,5},{7,6},{8,7},{9,8},{10,9},{11,1... | collective-permute-start | bytes 159752 | tf_op jit(solution)/shard_map/ppermute | solution.py:406

commit v7 on v4

--- a/solution.py
+++ b/solution.py
@@ -134,9 +134,8 @@
     return out
 
 
-def gather_columns(values, rows):
+def gather_columns(tile, values, rows):
     lane_row = lanes() // 8
-    tile = jnp.full((8, 128), SOLID, F32)
     for row, value in zip(rows, values):
         tile = jnp.where(lane_row == row, roll(value, 0, 8 * row + 4), tile)
     return tile
@@ -207,14 +206,21 @@
             message[50 + group] = stage[side, pl.ds(64 * (group + 2) + 7, 8, stride=8)]
 
 
-def join_rows(own, ahead, back, main, edge, x_ahead, x_back, stage):
+def own_rows(own, main, edge):
+    for i in range(Q):
+        rows = [own[i, k] for k in range(8)]
+        main[i, 0] = jnp.full((8, 128), SOLID, F32)
+        main[i, 15] = jnp.full((8, 128), SOLID, F32)
+        for k in range(8):
+            main[i, 4 + k] = rows[k]
+        edge[i] = gather_columns(jnp.full((8, 128), SOLID, F32), rows, range(4, 12))
+
+
+def join_rows(main_in, edge_in, ahead, back, main, edge, x_ahead, x_back, stage):
     place = lax.axis_index("gy")
     up = lax.axis_index("gz") % 2 == 0
     outside_low = place == 0
     outside_high = place == lax.axis_size("gy") - 1
-    for i in range(Q):
-        main[i, 0] = jnp.full((8, 128), SOLID, F32)
-        main[i, 15] = jnp.full((8, 128), SOLID, F32)
     for side, (message, low_rows) in enumerate(((ahead, up), (back, jnp.logical_not(up)))):
         outside = jnp.where(low_rows, outside_low, outside_high)
         first = jnp.where(low_rows, 1, 12)
@@ -236,11 +242,8 @@
             main[jnp.where(low_rows, UP_Y[k], DOWN_Y[k]), far] = value
     edges = []
     for i in range(Q):
-        rows = [own[i, k] for k in range(8)]
-        for k in range(8):
-            main[i, 4 + k] = rows[k]
-        rows = [main[i, k] for k in range(4)] + rows + [main[i, k] for k in range(12, 16)]
-        edges.append(gather_columns(rows, range(16)))
+        beside = [*range(4), *range(12, 16)]
+        edges.append(gather_columns(edge[i], [main[i, k] for k in beside], beside))
         edge[i] = edges[i]
     low_side = lanes() % 8 < 4
     for i in range(10):
@@ -270,7 +273,7 @@
     for row in range(2, 14):
         second(row)
     for i in range(Q):
-        edge[i] = gather_columns([out[i, k] for k in range(12)], range(2, 14))
+        edge[i] = gather_columns(out[i, 0], [out[i, k] for k in range(12)], range(2, 14))
 
 
 def patch_two_steps(inner, inner_edge, edge, ahead, back, flat, below, above):
@@ -319,9 +322,9 @@
 
 
 def last_two_steps(
-    flat_in, below, above, block_fluid, out, block_density, flat, middle, turn, final, wet_count, sems
+    flat_in, below, above, block_fluid, out, block_density, flat, middle, turn, final, wet_count, mean, sems
 ):
-    count_copy = pltpu.make_async_copy(block_fluid, wet_count, sems.at[2])
+    count_copy = pltpu.make_async_copy(block_fluid, wet_count, sems.at[4])
     count_copy.start()
     place = lax.axis_index("gz")
     at_low = place == 0
@@ -363,25 +366,21 @@
             turn[i, 8 * row : 8 * row + 8] = jnp.where(wet, value, 0.0)
     copies = []
     masses = []
-    for slot in range(2):
-        mass = None
-        for k in range(2):
-            layer = 2 * slot + k
-            values = [turn[i, pl.ds(layer + 2, 8, stride=8)] for i in range(Q)]
-            for i in range(Q):
-                final[i, layer] = values[i]
-            axis_sum = functools.reduce(jnp.add, values[1:7])
-            edge_sum = functools.reduce(jnp.add, values[7:])
-            density = values[0] * (1.0 / 3.0) + axis_sum * (1.0 / 18.0) + edge_sum * (1.0 / 36.0)
-            mass = density if mass is None else mass + density
-        masses.append(mass)
-        layers = slice(2 * slot, 2 * slot + 2)
-        copies.append(pltpu.make_async_copy(final.at[:, layers], out.at[:, layers], sems.at[slot]))
-        copies[slot].start()
+    for layer in range(4):
+        values = [turn[i, pl.ds(layer + 2, 8, stride=8)] for i in range(Q)]
+        for i in range(Q):
+            final[i, layer] = values[i]
+        copies.append(pltpu.make_async_copy(final.at[:, layer], out.at[:, layer], sems.at[layer]))
+        copies[layer].start()
+        axis_sum = functools.reduce(jnp.add, values[1:7])
+        edge_sum = functools.reduce(jnp.add, values[7:])
+        masses.append(values[0] * (1.0 / 3.0) + axis_sum * (1.0 / 18.0) + edge_sum * (1.0 / 36.0))
     count_copy.wait()
     for slot in range(2):
         count = jnp.maximum(wet_count[0, slot], 1).astype(F32)
-        block_density[0, slot] = jnp.sum(masses[slot]) / count
+        mean[0, slot] = jnp.sum(masses[2 * slot] + masses[2 * slot + 1]) / count
+    copies.append(pltpu.make_async_copy(mean, block_density, sems.at[5]))
+    copies[4].start()
     for copy in copies:
         copy.wait()
 
@@ -446,12 +445,14 @@
         scratch=[pltpu.VMEM((Q + 1, 64, 128), F32), pltpu.VMEM((2, 512, 128), F32)],
     )(high, low, above, below, moved)
     ahead, back = loop_exchange(ahead, back, "gy")
+    main, edge = call(own_rows, [shape(Q, 16, 8, 128), shape(Q, 8, 128)], [VMEM])(own)
     main, edge, x_ahead, x_back = call(
         join_rows,
         [shape(Q, 16, 8, 128), shape(Q, 8, 128), shape(10, 8, 128), shape(10, 8, 128)],
-        [VMEM] * 3,
+        [VMEM] * 4,
         scratch=[pltpu.VMEM((2, 512, 128), F32)],
-    )(own, ahead, back)
+        aliases={0: 0, 1: 1},
+    )(main, edge, ahead, back)
     x_ahead, x_back = loop_exchange(x_ahead, x_back, "gx")
     inner, inner_edge = call(
         two_steps,
@@ -469,13 +470,14 @@
         last_two_steps,
         [shape(Q, 4, 8, 128), shape(1, 2), shape(FLAT_ROWS, 128)],
         [VMEM] * 3 + [HBM],
-        [HBM, SMEM, VMEM],
+        [HBM, HBM, VMEM],
         scratch=[
             pltpu.VMEM((Q, 10, 8, 128), F32),
             pltpu.VMEM((Q, 64, 128), F32),
             pltpu.VMEM((Q, 4, 8, 128), F32),
             pltpu.SMEM((1, 2), jnp.int32),
-            pltpu.SemaphoreType.DMA((3,)),
+            pltpu.SMEM((1, 2), F32),
+            pltpu.SemaphoreType.DMA((6,)),
         ],
         aliases={0: 2},
     )(flat, below, above, in_hbm(block_fluid.transpose(1, 2, 0).reshape(1, 2)))

time: 45.9 us -> 45.8 us (level)
  transfers between devices with their start and end apart: 8 -> 8, of which waited for: 6 -> 6; matrix products, arithmetic and copies ran while one was open for 0% -> 0% of each run, Pallas kernels for 2% -> 3%
where the time goes in v7:
time: 45.8 us; the launch traced here: 45.6 us
  starting transfers between devices  23.6 us (52%)
  waiting for transfers between devices  15.2 us (33%)
  Pallas kernels  6.11 us (13%)
  between operations  0.69 us (2%)
    ppermute x4, starting transfers between devices, ring_exchange(): return (lax.ppermute(to_high, axis, up), lax.ppermute(to_low, axis, down))  18.7 us
    ppermute x4, waiting for transfers between devices, loop_exchange(): return (lax.ppermute(ahead, axes, pairs), lax.ppermute(back, axes, inverse))  9.14 us
    ppermute x4, waiting for transfers between devices, ring_exchange(): return (lax.ppermute(to_high, axis, up), lax.ppermute(to_low, axis, down))  6.11 us
    ppermute x4, starting transfers between devices, loop_exchange(): return (lax.ppermute(ahead, axes, pairs), lax.ppermute(back, axes, inverse))  4.85 us
    pallas_call x1, Pallas kernels, on_device(): call(last_two_steps, [shape(Q, 4, 8, 128), shape(1, 2), shape(FLAT_ROWS,...  2.06 us
    pallas_call x1, Pallas kernels, on_device(): call(two_steps, [shape(Q, 12, 8, 128), shape(Q, 8, 128)], [VMEM], scratch...  1.14 us
    pallas_call x1, Pallas kernels, on_device(): call(split_slabs, [shape(Q + 1, 2, 8, 128), shape(Q + 1, 2, 8, 128), shap...  1.04 us
  transfers between devices with their start and end apart: 8, of which 6 were waited for; matrix products, arithmetic and copies ran while one was open for 0% of the time, Pallas kernels for 3%

profile of v7, /device:TPU:26, one launch (start us, length us, event | category | flops | bytes accessed | tf_op | source)
XLA Modules:
  0.0 45.6 jit_solution(675654588274443674)
XLA Ops:
  0.6 1.0 %shard_map.59 = (f32[20,2,8,128]{3,2,1,0:T(8,128)S(1)}, f32[20,2,8,128]{3,2,1,0:T(8,128)S(1)}, f32[2,8,128]{2,1,0:T(8,128)S(1)}) custom-call(f32[19,4,8,128]{3,2,1,0:T(8,128)} %relative.1, s32[4,8,128]{2,1,0:T(8,128)} %fluid.1, s32[1,2]{1,0:T(1,128)} %bitcast.3), custom_call_target="tpu_custom_call" | custom-call | tf_op jit(solution)/shard_map/pallas_call | solution.py:430
  1.7 0.0 collective-permute-start.1
  1.7 15.8 %collective-permute-start = (f32[20,2,8,128]{3,2,1,0:T(8,128)S(1)}, f32[20,2,8,128]{3,2,1,0:T(8,128)S(1)}, u32[]{:S(2)}, u32[]{:S(2)}) collective-permute-start(f32[20,2,8,128]{3,2,1,0:T(8,128)S(1)} %get-tuple-element.22.low), channel_id=1, source_target_pairs={{1,0},{2,1},{3,2},{4,3},{5,4},{6,5},{7,6},{8,7},{9,8},{10,9},{11,1... | collective-permute-start | bytes 491528 | tf_op jit(solution)/shard_map/ppermute | solution.py:392
  17.5 3.0 %collective-permute-done.1.below = f32[20,2,8,128]{3,2,1,0:T(8,128)S(1)} collective-permute-done((f32[20,2,8,128]{3,2,1,0:T(8,128)S(1)}, f32[20,2,8,128]{3,2,1,0:T(8,128)S(1)}, u32[]{:S(2)}, u32[]{:S(2)}) %collective-permute-start.1) | collective-permute-done | bytes 163872 | tf_op jit(solution)/shard_map/ppermute | solution.py:392
  20.5 0.0 collective-permute-done.above
  20.5 0.5 %shard_map.60 = (f32[19,8,8,128]{3,2,1,0:T(8,128)S(1)}, f32[52,8,128]{2,1,0:T(8,128)S(1)}, f32[52,8,128]{2,1,0:T(8,128)S(1)}) custom-call(f32[20,2,8,128]{3,2,1,0:T(8,128)S(1)} %get-tuple-element.21.high, f32[20,2,8,128]{3,2,1,0:T(8,128)S(1)} %get-tuple-element.22.low, f32[20,2,8,128]{3,2,1,0:T(8,128)S(1)} %collective-permute-done.above, ...), custom_call_target="tpu_custom_call" | custom-call | tf_op jit(solution)/shard_map/pallas_call | solution.py:441
  20.9 1.5 %collective-permute-start.2 = (f32[52,8,128]{2,1,0:T(8,128)S(1)}, f32[52,8,128]{2,1,0:T(8,128)S(1)}, u32[]{:S(2)}, u32[]{:S(2)}) collective-permute-start(f32[52,8,128]{2,1,0:T(8,128)S(1)} %get-tuple-element.27), channel_id=1, source_target_pairs={{0,32},{1,0},{2,34},{3,2},{4,36},{5,4},{6,38},{7,6},{8,40},{9,8},{... | collective-permute-start | bytes 638984 | tf_op jit(solution)/shard_map/ppermute | solution.py:408
  22.4 0.5 %collective-permute-start.3 = (f32[52,8,128]{2,1,0:T(8,128)S(1)}, f32[52,8,128]{2,1,0:T(8,128)S(1)}, u32[]{:S(2)}, u32[]{:S(2)}) collective-permute-start(f32[52,8,128]{2,1,0:T(8,128)S(1)} %get-tuple-element.28), channel_id=1, source_target_pairs={{32,0},{0,1},{34,2},{2,3},{36,4},{4,5},{38,6},{6,7},{40,8},{8,9},{... | collective-permute-start | bytes 638984 | tf_op jit(solution)/shard_map/ppermute | solution.py:408
  23.0 0.2 shard_map.61
  23.2 4.2 %collective-permute-done.2.ahead = f32[52,8,128]{2,1,0:T(8,128)S(1)} collective-permute-done((f32[52,8,128]{2,1,0:T(8,128)S(1)}, f32[52,8,128]{2,1,0:T(8,128)S(1)}, u32[]{:S(2)}, u32[]{:S(2)}) %collective-permute-start.2) | collective-permute-done | bytes 213024 | tf_op jit(solution)/shard_map/ppermute | solution.py:408
  27.4 0.9 %collective-permute-done.3.back = f32[52,8,128]{2,1,0:T(8,128)S(1)} collective-permute-done((f32[52,8,128]{2,1,0:T(8,128)S(1)}, f32[52,8,128]{2,1,0:T(8,128)S(1)}, u32[]{:S(2)}, u32[]{:S(2)}) %collective-permute-start.3) | collective-permute-done | bytes 213024 | tf_op jit(solution)/shard_map/ppermute | solution.py:408
  28.3 0.4 shard_map.62
  28.7 2.8 %collective-permute-start.4 = (f32[10,8,128]{2,1,0:T(8,128)S(1)}, f32[10,8,128]{2,1,0:T(8,128)S(1)}, u32[]{:S(2)}, u32[]{:S(2)}) collective-permute-start(f32[10,8,128]{2,1,0:T(8,128)S(1)} %get-tuple-element.33), channel_id=1, source_target_pairs={{0,128},{1,0},{2,130},{3,2},{4,132},{5,4},{6,134},{7,6},{8,136},{9... | collective-permute-start | bytes 122888 | tf_op jit(solution)/shard_map/ppermute | solution.py:408
  31.5 0.0 collective-permute-start.5
  31.5 1.1 %shard_map.63 = (f32[19,12,8,128]{3,2,1,0:T(8,128)S(1)}, f32[19,8,128]{2,1,0:T(8,128)S(1)}) custom-call(f32[19,16,8,128]{3,2,1,0:T(8,128)S(1)} %get-tuple-element.29.main), custom_call_target="tpu_custom_call" | custom-call | tf_op jit(solution)/shard_map/pallas_call | solution.py:457
  32.7 0.5 %collective-permute-done.4.ahead = f32[10,8,128]{2,1,0:T(8,128)S(1)} collective-permute-done((f32[10,8,128]{2,1,0:T(8,128)S(1)}, f32[10,8,128]{2,1,0:T(8,128)S(1)}, u32[]{:S(2)}, u32[]{:S(2)}) %collective-permute-start.4) | collective-permute-done | bytes 40992 | tf_op jit(solution)/shard_map/ppermute | solution.py:408
  33.2 3.5 %collective-permute-done.5.back = f32[10,8,128]{2,1,0:T(8,128)S(1)} collective-permute-done((f32[10,8,128]{2,1,0:T(8,128)S(1)}, f32[10,8,128]{2,1,0:T(8,128)S(1)}, u32[]{:S(2)}, u32[]{:S(2)}) %collective-permute-start.5) | collective-permute-done | bytes 40992 | tf_op jit(solution)/shard_map/ppermute | solution.py:408
  36.8 0.7 %shard_map.64 = (f32[2176,128]{1,0:T(8,128)S(1)}, f32[43,8,128]{2,1,0:T(8,128)S(1)}, f32[43,8,128]{2,1,0:T(8,128)S(1)}) custom-call(f32[19,12,8,128]{3,2,1,0:T(8,128)S(1)} %get-tuple-element.30.inner, f32[19,8,128]{2,1,0:T(8,128)S(1)} %get-tuple-element.31.inner_edge, f32[19,8,128]{2,1,0:T(8,128)S(1)} %get-tuple-element.32.edge, ...), custom_call_target="tpu_custom_call" | custom-call | tf_op jit(solution)/shard_map/pallas_call | solution.py:463
  37.5 0.0 collective-permute-start.6
  37.5 2.9 %collective-permute-start.7 = (f32[43,8,128]{2,1,0:T(8,128)S(1)}, f32[43,8,128]{2,1,0:T(8,128)S(1)}, u32[]{:S(2)}, u32[]{:S(2)}) collective-permute-start(f32[43,8,128]{2,1,0:T(8,128)S(1)} %get-tuple-element.37), channel_id=1, source_target_pairs={{1,0},{2,1},{3,2},{4,3},{5,4},{6,5},{7,6},{8,7},{9,8},{10,9},{11,1... | collective-permute-start | bytes 528392 | tf_op jit(solution)/shard_map/ppermute | solution.py:392
  40.5 3.1 %collective-permute-done.6.below = f32[43,8,128]{2,1,0:T(8,128)S(1)} collective-permute-done((f32[43,8,128]{2,1,0:T(8,128)S(1)}, f32[43,8,128]{2,1,0:T(8,128)S(1)}, u32[]{:S(2)}, u32[]{:S(2)}) %collective-permute-start.6) | collective-permute-done | bytes 176160 | tf_op jit(solution)/shard_map/ppermute | solution.py:392
  43.6 0.0 collective-permute-done.7.above
  43.6 2.1 %shard_map.65 = (f32[19,4,8,128]{3,2,1,0:T(8,128)}, f32[1,2]{1,0:T(1,128)}, f32[2176,128]{1,0:T(8,128)S(1)}) custom-call(f32[2176,128]{1,0:T(8,128)S(1)} %get-tuple-element.35.flat_in, f32[43,8,128]{2,1,0:T(8,128)S(1)} %collective-permute-done.6.below, f32[43,8,128]{2,1,0:T(8,128)S(1)} %collective-permute-done.7.above, ...), custom_call_target="tpu_custom_call", output_to_operand_aliasing={{2}: (0, {})} | custom-call | tf_op jit(solution)/shard_map/pallas_call | solution.py:469
Async XLA Ops:
  1.7 18.8 %collective-permute-start.1 = (f32[20,2,8,128]{3,2,1,0:T(8,128)S(1)}, f32[20,2,8,128]{3,2,1,0:T(8,128)S(1)}, u32[]{:S(2)}, u32[]{:S(2)}) collective-permute-start(f32[20,2,8,128]{3,2,1,0:T(8,128)S(1)} %get-tuple-element.21.high), channel_id=1, source_target_pairs={{0,1},{1,2},{2,3},{3,4},{4,5},{5,6},{6,7},{7,8},{8,9},{9,10},{10,1... | collective-permute-start | bytes 491528 | tf_op jit(solution)/shard_map/ppermute | solution.py:392
  1.7 18.7 %collective-permute-start = (f32[20,2,8,128]{3,2,1,0:T(8,128)S(1)}, f32[20,2,8,128]{3,2,1,0:T(8,128)S(1)}, u32[]{:S(2)}, u32[]{:S(2)}) collective-permute-start(f32[20,2,8,128]{3,2,1,0:T(8,128)S(1)} %get-tuple-element.22.low), channel_id=1, source_target_pairs={{1,0},{2,1},{3,2},{4,3},{5,4},{6,5},{7,6},{8,7},{9,8},{10,9},{11,1... | collective-permute-start | bytes 491528 | tf_op jit(solution)/shard_map/ppermute | solution.py:392
  20.9 6.5 %collective-permute-start.2 = (f32[52,8,128]{2,1,0:T(8,128)S(1)}, f32[52,8,128]{2,1,0:T(8,128)S(1)}, u32[]{:S(2)}, u32[]{:S(2)}) collective-permute-start(f32[52,8,128]{2,1,0:T(8,128)S(1)} %get-tuple-element.27), channel_id=1, source_target_pairs={{0,32},{1,0},{2,34},{3,2},{4,36},{5,4},{6,38},{7,6},{8,40},{9,8},{... | collective-permute-start | bytes 638984 | tf_op jit(solution)/shard_map/ppermute | solution.py:408
  22.4 5.8 %collective-permute-start.3 = (f32[52,8,128]{2,1,0:T(8,128)S(1)}, f32[52,8,128]{2,1,0:T(8,128)S(1)}, u32[]{:S(2)}, u32[]{:S(2)}) collective-permute-start(f32[52,8,128]{2,1,0:T(8,128)S(1)} %get-tuple-element.28), channel_id=1, source_target_pairs={{32,0},{0,1},{34,2},{2,3},{36,4},{4,5},{38,6},{6,7},{40,8},{8,9},{... | collective-permute-start | bytes 638984 | tf_op jit(solution)/shard_map/ppermute | solution.py:408
  28.7 4.5 %collective-permute-start.4 = (f32[10,8,128]{2,1,0:T(8,128)S(1)}, f32[10,8,128]{2,1,0:T(8,128)S(1)}, u32[]{:S(2)}, u32[]{:S(2)}) collective-permute-start(f32[10,8,128]{2,1,0:T(8,128)S(1)} %get-tuple-element.33), channel_id=1, source_target_pairs={{0,128},{1,0},{2,130},{3,2},{4,132},{5,4},{6,134},{7,6},{8,136},{9... | collective-permute-start | bytes 122888 | tf_op jit(solution)/shard_map/ppermute | solution.py:408
  31.5 5.2 %collective-permute-start.5 = (f32[10,8,128]{2,1,0:T(8,128)S(1)}, f32[10,8,128]{2,1,0:T(8,128)S(1)}, u32[]{:S(2)}, u32[]{:S(2)}) collective-permute-start(f32[10,8,128]{2,1,0:T(8,128)S(1)} %get-tuple-element.34), channel_id=1, source_target_pairs={{128,0},{0,1},{130,2},{2,3},{132,4},{4,5},{134,6},{6,7},{136,8},{8... | collective-permute-start | bytes 122888 | tf_op jit(solution)/shard_map/ppermute | solution.py:408
  37.5 6.1 %collective-permute-start.6 = (f32[43,8,128]{2,1,0:T(8,128)S(1)}, f32[43,8,128]{2,1,0:T(8,128)S(1)}, u32[]{:S(2)}, u32[]{:S(2)}) collective-permute-start(f32[43,8,128]{2,1,0:T(8,128)S(1)} %get-tuple-element.36), channel_id=1, source_target_pairs={{0,1},{1,2},{2,3},{3,4},{4,5},{5,6},{6,7},{7,8},{8,9},{9,10},{10,1... | collective-permute-start | bytes 528392 | tf_op jit(solution)/shard_map/ppermute | solution.py:392
  37.5 6.1 %collective-permute-start.7 = (f32[43,8,128]{2,1,0:T(8,128)S(1)}, f32[43,8,128]{2,1,0:T(8,128)S(1)}, u32[]{:S(2)}, u32[]{:S(2)}) collective-permute-start(f32[43,8,128]{2,1,0:T(8,128)S(1)} %get-tuple-element.37), channel_id=1, source_target_pairs={{1,0},{2,1},{3,2},{4,3},{5,4},{6,5},{7,6},{8,7},{9,8},{10,9},{11,1... | collective-permute-start | bytes 528392 | tf_op jit(solution)/shard_map/ppermute | solution.py:392

commit v8 on v7

--- a/solution.py
+++ b/solution.py
@@ -295,10 +295,11 @@
                 values.append(jnp.where(low_side, message, edge[i]))
             else:
                 values.append(jnp.where(low_side, edge[i], message))
-        for step in range(2):
-            wet = values[0] != SOLID
-            values = relax_wet(stream_patch(values), wet)
         sides.append(values)
+    for step in range(2):
+        for side in range(2):
+            wet = sides[side][0] != SOLID
+            sides[side] = relax_wet(stream_patch(sides[side]), wet)
     lane = lanes()
     seam = (lane < 2) | (lane >= 126)
     for i in range(Q):
@@ -322,7 +323,7 @@
 
 
 def last_two_steps(
-    flat_in, below, above, block_fluid, out, block_density, flat, middle, turn, final, wet_count, mean, sems
+    flat_in, below, above, block_fluid, out, block_density, flat, middle, turn, patch, columns, final, wet_count, mean, sems
 ):
     count_copy = pltpu.make_async_copy(block_fluid, wet_count, sems.at[4])
     count_copy.start()
@@ -348,39 +349,44 @@
         for i in range(Q):
             middle[i, row - 3] = values[i]
 
-    for row in range(3, 13):
-        third(row)
-    patches = []
     for side in range(2):
         values = [joined(i, 12 + side) for i in range(Q)]
         wet = values[0] != SOLID
         values = relax_wet(stream_patch(values), wet)
-        patches.append(stream_patch(values))
-    own_columns = [jnp.where(low_side, patches[1][i], patches[0][i]) for i in range(Q)]
+        for i in range(Q):
+            patch[side, i] = values[i]
+    for row in range(3, 13):
+        third(row)
+    streamed = [stream_patch([patch[side, i] for i in range(Q)]) for side in range(2)]
+    for i in range(Q):
+        columns[i] = jnp.where(low_side, streamed[1][i], streamed[0][i])
     seam = (lane < 2) | (lane >= 126)
+    mass = jnp.zeros((8, 128), F32)
     for row in range(8):
         wet = middle[0, row + 1] != SOLID
         values = stream_row(lambda i, at: middle[i, at], row + 1)
         for i in range(Q):
-            value = jnp.where(seam, roll(own_columns[i], 0, -(8 * (row + 4) + 4)), values[i])
-            turn[i, 8 * row : 8 * row + 8] = jnp.where(wet, value, 0.0)
-    copies = []
-    masses = []
-    for layer in range(4):
-        values = [turn[i, pl.ds(layer + 2, 8, stride=8)] for i in range(Q)]
-        for i in range(Q):
-            final[i, layer] = values[i]
-        copies.append(pltpu.make_async_copy(final.at[:, layer], out.at[:, layer], sems.at[layer]))
-        copies[layer].start()
+            value = jnp.where(seam, roll(columns[i], 0, -(8 * (row + 4) + 4)), values[i])
+            values[i] = jnp.where(wet, value, 0.0)
+            turn[i, 8 * row : 8 * row + 8] = values[i]
         axis_sum = functools.reduce(jnp.add, values[1:7])
         edge_sum = functools.reduce(jnp.add, values[7:])
-        masses.append(values[0] * (1.0 / 3.0) + axis_sum * (1.0 / 18.0) + edge_sum * (1.0 / 36.0))
+        mass += values[0] * (1.0 / 3.0) + axis_sum * (1.0 / 18.0) + edge_sum * (1.0 / 36.0)
+    mass = jnp.sum(mass, axis=1, keepdims=True)
+    layer = lax.broadcasted_iota(jnp.int32, (8, 1), 0) // 2
+    totals = [jnp.sum(jnp.where(layer == slot + 1, mass, 0.0), axis=0, keepdims=True) for slot in range(2)]
+    slot = lax.broadcasted_iota(jnp.int32, (1, 2), 1)
+    totals = jnp.where(slot == 0, totals[0], totals[1])
+    copies = []
+    for layer in range(4):
+        for i in range(Q):
+            final[i, layer] = turn[i, pl.ds(layer + 2, 8, stride=8)]
+        copies.append(pltpu.make_async_copy(final.at[:, layer], out.at[:, layer], sems.at[layer]))
+        copies[-1].start()
     count_copy.wait()
-    for slot in range(2):
-        count = jnp.maximum(wet_count[0, slot], 1).astype(F32)
-        mean[0, slot] = jnp.sum(masses[2 * slot] + masses[2 * slot + 1]) / count
+    mean[...] = totals / jnp.maximum(wet_count[...], 1).astype(F32)
     copies.append(pltpu.make_async_copy(mean, block_density, sems.at[5]))
-    copies[4].start()
+    copies[-1].start()
     for copy in copies:
         copy.wait()
 
@@ -474,9 +480,11 @@
         scratch=[
             pltpu.VMEM((Q, 10, 8, 128), F32),
             pltpu.VMEM((Q, 64, 128), F32),
+            pltpu.VMEM((2, Q, 8, 128), F32),
+            pltpu.VMEM((Q, 8, 128), F32),
             pltpu.VMEM((Q, 4, 8, 128), F32),
-            pltpu.SMEM((1, 2), jnp.int32),
-            pltpu.SMEM((1, 2), F32),
+            pltpu.VMEM((1, 2), jnp.int32),
+            pltpu.VMEM((1, 2), F32),
             pltpu.SemaphoreType.DMA((6,)),
         ],
         aliases={0: 2},

time: 45.8 us -> 45.6 us (level)
  no operation moved by 1% of the time
where the time goes in v8:
time: 45.6 us; the launch traced here: 45.4 us
  starting transfers between devices  23.6 us (52%)
  waiting for transfers between devices  15.2 us (33%)
  Pallas kernels  5.89 us (13%)
  between operations  0.69 us (2%)
    ppermute x4, starting transfers between devices, ring_exchange(): return (lax.ppermute(to_high, axis, up), lax.ppermute(to_low, axis, down))  18.7 us
    ppermute x4, waiting for transfers between devices, loop_exchange(): return (lax.ppermute(ahead, axes, pairs), lax.ppermute(back, axes, inverse))  9.14 us
    ppermute x4, waiting for transfers between devices, ring_exchange(): return (lax.ppermute(to_high, axis, up), lax.ppermute(to_low, axis, down))  6.11 us
    ppermute x4, starting transfers between devices, loop_exchange(): return (lax.ppermute(ahead, axes, pairs), lax.ppermute(back, axes, inverse))  4.85 us
    pallas_call x1, Pallas kernels, on_device(): call(last_two_steps, [shape(Q, 4, 8, 128), shape(1, 2), shape(FLAT_ROWS,...  1.83 us
    pallas_call x1, Pallas kernels, on_device(): call(two_steps, [shape(Q, 12, 8, 128), shape(Q, 8, 128)], [VMEM], scratch...  1.14 us
    pallas_call x1, Pallas kernels, on_device(): call(split_slabs, [shape(Q + 1, 2, 8, 128), shape(Q + 1, 2, 8, 128), shap...  1.04 us
  transfers between devices with their start and end apart: 8, of which 6 were waited for; matrix products, arithmetic and copies ran while one was open for 0% of the time, Pallas kernels for 3%

profile of v8, /device:TPU:26, one launch (start us, length us, event | category | flops | bytes accessed | tf_op | source)
XLA Modules:
  0.0 45.4 jit_solution(13665975803631442475)
XLA Ops:
  0.6 1.0 %shard_map.59 = (f32[20,2,8,128]{3,2,1,0:T(8,128)S(1)}, f32[20,2,8,128]{3,2,1,0:T(8,128)S(1)}, f32[2,8,128]{2,1,0:T(8,128)S(1)}) custom-call(f32[19,4,8,128]{3,2,1,0:T(8,128)} %relative.1, s32[4,8,128]{2,1,0:T(8,128)} %fluid.1, s32[1,2]{1,0:T(1,128)} %bitcast.3), custom_call_target="tpu_custom_call" | custom-call | tf_op jit(solution)/shard_map/pallas_call | solution.py:436
  1.7 0.0 collective-permute-start.1
  1.7 15.8 %collective-permute-start = (f32[20,2,8,128]{3,2,1,0:T(8,128)S(1)}, f32[20,2,8,128]{3,2,1,0:T(8,128)S(1)}, u32[]{:S(2)}, u32[]{:S(2)}) collective-permute-start(f32[20,2,8,128]{3,2,1,0:T(8,128)S(1)} %get-tuple-element.22.low), channel_id=1, source_target_pairs={{1,0},{2,1},{3,2},{4,3},{5,4},{6,5},{7,6},{8,7},{9,8},{10,9},{11,1... | collective-permute-start | bytes 491528 | tf_op jit(solution)/shard_map/ppermute | solution.py:398
  17.5 3.0 %collective-permute-done.1.below = f32[20,2,8,128]{3,2,1,0:T(8,128)S(1)} collective-permute-done((f32[20,2,8,128]{3,2,1,0:T(8,128)S(1)}, f32[20,2,8,128]{3,2,1,0:T(8,128)S(1)}, u32[]{:S(2)}, u32[]{:S(2)}) %collective-permute-start.1) | collective-permute-done | bytes 163872 | tf_op jit(solution)/shard_map/ppermute | solution.py:398
  20.5 0.0 collective-permute-done.above
  20.5 0.5 %shard_map.60 = (f32[19,8,8,128]{3,2,1,0:T(8,128)S(1)}, f32[52,8,128]{2,1,0:T(8,128)S(1)}, f32[52,8,128]{2,1,0:T(8,128)S(1)}) custom-call(f32[20,2,8,128]{3,2,1,0:T(8,128)S(1)} %get-tuple-element.21.high, f32[20,2,8,128]{3,2,1,0:T(8,128)S(1)} %get-tuple-element.22.low, f32[20,2,8,128]{3,2,1,0:T(8,128)S(1)} %collective-permute-done.above, ...), custom_call_target="tpu_custom_call" | custom-call | tf_op jit(solution)/shard_map/pallas_call | solution.py:447
  20.9 1.5 %collective-permute-start.2 = (f32[52,8,128]{2,1,0:T(8,128)S(1)}, f32[52,8,128]{2,1,0:T(8,128)S(1)}, u32[]{:S(2)}, u32[]{:S(2)}) collective-permute-start(f32[52,8,128]{2,1,0:T(8,128)S(1)} %get-tuple-element.27), channel_id=1, source_target_pairs={{0,32},{1,0},{2,34},{3,2},{4,36},{5,4},{6,38},{7,6},{8,40},{9,8},{... | collective-permute-start | bytes 638984 | tf_op jit(solution)/shard_map/ppermute | solution.py:414
  22.4 0.5 %collective-permute-start.3 = (f32[52,8,128]{2,1,0:T(8,128)S(1)}, f32[52,8,128]{2,1,0:T(8,128)S(1)}, u32[]{:S(2)}, u32[]{:S(2)}) collective-permute-start(f32[52,8,128]{2,1,0:T(8,128)S(1)} %get-tuple-element.28), channel_id=1, source_target_pairs={{32,0},{0,1},{34,2},{2,3},{36,4},{4,5},{38,6},{6,7},{40,8},{8,9},{... | collective-permute-start | bytes 638984 | tf_op jit(solution)/shard_map/ppermute | solution.py:414
  23.0 0.2 shard_map.61
  23.2 4.2 %collective-permute-done.2.ahead = f32[52,8,128]{2,1,0:T(8,128)S(1)} collective-permute-done((f32[52,8,128]{2,1,0:T(8,128)S(1)}, f32[52,8,128]{2,1,0:T(8,128)S(1)}, u32[]{:S(2)}, u32[]{:S(2)}) %collective-permute-start.2) | collective-permute-done | bytes 213024 | tf_op jit(solution)/shard_map/ppermute | solution.py:414
  27.4 0.9 %collective-permute-done.3.back = f32[52,8,128]{2,1,0:T(8,128)S(1)} collective-permute-done((f32[52,8,128]{2,1,0:T(8,128)S(1)}, f32[52,8,128]{2,1,0:T(8,128)S(1)}, u32[]{:S(2)}, u32[]{:S(2)}) %collective-permute-start.3) | collective-permute-done | bytes 213024 | tf_op jit(solution)/shard_map/ppermute | solution.py:414
  28.3 0.4 shard_map.62
  28.7 2.8 %collective-permute-start.4 = (f32[10,8,128]{2,1,0:T(8,128)S(1)}, f32[10,8,128]{2,1,0:T(8,128)S(1)}, u32[]{:S(2)}, u32[]{:S(2)}) collective-permute-start(f32[10,8,128]{2,1,0:T(8,128)S(1)} %get-tuple-element.33), channel_id=1, source_target_pairs={{0,128},{1,0},{2,130},{3,2},{4,132},{5,4},{6,134},{7,6},{8,136},{9... | collective-permute-start | bytes 122888 | tf_op jit(solution)/shard_map/ppermute | solution.py:414
  31.5 0.0 collective-permute-start.5
  31.5 1.1 %shard_map.63 = (f32[19,12,8,128]{3,2,1,0:T(8,128)S(1)}, f32[19,8,128]{2,1,0:T(8,128)S(1)}) custom-call(f32[19,16,8,128]{3,2,1,0:T(8,128)S(1)} %get-tuple-element.29.main), custom_call_target="tpu_custom_call" | custom-call | tf_op jit(solution)/shard_map/pallas_call | solution.py:463
  32.7 0.5 %collective-permute-done.4.ahead = f32[10,8,128]{2,1,0:T(8,128)S(1)} collective-permute-done((f32[10,8,128]{2,1,0:T(8,128)S(1)}, f32[10,8,128]{2,1,0:T(8,128)S(1)}, u32[]{:S(2)}, u32[]{:S(2)}) %collective-permute-start.4) | collective-permute-done | bytes 40992 | tf_op jit(solution)/shard_map/ppermute | solution.py:414
  33.2 3.5 %collective-permute-done.5.back = f32[10,8,128]{2,1,0:T(8,128)S(1)} collective-permute-done((f32[10,8,128]{2,1,0:T(8,128)S(1)}, f32[10,8,128]{2,1,0:T(8,128)S(1)}, u32[]{:S(2)}, u32[]{:S(2)}) %collective-permute-start.5) | collective-permute-done | bytes 40992 | tf_op jit(solution)/shard_map/ppermute | solution.py:414
  36.8 0.7 %shard_map.64 = (f32[2176,128]{1,0:T(8,128)S(1)}, f32[43,8,128]{2,1,0:T(8,128)S(1)}, f32[43,8,128]{2,1,0:T(8,128)S(1)}) custom-call(f32[19,12,8,128]{3,2,1,0:T(8,128)S(1)} %get-tuple-element.30.inner, f32[19,8,128]{2,1,0:T(8,128)S(1)} %get-tuple-element.31.inner_edge, f32[19,8,128]{2,1,0:T(8,128)S(1)} %get-tuple-element.32.edge, ...), custom_call_target="tpu_custom_call" | custom-call | tf_op jit(solution)/shard_map/pallas_call | solution.py:469
  37.5 0.0 collective-permute-start.6
  37.5 2.9 %collective-permute-start.7 = (f32[43,8,128]{2,1,0:T(8,128)S(1)}, f32[43,8,128]{2,1,0:T(8,128)S(1)}, u32[]{:S(2)}, u32[]{:S(2)}) collective-permute-start(f32[43,8,128]{2,1,0:T(8,128)S(1)} %get-tuple-element.37), channel_id=1, source_target_pairs={{1,0},{2,1},{3,2},{4,3},{5,4},{6,5},{7,6},{8,7},{9,8},{10,9},{11,1... | collective-permute-start | bytes 528392 | tf_op jit(solution)/shard_map/ppermute | solution.py:398
  40.4 3.1 %collective-permute-done.6.below = f32[43,8,128]{2,1,0:T(8,128)S(1)} collective-permute-done((f32[43,8,128]{2,1,0:T(8,128)S(1)}, f32[43,8,128]{2,1,0:T(8,128)S(1)}, u32[]{:S(2)}, u32[]{:S(2)}) %collective-permute-start.6) | collective-permute-done | bytes 176160 | tf_op jit(solution)/shard_map/ppermute | solution.py:398
  43.6 0.0 collective-permute-done.7.above
  43.6 1.8 %shard_map.65 = (f32[19,4,8,128]{3,2,1,0:T(8,128)}, f32[1,2]{1,0:T(1,128)}, f32[2176,128]{1,0:T(8,128)S(1)}) custom-call(f32[2176,128]{1,0:T(8,128)S(1)} %get-tuple-element.35.flat_in, f32[43,8,128]{2,1,0:T(8,128)S(1)} %collective-permute-done.6.below, f32[43,8,128]{2,1,0:T(8,128)S(1)} %collective-permute-done.7.above, ...), custom_call_target="tpu_custom_call", output_to_operand_aliasing={{2}: (0, {})} | custom-call | tf_op jit(solution)/shard_map/pallas_call | solution.py:475
Async XLA Ops:
  1.7 18.8 %collective-permute-start.1 = (f32[20,2,8,128]{3,2,1,0:T(8,128)S(1)}, f32[20,2,8,128]{3,2,1,0:T(8,128)S(1)}, u32[]{:S(2)}, u32[]{:S(2)}) collective-permute-start(f32[20,2,8,128]{3,2,1,0:T(8,128)S(1)} %get-tuple-element.21.high), channel_id=1, source_target_pairs={{0,1},{1,2},{2,3},{3,4},{4,5},{5,6},{6,7},{7,8},{8,9},{9,10},{10,1... | collective-permute-start | bytes 491528 | tf_op jit(solution)/shard_map/ppermute | solution.py:398
  1.7 18.7 %collective-permute-start = (f32[20,2,8,128]{3,2,1,0:T(8,128)S(1)}, f32[20,2,8,128]{3,2,1,0:T(8,128)S(1)}, u32[]{:S(2)}, u32[]{:S(2)}) collective-permute-start(f32[20,2,8,128]{3,2,1,0:T(8,128)S(1)} %get-tuple-element.22.low), channel_id=1, source_target_pairs={{1,0},{2,1},{3,2},{4,3},{5,4},{6,5},{7,6},{8,7},{9,8},{10,9},{11,1... | collective-permute-start | bytes 491528 | tf_op jit(solution)/shard_map/ppermute | solution.py:398
  20.9 6.5 %collective-permute-start.2 = (f32[52,8,128]{2,1,0:T(8,128)S(1)}, f32[52,8,128]{2,1,0:T(8,128)S(1)}, u32[]{:S(2)}, u32[]{:S(2)}) collective-permute-start(f32[52,8,128]{2,1,0:T(8,128)S(1)} %get-tuple-element.27), channel_id=1, source_target_pairs={{0,32},{1,0},{2,34},{3,2},{4,36},{5,4},{6,38},{7,6},{8,40},{9,8},{... | collective-permute-start | bytes 638984 | tf_op jit(solution)/shard_map/ppermute | solution.py:414
  22.4 5.8 %collective-permute-start.3 = (f32[52,8,128]{2,1,0:T(8,128)S(1)}, f32[52,8,128]{2,1,0:T(8,128)S(1)}, u32[]{:S(2)}, u32[]{:S(2)}) collective-permute-start(f32[52,8,128]{2,1,0:T(8,128)S(1)} %get-tuple-element.28), channel_id=1, source_target_pairs={{32,0},{0,1},{34,2},{2,3},{36,4},{4,5},{38,6},{6,7},{40,8},{8,9},{... | collective-permute-start | bytes 638984 | tf_op jit(solution)/shard_map/ppermute | solution.py:414
  28.7 4.5 %collective-permute-start.4 = (f32[10,8,128]{2,1,0:T(8,128)S(1)}, f32[10,8,128]{2,1,0:T(8,128)S(1)}, u32[]{:S(2)}, u32[]{:S(2)}) collective-permute-start(f32[10,8,128]{2,1,0:T(8,128)S(1)} %get-tuple-element.33), channel_id=1, source_target_pairs={{0,128},{1,0},{2,130},{3,2},{4,132},{5,4},{6,134},{7,6},{8,136},{9... | collective-permute-start | bytes 122888 | tf_op jit(solution)/shard_map/ppermute | solution.py:414
  31.5 5.2 %collective-permute-start.5 = (f32[10,8,128]{2,1,0:T(8,128)S(1)}, f32[10,8,128]{2,1,0:T(8,128)S(1)}, u32[]{:S(2)}, u32[]{:S(2)}) collective-permute-start(f32[10,8,128]{2,1,0:T(8,128)S(1)} %get-tuple-element.34), channel_id=1, source_target_pairs={{128,0},{0,1},{130,2},{2,3},{132,4},{4,5},{134,6},{6,7},{136,8},{8... | collective-permute-start | bytes 122888 | tf_op jit(solution)/shard_map/ppermute | solution.py:414
  37.5 6.1 %collective-permute-start.6 = (f32[43,8,128]{2,1,0:T(8,128)S(1)}, f32[43,8,128]{2,1,0:T(8,128)S(1)}, u32[]{:S(2)}, u32[]{:S(2)}) collective-permute-start(f32[43,8,128]{2,1,0:T(8,128)S(1)} %get-tuple-element.36), channel_id=1, source_target_pairs={{0,1},{1,2},{2,3},{3,4},{4,5},{5,6},{6,7},{7,8},{8,9},{9,10},{10,1... | collective-permute-start | bytes 528392 | tf_op jit(solution)/shard_map/ppermute | solution.py:398
  37.5 6.1 %collective-permute-start.7 = (f32[43,8,128]{2,1,0:T(8,128)S(1)}, f32[43,8,128]{2,1,0:T(8,128)S(1)}, u32[]{:S(2)}, u32[]{:S(2)}) collective-permute-start(f32[43,8,128]{2,1,0:T(8,128)S(1)} %get-tuple-element.37), channel_id=1, source_target_pairs={{1,0},{2,1},{3,2},{4,3},{5,4},{6,5},{7,6},{8,7},{9,8},{10,9},{11,1... | collective-permute-start | bytes 528392 | tf_op jit(solution)/shard_map/ppermute | solution.py:398

commit v9 on v8

--- a/solution.py
+++ b/solution.py
@@ -276,30 +276,40 @@
         edge[i] = gather_columns(out[i, 0], [out[i, k] for k in range(12)], range(2, 14))
 
 
-def patch_two_steps(inner, inner_edge, edge, ahead, back, flat, below, above):
-    up = lax.axis_index("gz") % 2 == 0
+def side_two_steps(edge, message, at_low_end):
     place = lax.axis_index("gx")
-    at_low = place == 0
-    at_high = place == lax.axis_size("gx") - 1
+    outside = place == jnp.where(at_low_end, 0, lax.axis_size("gx") - 1)
+    low_side = lanes() % 8 < 4
+    values = []
+    for i in range(Q):
+        beside = message[i % 10]
+        if i >= 10:
+            beside = jnp.where(at_low_end, roll(beside, 0, -4), roll(beside, 0, 4))
+        beside = jnp.where(outside, SOLID, beside)
+        low = jnp.where(at_low_end, beside, edge[i])
+        high = jnp.where(at_low_end, edge[i], beside)
+        values.append(jnp.where(low_side, low, high))
+    for step in range(2):
+        wet = values[0] != SOLID
+        values = relax_wet(stream_patch(values), wet)
+    return values
+
+
+def first_side(edge, ahead, side):
+    values = side_two_steps(edge, ahead, lax.rem(lax.axis_index("gz"), 2) == 0)
+    for i in range(Q):
+        side[i] = values[i]
+
+
+def patch_two_steps(inner, inner_edge, edge, side_ahead, back, flat, z_low, z_high):
+    up = lax.rem(lax.axis_index("gz"), 2) == 0
     column = lanes() % 8
     low_side = column < 4
-    sides = []
-    for side in range(2):
-        values = []
-        for i in range(Q):
-            message = jnp.where(up == (side == 0), ahead[i % 10], back[i % 10])
-            if i >= 10:
-                message = roll(message, 0, (-4, 4)[side])
-            message = jnp.where((at_low, at_high)[side], SOLID, message)
-            if side == 0:
-                values.append(jnp.where(low_side, message, edge[i]))
-            else:
-                values.append(jnp.where(low_side, edge[i], message))
-        sides.append(values)
-    for step in range(2):
-        for side in range(2):
-            wet = sides[side][0] != SOLID
-            sides[side] = relax_wet(stream_patch(sides[side]), wet)
+    other = side_two_steps(edge, back, jnp.logical_not(up))
+    sides = [
+        [jnp.where(up, side_ahead[i], other[i]) for i in range(Q)],
+        [jnp.where(up, other[i], side_ahead[i]) for i in range(Q)],
+    ]
     lane = lanes()
     seam = (lane < 2) | (lane >= 126)
     for i in range(Q):
@@ -315,11 +325,11 @@
             flat[at : at + 8] = jnp.where(stale, sides[side][i], fresh)
     flat[8 * PER_SLOT * Q :] = jnp.full((FLAT_ROWS - 8 * PER_SLOT * Q, 128), SOLID, F32)
     for group in range(NEAR):
-        above[group] = flat[pl.ds(64 * group + 5, 8, stride=8)]
-        below[group] = flat[pl.ds(64 * group + 2, 8, stride=8)]
+        z_high[group] = flat[pl.ds(64 * group + 5, 8, stride=8)]
+        z_low[group] = flat[pl.ds(64 * group + 2, 8, stride=8)]
     for group in range(FAR):
-        above[NEAR + group] = flat[pl.ds(64 * group + 4, 8, stride=8)]
-        below[NEAR + group] = flat[pl.ds(8 * 5 * PER_SLOT + 64 * group + 3, 8, stride=8)]
+        z_high[NEAR + group] = flat[pl.ds(64 * group + 4, 8, stride=8)]
+        z_low[NEAR + group] = flat[pl.ds(8 * 5 * PER_SLOT + 64 * group + 3, 8, stride=8)]
 
 
 def last_two_steps(
@@ -466,11 +476,12 @@
         [VMEM],
         scratch=[pltpu.VMEM((Q, 14, 8, 128), F32)],
     )(main)
+    side = call(first_side, [shape(Q, 8, 128)], [VMEM] * 2)(edge, x_ahead)[0]
     flat, z_low, z_high = call(
         patch_two_steps,
         [shape(FLAT_ROWS, 128), shape(NEAR + FAR, 8, 128), shape(NEAR + FAR, 8, 128)],
         [VMEM] * 5,
-    )(inner, inner_edge, edge, x_ahead, x_back)
+    )(inner, inner_edge, edge, side, x_back)
     below, above = ring_exchange(z_low, z_high, "gz")
     out, block_density, _ = call(
         last_two_steps,

time: 45.6 us -> 45.5 us (level)
  transfers between devices with their start and end apart: 8 -> 8, of which waited for: 6 -> 6; matrix products, arithmetic and copies ran while one was open for 0% -> 0% of each run, Pallas kernels for 3% -> 4%
where the time goes in v9:
time: 45.5 us; the launch traced here: 45.4 us
  starting transfers between devices  23.6 us (52%)
  waiting for transfers between devices  15 us (33%)
  Pallas kernels  6.15 us (14%)
  between operations  0.69 us (2%)
    ppermute x4, starting transfers between devices, ring_exchange(): return (lax.ppermute(to_high, axis, up), lax.ppermute(to_low, axis, down))  18.7 us
    ppermute x4, waiting for transfers between devices, loop_exchange(): return (lax.ppermute(ahead, axes, pairs), lax.ppermute(back, axes, inverse))  8.84 us
    ppermute x4, waiting for transfers between devices, ring_exchange(): return (lax.ppermute(to_high, axis, up), lax.ppermute(to_low, axis, down))  6.11 us
    ppermute x4, starting transfers between devices, loop_exchange(): return (lax.ppermute(ahead, axes, pairs), lax.ppermute(back, axes, inverse))  4.85 us
    pallas_call x1, Pallas kernels, on_device(): call(last_two_steps, [shape(Q, 4, 8, 128), shape(1, 2), shape(FLAT_ROWS,...  1.84 us
    pallas_call x1, Pallas kernels, on_device(): call(two_steps, [shape(Q, 12, 8, 128), shape(Q, 8, 128)], [VMEM], scratch...  1.14 us
    pallas_call x1, Pallas kernels, on_device(): call(split_slabs, [shape(Q + 1, 2, 8, 128), shape(Q + 1, 2, 8, 128), shap...  1.04 us
  transfers between devices with their start and end apart: 8, of which 6 were waited for; matrix products, arithmetic and copies ran while one was open for 0% of the time, Pallas kernels for 4%

profile of v9, /device:TPU:26, one launch (start us, length us, event | category | flops | bytes accessed | tf_op | source)
XLA Modules:
  0.0 45.4 jit_solution(10476831122881544615)
XLA Ops:
  0.6 1.0 %shard_map.59 = (f32[20,2,8,128]{3,2,1,0:T(8,128)S(1)}, f32[20,2,8,128]{3,2,1,0:T(8,128)S(1)}, f32[2,8,128]{2,1,0:T(8,128)S(1)}) custom-call(f32[19,4,8,128]{3,2,1,0:T(8,128)} %relative.1, s32[4,8,128]{2,1,0:T(8,128)} %fluid.1, s32[1,2]{1,0:T(1,128)} %bitcast.3), custom_call_target="tpu_custom_call" | custom-call | tf_op jit(solution)/shard_map/pallas_call | solution.py:446
  1.7 0.0 collective-permute-start.1
  1.7 15.8 %collective-permute-start = (f32[20,2,8,128]{3,2,1,0:T(8,128)S(1)}, f32[20,2,8,128]{3,2,1,0:T(8,128)S(1)}, u32[]{:S(2)}, u32[]{:S(2)}) collective-permute-start(f32[20,2,8,128]{3,2,1,0:T(8,128)S(1)} %get-tuple-element.22.low), channel_id=1, source_target_pairs={{1,0},{2,1},{3,2},{4,3},{5,4},{6,5},{7,6},{8,7},{9,8},{10,9},{11,1... | collective-permute-start | bytes 491528 | tf_op jit(solution)/shard_map/ppermute | solution.py:408
  17.5 3.0 %collective-permute-done.1.below = f32[20,2,8,128]{3,2,1,0:T(8,128)S(1)} collective-permute-done((f32[20,2,8,128]{3,2,1,0:T(8,128)S(1)}, f32[20,2,8,128]{3,2,1,0:T(8,128)S(1)}, u32[]{:S(2)}, u32[]{:S(2)}) %collective-permute-start.1) | collective-permute-done | bytes 163872 | tf_op jit(solution)/shard_map/ppermute | solution.py:408
  20.5 0.0 collective-permute-done.above
  20.5 0.5 %shard_map.60 = (f32[19,8,8,128]{3,2,1,0:T(8,128)S(1)}, f32[52,8,128]{2,1,0:T(8,128)S(1)}, f32[52,8,128]{2,1,0:T(8,128)S(1)}) custom-call(f32[20,2,8,128]{3,2,1,0:T(8,128)S(1)} %get-tuple-element.21.high, f32[20,2,8,128]{3,2,1,0:T(8,128)S(1)} %get-tuple-element.22.low, f32[20,2,8,128]{3,2,1,0:T(8,128)S(1)} %collective-permute-done.above, ...), custom_call_target="tpu_custom_call" | custom-call | tf_op jit(solution)/shard_map/pallas_call | solution.py:457
  20.9 1.5 %collective-permute-start.2 = (f32[52,8,128]{2,1,0:T(8,128)S(1)}, f32[52,8,128]{2,1,0:T(8,128)S(1)}, u32[]{:S(2)}, u32[]{:S(2)}) collective-permute-start(f32[52,8,128]{2,1,0:T(8,128)S(1)} %get-tuple-element.27), channel_id=1, source_target_pairs={{0,32},{1,0},{2,34},{3,2},{4,36},{5,4},{6,38},{7,6},{8,40},{9,8},{... | collective-permute-start | bytes 638984 | tf_op jit(solution)/shard_map/ppermute | solution.py:424
  22.4 0.5 %collective-permute-start.3 = (f32[52,8,128]{2,1,0:T(8,128)S(1)}, f32[52,8,128]{2,1,0:T(8,128)S(1)}, u32[]{:S(2)}, u32[]{:S(2)}) collective-permute-start(f32[52,8,128]{2,1,0:T(8,128)S(1)} %get-tuple-element.28), channel_id=1, source_target_pairs={{32,0},{0,1},{34,2},{2,3},{36,4},{4,5},{38,6},{6,7},{40,8},{8,9},{... | collective-permute-start | bytes 638984 | tf_op jit(solution)/shard_map/ppermute | solution.py:424
  23.0 0.2 shard_map.61
  23.2 4.2 %collective-permute-done.2.ahead = f32[52,8,128]{2,1,0:T(8,128)S(1)} collective-permute-done((f32[52,8,128]{2,1,0:T(8,128)S(1)}, f32[52,8,128]{2,1,0:T(8,128)S(1)}, u32[]{:S(2)}, u32[]{:S(2)}) %collective-permute-start.2) | collective-permute-done | bytes 213024 | tf_op jit(solution)/shard_map/ppermute | solution.py:424
  27.4 0.9 %collective-permute-done.3.back = f32[52,8,128]{2,1,0:T(8,128)S(1)} collective-permute-done((f32[52,8,128]{2,1,0:T(8,128)S(1)}, f32[52,8,128]{2,1,0:T(8,128)S(1)}, u32[]{:S(2)}, u32[]{:S(2)}) %collective-permute-start.3) | collective-permute-done | bytes 213024 | tf_op jit(solution)/shard_map/ppermute | solution.py:424
  28.3 0.4 shard_map.62
  28.7 2.8 %collective-permute-start.4 = (f32[10,8,128]{2,1,0:T(8,128)S(1)}, f32[10,8,128]{2,1,0:T(8,128)S(1)}, u32[]{:S(2)}, u32[]{:S(2)}) collective-permute-start(f32[10,8,128]{2,1,0:T(8,128)S(1)} %get-tuple-element.33), channel_id=1, source_target_pairs={{0,128},{1,0},{2,130},{3,2},{4,132},{5,4},{6,134},{7,6},{8,136},{9... | collective-permute-start | bytes 122888 | tf_op jit(solution)/shard_map/ppermute | solution.py:424
  31.5 0.0 collective-permute-start.5
  31.5 1.1 %shard_map.63 = (f32[19,12,8,128]{3,2,1,0:T(8,128)S(1)}, f32[19,8,128]{2,1,0:T(8,128)S(1)}) custom-call(f32[19,16,8,128]{3,2,1,0:T(8,128)S(1)} %get-tuple-element.29.main), custom_call_target="tpu_custom_call" | custom-call | tf_op jit(solution)/shard_map/pallas_call | solution.py:473
  32.7 0.5 %collective-permute-done.4.ahead = f32[10,8,128]{2,1,0:T(8,128)S(1)} collective-permute-done((f32[10,8,128]{2,1,0:T(8,128)S(1)}, f32[10,8,128]{2,1,0:T(8,128)S(1)}, u32[]{:S(2)}, u32[]{:S(2)}) %collective-permute-start.4) | collective-permute-done | bytes 40992 | tf_op jit(solution)/shard_map/ppermute | solution.py:424
  33.2 0.3 shard_map.64.side_ahead
  33.5 3.2 %collective-permute-done.5.back = f32[10,8,128]{2,1,0:T(8,128)S(1)} collective-permute-done((f32[10,8,128]{2,1,0:T(8,128)S(1)}, f32[10,8,128]{2,1,0:T(8,128)S(1)}, u32[]{:S(2)}, u32[]{:S(2)}) %collective-permute-start.5) | collective-permute-done | bytes 40992 | tf_op jit(solution)/shard_map/ppermute | solution.py:424
  36.8 0.7 %shard_map.65 = (f32[2176,128]{1,0:T(8,128)S(1)}, f32[43,8,128]{2,1,0:T(8,128)S(1)}, f32[43,8,128]{2,1,0:T(8,128)S(1)}) custom-call(f32[19,12,8,128]{3,2,1,0:T(8,128)S(1)} %get-tuple-element.30.inner, f32[19,8,128]{2,1,0:T(8,128)S(1)} %get-tuple-element.31.inner_edge, f32[19,8,128]{2,1,0:T(8,128)S(1)} %get-tuple-element.32.edge, ...), custom_call_target="tpu_custom_call" | custom-call | tf_op jit(solution)/shard_map/pallas_call | solution.py:480
  37.4 0.0 collective-permute-start.6
  37.5 2.9 %collective-permute-start.7 = (f32[43,8,128]{2,1,0:T(8,128)S(1)}, f32[43,8,128]{2,1,0:T(8,128)S(1)}, u32[]{:S(2)}, u32[]{:S(2)}) collective-permute-start(f32[43,8,128]{2,1,0:T(8,128)S(1)} %get-tuple-element.37), channel_id=1, source_target_pairs={{1,0},{2,1},{3,2},{4,3},{5,4},{6,5},{7,6},{8,7},{9,8},{10,9},{11,1... | collective-permute-start | bytes 528392 | tf_op jit(solution)/shard_map/ppermute | solution.py:408
  40.4 3.1 %collective-permute-done.6.below = f32[43,8,128]{2,1,0:T(8,128)S(1)} collective-permute-done((f32[43,8,128]{2,1,0:T(8,128)S(1)}, f32[43,8,128]{2,1,0:T(8,128)S(1)}, u32[]{:S(2)}, u32[]{:S(2)}) %collective-permute-start.6) | collective-permute-done | bytes 176160 | tf_op jit(solution)/shard_map/ppermute | solution.py:408
  43.5 0.0 collective-permute-done.7.above
  43.5 1.8 %shard_map.66 = (f32[19,4,8,128]{3,2,1,0:T(8,128)}, f32[1,2]{1,0:T(1,128)}, f32[2176,128]{1,0:T(8,128)S(1)}) custom-call(f32[2176,128]{1,0:T(8,128)S(1)} %get-tuple-element.35.flat_in, f32[43,8,128]{2,1,0:T(8,128)S(1)} %collective-permute-done.6.below, f32[43,8,128]{2,1,0:T(8,128)S(1)} %collective-permute-done.7.above, ...), custom_call_target="tpu_custom_call", output_to_operand_aliasing={{2}: (0, {})} | custom-call | tf_op jit(solution)/shard_map/pallas_call | solution.py:486
Async XLA Ops:
  1.7 18.8 %collective-permute-start.1 = (f32[20,2,8,128]{3,2,1,0:T(8,128)S(1)}, f32[20,2,8,128]{3,2,1,0:T(8,128)S(1)}, u32[]{:S(2)}, u32[]{:S(2)}) collective-permute-start(f32[20,2,8,128]{3,2,1,0:T(8,128)S(1)} %get-tuple-element.21.high), channel_id=1, source_target_pairs={{0,1},{1,2},{2,3},{3,4},{4,5},{5,6},{6,7},{7,8},{8,9},{9,10},{10,1... | collective-permute-start | bytes 491528 | tf_op jit(solution)/shard_map/ppermute | solution.py:408
  1.7 18.7 %collective-permute-start = (f32[20,2,8,128]{3,2,1,0:T(8,128)S(1)}, f32[20,2,8,128]{3,2,1,0:T(8,128)S(1)}, u32[]{:S(2)}, u32[]{:S(2)}) collective-permute-start(f32[20,2,8,128]{3,2,1,0:T(8,128)S(1)} %get-tuple-element.22.low), channel_id=1, source_target_pairs={{1,0},{2,1},{3,2},{4,3},{5,4},{6,5},{7,6},{8,7},{9,8},{10,9},{11,1... | collective-permute-start | bytes 491528 | tf_op jit(solution)/shard_map/ppermute | solution.py:408
  20.9 6.5 %collective-permute-start.2 = (f32[52,8,128]{2,1,0:T(8,128)S(1)}, f32[52,8,128]{2,1,0:T(8,128)S(1)}, u32[]{:S(2)}, u32[]{:S(2)}) collective-permute-start(f32[52,8,128]{2,1,0:T(8,128)S(1)} %get-tuple-element.27), channel_id=1, source_target_pairs={{0,32},{1,0},{2,34},{3,2},{4,36},{5,4},{6,38},{7,6},{8,40},{9,8},{... | collective-permute-start | bytes 638984 | tf_op jit(solution)/shard_map/ppermute | solution.py:424
  22.4 5.8 %collective-permute-start.3 = (f32[52,8,128]{2,1,0:T(8,128)S(1)}, f32[52,8,128]{2,1,0:T(8,128)S(1)}, u32[]{:S(2)}, u32[]{:S(2)}) collective-permute-start(f32[52,8,128]{2,1,0:T(8,128)S(1)} %get-tuple-element.28), channel_id=1, source_target_pairs={{32,0},{0,1},{34,2},{2,3},{36,4},{4,5},{38,6},{6,7},{40,8},{8,9},{... | collective-permute-start | bytes 638984 | tf_op jit(solution)/shard_map/ppermute | solution.py:424
  28.7 4.5 %collective-permute-start.4 = (f32[10,8,128]{2,1,0:T(8,128)S(1)}, f32[10,8,128]{2,1,0:T(8,128)S(1)}, u32[]{:S(2)}, u32[]{:S(2)}) collective-permute-start(f32[10,8,128]{2,1,0:T(8,128)S(1)} %get-tuple-element.33), channel_id=1, source_target_pairs={{0,128},{1,0},{2,130},{3,2},{4,132},{5,4},{6,134},{7,6},{8,136},{9... | collective-permute-start | bytes 122888 | tf_op jit(solution)/shard_map/ppermute | solution.py:424
  31.5 5.2 %collective-permute-start.5 = (f32[10,8,128]{2,1,0:T(8,128)S(1)}, f32[10,8,128]{2,1,0:T(8,128)S(1)}, u32[]{:S(2)}, u32[]{:S(2)}) collective-permute-start(f32[10,8,128]{2,1,0:T(8,128)S(1)} %get-tuple-element.34), channel_id=1, source_target_pairs={{128,0},{0,1},{130,2},{2,3},{132,4},{4,5},{134,6},{6,7},{136,8},{8... | collective-permute-start | bytes 122888 | tf_op jit(solution)/shard_map/ppermute | solution.py:424
  37.4 6.1 %collective-permute-start.6 = (f32[43,8,128]{2,1,0:T(8,128)S(1)}, f32[43,8,128]{2,1,0:T(8,128)S(1)}, u32[]{:S(2)}, u32[]{:S(2)}) collective-permute-start(f32[43,8,128]{2,1,0:T(8,128)S(1)} %get-tuple-element.36), channel_id=1, source_target_pairs={{0,1},{1,2},{2,3},{3,4},{4,5},{5,6},{6,7},{7,8},{8,9},{9,10},{10,1... | collective-permute-start | bytes 528392 | tf_op jit(solution)/shard_map/ppermute | solution.py:408
  37.5 6.1 %collective-permute-start.7 = (f32[43,8,128]{2,1,0:T(8,128)S(1)}, f32[43,8,128]{2,1,0:T(8,128)S(1)}, u32[]{:S(2)}, u32[]{:S(2)}) collective-permute-start(f32[43,8,128]{2,1,0:T(8,128)S(1)} %get-tuple-element.37), channel_id=1, source_target_pairs={{1,0},{2,1},{3,2},{4,3},{5,4},{6,5},{7,6},{8,7},{9,8},{10,9},{11,1... | collective-permute-start | bytes 528392 | tf_op jit(solution)/shard_map/ppermute | solution.py:408

commit v10 on v9

--- a/solution.py
+++ b/solution.py
@@ -257,7 +257,7 @@
             x_back[i] = edges[i]
 
 
-def two_steps(main, out, edge, middle):
+def two_steps(main, flat, edge, middle):
     def first(row):
         values = relax_row(lambda i, at: main[i, at], row)
         for i in range(Q):
@@ -266,14 +266,18 @@
     def second(row):
         values = relax_row(lambda i, at: middle[i, at], row - 1)
         for i in range(Q):
-            out[i, row - 2] = values[i]
+            at = 8 * (PER_SLOT * SLOT[i] + row - 2)
+            flat[at : at + 8] = values[i]
 
     for row in range(1, 15):
         first(row)
     for row in range(2, 14):
         second(row)
     for i in range(Q):
-        edge[i] = gather_columns(out[i, 0], [out[i, k] for k in range(12)], range(2, 14))
+        at = 8 * PER_SLOT * SLOT[i]
+        rows = [flat[at + 8 * k : at + 8 * k + 8] for k in range(12)]
+        edge[i] = gather_columns(rows[0], rows, range(2, 14))
+    flat[8 * PER_SLOT * Q :] = jnp.full((FLAT_ROWS - 8 * PER_SLOT * Q, 128), SOLID, F32)
 
 
 def side_two_steps(edge, message, at_low_end):
@@ -301,7 +305,7 @@
         side[i] = values[i]
 
 
-def patch_two_steps(inner, inner_edge, edge, side_ahead, back, flat, z_low, z_high):
+def patch_two_steps(flat_in, inner_edge, edge, side_ahead, back, flat, z_low, z_high):
     up = lax.rem(lax.axis_index("gz"), 2) == 0
     column = lanes() % 8
     low_side = column < 4
@@ -316,14 +320,13 @@
         own_columns = jnp.where(low_side, sides[1][i], sides[0][i])
         first = PER_SLOT * SLOT[i]
         for row in range(12):
-            value = jnp.where(seam, roll(own_columns, 0, -(8 * (row + 2) + 4)), inner[i, row])
-            flat[8 * (first + row) : 8 * (first + row) + 8] = value
+            value = roll(own_columns, 0, -(8 * (row + 2) + 4))
+            pltpu.store(flat.at[8 * (first + row) : 8 * (first + row) + 8], value, mask=seam)
         fresh = inner_edge[i]
         for side in range(2):
             stale = (column < 6) if side == 0 else (column >= 2)
             at = 8 * (first + 12 + side)
             flat[at : at + 8] = jnp.where(stale, sides[side][i], fresh)
-    flat[8 * PER_SLOT * Q :] = jnp.full((FLAT_ROWS - 8 * PER_SLOT * Q, 128), SOLID, F32)
     for group in range(NEAR):
         z_high[group] = flat[pl.ds(64 * group + 5, 8, stride=8)]
         z_low[group] = flat[pl.ds(64 * group + 2, 8, stride=8)]
@@ -470,9 +473,9 @@
         aliases={0: 0, 1: 1},
     )(main, edge, ahead, back)
     x_ahead, x_back = loop_exchange(x_ahead, x_back, "gx")
-    inner, inner_edge = call(
+    flat, inner_edge = call(
         two_steps,
-        [shape(Q, 12, 8, 128), shape(Q, 8, 128)],
+        [shape(FLAT_ROWS, 128), shape(Q, 8, 128)],
         [VMEM],
         scratch=[pltpu.VMEM((Q, 14, 8, 128), F32)],
     )(main)
@@ -481,7 +484,8 @@
         patch_two_steps,
         [shape(FLAT_ROWS, 128), shape(NEAR + FAR, 8, 128), shape(NEAR + FAR, 8, 128)],
         [VMEM] * 5,
-    )(inner, inner_edge, edge, side, x_back)
+        aliases={0: 0},
+    )(flat, inner_edge, edge, side, x_back)
     below, above = ring_exchange(z_low, z_high, "gz")
     out, block_density, _ = call(
         last_two_steps,

time: 45.5 us -> 45.5 us (level)
  no operation moved by 1% of the time
where the time goes in v10:
time: 45.5 us; the launch traced here: 45.4 us
  starting transfers between devices  23.6 us (52%)
  waiting for transfers between devices  15 us (33%)
  Pallas kernels  6.15 us (14%)
  between operations  0.69 us (2%)
    ppermute x4, starting transfers between devices, ring_exchange(): return (lax.ppermute(to_high, axis, up), lax.ppermute(to_low, axis, down))  18.7 us
    ppermute x4, waiting for transfers between devices, loop_exchange(): return (lax.ppermute(ahead, axes, pairs), lax.ppermute(back, axes, inverse))  8.84 us
    ppermute x4, waiting for transfers between devices, ring_exchange(): return (lax.ppermute(to_high, axis, up), lax.ppermute(to_low, axis, down))  6.11 us
    ppermute x4, starting transfers between devices, loop_exchange(): return (lax.ppermute(ahead, axes, pairs), lax.ppermute(back, axes, inverse))  4.85 us
    pallas_call x1, Pallas kernels, on_device(): call(last_two_steps, [shape(Q, 4, 8, 128), shape(1, 2), shape(FLAT_ROWS,...  1.85 us
    pallas_call x1, Pallas kernels, on_device(): call(two_steps, [shape(FLAT_ROWS, 128), shape(Q, 8, 128)], [VMEM], scratc...  1.14 us
    pallas_call x1, Pallas kernels, on_device(): call(split_slabs, [shape(Q + 1, 2, 8, 128), shape(Q + 1, 2, 8, 128), shap...  1.04 us
  transfers between devices with their start and end apart: 8, of which 6 were waited for; matrix products, arithmetic and copies ran while one was open for 0% of the time, Pallas kernels for 4%

profile of v10, /device:TPU:26, one launch (start us, length us, event | category | flops | bytes accessed | tf_op | source)
XLA Modules:
  0.0 45.4 jit_solution(4258358886359790903)
XLA Ops:
  0.6 1.0 %shard_map.59 = (f32[20,2,8,128]{3,2,1,0:T(8,128)S(1)}, f32[20,2,8,128]{3,2,1,0:T(8,128)S(1)}, f32[2,8,128]{2,1,0:T(8,128)S(1)}) custom-call(f32[19,4,8,128]{3,2,1,0:T(8,128)} %relative.1, s32[4,8,128]{2,1,0:T(8,128)} %fluid.1, s32[1,2]{1,0:T(1,128)} %bitcast.3), custom_call_target="tpu_custom_call" | custom-call | tf_op jit(solution)/shard_map/pallas_call | solution.py:449
  1.7 0.0 collective-permute-start.1
  1.7 15.8 %collective-permute-start = (f32[20,2,8,128]{3,2,1,0:T(8,128)S(1)}, f32[20,2,8,128]{3,2,1,0:T(8,128)S(1)}, u32[]{:S(2)}, u32[]{:S(2)}) collective-permute-start(f32[20,2,8,128]{3,2,1,0:T(8,128)S(1)} %get-tuple-element.22.low), channel_id=1, source_target_pairs={{1,0},{2,1},{3,2},{4,3},{5,4},{6,5},{7,6},{8,7},{9,8},{10,9},{11,1... | collective-permute-start | bytes 491528 | tf_op jit(solution)/shard_map/ppermute | solution.py:411
  17.5 3.0 %collective-permute-done.1.below = f32[20,2,8,128]{3,2,1,0:T(8,128)S(1)} collective-permute-done((f32[20,2,8,128]{3,2,1,0:T(8,128)S(1)}, f32[20,2,8,128]{3,2,1,0:T(8,128)S(1)}, u32[]{:S(2)}, u32[]{:S(2)}) %collective-permute-start.1) | collective-permute-done | bytes 163872 | tf_op jit(solution)/shard_map/ppermute | solution.py:411
  20.5 0.0 collective-permute-done.above
  20.5 0.5 %shard_map.60 = (f32[19,8,8,128]{3,2,1,0:T(8,128)S(1)}, f32[52,8,128]{2,1,0:T(8,128)S(1)}, f32[52,8,128]{2,1,0:T(8,128)S(1)}) custom-call(f32[20,2,8,128]{3,2,1,0:T(8,128)S(1)} %get-tuple-element.21.high, f32[20,2,8,128]{3,2,1,0:T(8,128)S(1)} %get-tuple-element.22.low, f32[20,2,8,128]{3,2,1,0:T(8,128)S(1)} %collective-permute-done.above, ...), custom_call_target="tpu_custom_call" | custom-call | tf_op jit(solution)/shard_map/pallas_call | solution.py:460
  20.9 1.5 %collective-permute-start.2 = (f32[52,8,128]{2,1,0:T(8,128)S(1)}, f32[52,8,128]{2,1,0:T(8,128)S(1)}, u32[]{:S(2)}, u32[]{:S(2)}) collective-permute-start(f32[52,8,128]{2,1,0:T(8,128)S(1)} %get-tuple-element.27), channel_id=1, source_target_pairs={{0,32},{1,0},{2,34},{3,2},{4,36},{5,4},{6,38},{7,6},{8,40},{9,8},{... | collective-permute-start | bytes 638984 | tf_op jit(solution)/shard_map/ppermute | solution.py:427
  22.4 0.5 %collective-permute-start.3 = (f32[52,8,128]{2,1,0:T(8,128)S(1)}, f32[52,8,128]{2,1,0:T(8,128)S(1)}, u32[]{:S(2)}, u32[]{:S(2)}) collective-permute-start(f32[52,8,128]{2,1,0:T(8,128)S(1)} %get-tuple-element.28), channel_id=1, source_target_pairs={{32,0},{0,1},{34,2},{2,3},{36,4},{4,5},{38,6},{6,7},{40,8},{8,9},{... | collective-permute-start | bytes 638984 | tf_op jit(solution)/shard_map/ppermute | solution.py:427
  23.0 0.2 shard_map.61
  23.2 4.2 %collective-permute-done.2.ahead = f32[52,8,128]{2,1,0:T(8,128)S(1)} collective-permute-done((f32[52,8,128]{2,1,0:T(8,128)S(1)}, f32[52,8,128]{2,1,0:T(8,128)S(1)}, u32[]{:S(2)}, u32[]{:S(2)}) %collective-permute-start.2) | collective-permute-done | bytes 213024 | tf_op jit(solution)/shard_map/ppermute | solution.py:427
  27.4 0.9 %collective-permute-done.3.back = f32[52,8,128]{2,1,0:T(8,128)S(1)} collective-permute-done((f32[52,8,128]{2,1,0:T(8,128)S(1)}, f32[52,8,128]{2,1,0:T(8,128)S(1)}, u32[]{:S(2)}, u32[]{:S(2)}) %collective-permute-start.3) | collective-permute-done | bytes 213024 | tf_op jit(solution)/shard_map/ppermute | solution.py:427
  28.3 0.4 shard_map.62
  28.7 2.8 %collective-permute-start.4 = (f32[10,8,128]{2,1,0:T(8,128)S(1)}, f32[10,8,128]{2,1,0:T(8,128)S(1)}, u32[]{:S(2)}, u32[]{:S(2)}) collective-permute-start(f32[10,8,128]{2,1,0:T(8,128)S(1)} %get-tuple-element.33), channel_id=1, source_target_pairs={{0,128},{1,0},{2,130},{3,2},{4,132},{5,4},{6,134},{7,6},{8,136},{9... | collective-permute-start | bytes 122888 | tf_op jit(solution)/shard_map/ppermute | solution.py:427
  31.5 0.0 collective-permute-start.5
  31.5 1.1 %shard_map.63 = (f32[2176,128]{1,0:T(8,128)S(1)}, f32[19,8,128]{2,1,0:T(8,128)S(1)}) custom-call(f32[19,16,8,128]{3,2,1,0:T(8,128)S(1)} %get-tuple-element.29.main), custom_call_target="tpu_custom_call" | custom-call | tf_op jit(solution)/shard_map/pallas_call | solution.py:476
  32.7 0.5 %collective-permute-done.4.ahead = f32[10,8,128]{2,1,0:T(8,128)S(1)} collective-permute-done((f32[10,8,128]{2,1,0:T(8,128)S(1)}, f32[10,8,128]{2,1,0:T(8,128)S(1)}, u32[]{:S(2)}, u32[]{:S(2)}) %collective-permute-start.4) | collective-permute-done | bytes 40992 | tf_op jit(solution)/shard_map/ppermute | solution.py:427
  33.2 0.3 shard_map.64.side_ahead
  33.5 3.2 %collective-permute-done.5.back = f32[10,8,128]{2,1,0:T(8,128)S(1)} collective-permute-done((f32[10,8,128]{2,1,0:T(8,128)S(1)}, f32[10,8,128]{2,1,0:T(8,128)S(1)}, u32[]{:S(2)}, u32[]{:S(2)}) %collective-permute-start.5) | collective-permute-done | bytes 40992 | tf_op jit(solution)/shard_map/ppermute | solution.py:427
  36.8 0.7 %shard_map.65 = (f32[2176,128]{1,0:T(8,128)S(1)}, f32[43,8,128]{2,1,0:T(8,128)S(1)}, f32[43,8,128]{2,1,0:T(8,128)S(1)}) custom-call(f32[2176,128]{1,0:T(8,128)S(1)} %get-tuple-element.30.flat_in, f32[19,8,128]{2,1,0:T(8,128)S(1)} %get-tuple-element.31.inner_edge, f32[19,8,128]{2,1,0:T(8,128)S(1)} %get-tuple-element.32.edge, ...), custom_call_target="tpu_custom_call", output_to_operand_aliasing={{0}: (0, {})} | custom-call | tf_op jit(solution)/shard_map/pallas_call | solution.py:483
  37.4 0.0 collective-permute-start.6
  37.5 2.9 %collective-permute-start.7 = (f32[43,8,128]{2,1,0:T(8,128)S(1)}, f32[43,8,128]{2,1,0:T(8,128)S(1)}, u32[]{:S(2)}, u32[]{:S(2)}) collective-permute-start(f32[43,8,128]{2,1,0:T(8,128)S(1)} %get-tuple-element.37), channel_id=1, source_target_pairs={{1,0},{2,1},{3,2},{4,3},{5,4},{6,5},{7,6},{8,7},{9,8},{10,9},{11,1... | collective-permute-start | bytes 528392 | tf_op jit(solution)/shard_map/ppermute | solution.py:411
  40.4 3.1 %collective-permute-done.6.below = f32[43,8,128]{2,1,0:T(8,128)S(1)} collective-permute-done((f32[43,8,128]{2,1,0:T(8,128)S(1)}, f32[43,8,128]{2,1,0:T(8,128)S(1)}, u32[]{:S(2)}, u32[]{:S(2)}) %collective-permute-start.6) | collective-permute-done | bytes 176160 | tf_op jit(solution)/shard_map/ppermute | solution.py:411
  43.5 0.0 collective-permute-done.7.above
  43.5 1.9 %shard_map.66 = (f32[19,4,8,128]{3,2,1,0:T(8,128)}, f32[1,2]{1,0:T(1,128)}, f32[2176,128]{1,0:T(8,128)S(1)}) custom-call(f32[2176,128]{1,0:T(8,128)S(1)} %get-tuple-element.35.flat_in, f32[43,8,128]{2,1,0:T(8,128)S(1)} %collective-permute-done.6.below, f32[43,8,128]{2,1,0:T(8,128)S(1)} %collective-permute-done.7.above, ...), custom_call_target="tpu_custom_call", output_to_operand_aliasing={{2}: (0, {})} | custom-call | tf_op jit(solution)/shard_map/pallas_call | solution.py:490
Async XLA Ops:
  1.7 18.8 %collective-permute-start.1 = (f32[20,2,8,128]{3,2,1,0:T(8,128)S(1)}, f32[20,2,8,128]{3,2,1,0:T(8,128)S(1)}, u32[]{:S(2)}, u32[]{:S(2)}) collective-permute-start(f32[20,2,8,128]{3,2,1,0:T(8,128)S(1)} %get-tuple-element.21.high), channel_id=1, source_target_pairs={{0,1},{1,2},{2,3},{3,4},{4,5},{5,6},{6,7},{7,8},{8,9},{9,10},{10,1... | collective-permute-start | bytes 491528 | tf_op jit(solution)/shard_map/ppermute | solution.py:411
  1.7 18.7 %collective-permute-start = (f32[20,2,8,128]{3,2,1,0:T(8,128)S(1)}, f32[20,2,8,128]{3,2,1,0:T(8,128)S(1)}, u32[]{:S(2)}, u32[]{:S(2)}) collective-permute-start(f32[20,2,8,128]{3,2,1,0:T(8,128)S(1)} %get-tuple-element.22.low), channel_id=1, source_target_pairs={{1,0},{2,1},{3,2},{4,3},{5,4},{6,5},{7,6},{8,7},{9,8},{10,9},{11,1... | collective-permute-start | bytes 491528 | tf_op jit(solution)/shard_map/ppermute | solution.py:411
  20.9 6.5 %collective-permute-start.2 = (f32[52,8,128]{2,1,0:T(8,128)S(1)}, f32[52,8,128]{2,1,0:T(8,128)S(1)}, u32[]{:S(2)}, u32[]{:S(2)}) collective-permute-start(f32[52,8,128]{2,1,0:T(8,128)S(1)} %get-tuple-element.27), channel_id=1, source_target_pairs={{0,32},{1,0},{2,34},{3,2},{4,36},{5,4},{6,38},{7,6},{8,40},{9,8},{... | collective-permute-start | bytes 638984 | tf_op jit(solution)/shard_map/ppermute | solution.py:427
  22.4 5.8 %collective-permute-start.3 = (f32[52,8,128]{2,1,0:T(8,128)S(1)}, f32[52,8,128]{2,1,0:T(8,128)S(1)}, u32[]{:S(2)}, u32[]{:S(2)}) collective-permute-start(f32[52,8,128]{2,1,0:T(8,128)S(1)} %get-tuple-element.28), channel_id=1, source_target_pairs={{32,0},{0,1},{34,2},{2,3},{36,4},{4,5},{38,6},{6,7},{40,8},{8,9},{... | collective-permute-start | bytes 638984 | tf_op jit(solution)/shard_map/ppermute | solution.py:427
  28.7 4.5 %collective-permute-start.4 = (f32[10,8,128]{2,1,0:T(8,128)S(1)}, f32[10,8,128]{2,1,0:T(8,128)S(1)}, u32[]{:S(2)}, u32[]{:S(2)}) collective-permute-start(f32[10,8,128]{2,1,0:T(8,128)S(1)} %get-tuple-element.33), channel_id=1, source_target_pairs={{0,128},{1,0},{2,130},{3,2},{4,132},{5,4},{6,134},{7,6},{8,136},{9... | collective-permute-start | bytes 122888 | tf_op jit(solution)/shard_map/ppermute | solution.py:427
  31.5 5.2 %collective-permute-start.5 = (f32[10,8,128]{2,1,0:T(8,128)S(1)}, f32[10,8,128]{2,1,0:T(8,128)S(1)}, u32[]{:S(2)}, u32[]{:S(2)}) collective-permute-start(f32[10,8,128]{2,1,0:T(8,128)S(1)} %get-tuple-element.34), channel_id=1, source_target_pairs={{128,0},{0,1},{130,2},{2,3},{132,4},{4,5},{134,6},{6,7},{136,8},{8... | collective-permute-start | bytes 122888 | tf_op jit(solution)/shard_map/ppermute | solution.py:427
  37.4 6.1 %collective-permute-start.6 = (f32[43,8,128]{2,1,0:T(8,128)S(1)}, f32[43,8,128]{2,1,0:T(8,128)S(1)}, u32[]{:S(2)}, u32[]{:S(2)}) collective-permute-start(f32[43,8,128]{2,1,0:T(8,128)S(1)} %get-tuple-element.36), channel_id=1, source_target_pairs={{0,1},{1,2},{2,3},{3,4},{4,5},{5,6},{6,7},{7,8},{8,9},{9,10},{10,1... | collective-permute-start | bytes 528392 | tf_op jit(solution)/shard_map/ppermute | solution.py:411
  37.5 6.1 %collective-permute-start.7 = (f32[43,8,128]{2,1,0:T(8,128)S(1)}, f32[43,8,128]{2,1,0:T(8,128)S(1)}, u32[]{:S(2)}, u32[]{:S(2)}) collective-permute-start(f32[43,8,128]{2,1,0:T(8,128)S(1)} %get-tuple-element.37), channel_id=1, source_target_pairs={{1,0},{2,1},{3,2},{4,3},{5,4},{6,5},{7,6},{8,7},{9,8},{10,9},{11,1... | collective-permute-start | bytes 528392 | tf_op jit(solution)/shard_map/ppermute | solution.py:411
